TPU v7x, 256 devices: a whole 4x4x8 slice. The times are simulated.
256 devices in a mesh: seq: 64 (over x, z, core), batch: 4 (over y).
Axes of the slice: x: 4, y: 4, z: 8, core: 2. Of those that a mesh axis runs over, the one named last changes fastest.
Arguments:
- events: bfloat16 [4, 32768, 1, 256], P('batch', 'seq'), may hold values from -6 to 6
- spectral_filter: float32 [2, 32768, 256], P(None, None, 'seq'), may hold values from -6 to 6
- ln_gain: float32 [256], replicated, may hold values from 0.1 to 1.9
- w_in: bfloat16 [64, 1024, 256], P('seq', 'batch'), may hold values from -0.375 to 0.375
- w_out: bfloat16 [64, 1024, 256], P('seq', 'batch'), may hold values from -0.1875 to 0.1875
- gate_weight: bfloat16 [3, 256, 64], replicated, may hold values from -0.375 to 0.375
- gate_table: float32 [3, 16], replicated, may hold values from -4 to 4
- routes: int32 [4, 32768, 1, 1], P('batch', 'seq'), may hold values from 0 to 63; in each aligned block of 512 rows (0 to 511, 512 to 1023, ..., all dimensions but the last counted through in order) at most 16 rows name the same one
- gate_index: int32 [4, 32768, 1, 3], P('batch', 'seq'), may hold values from 0 to 15
Outputs:
- task_out: bfloat16 [3, 4, 32768, 1, 256], P(None, 'batch', 'seq')
Inputs may be any that keep to these rules, and one draw needn't show every extreme that they name: `routes`: in each aligned block of 512 rows (the events of one device) no expert is named by more than 16 rows; in some block one expert is named by exactly 16.
All inputs are finite; a program needn't handle non-finite values.
Results may differ from a plain program's by a relative error of at most 0.0072.
Values may be sent and summed in bfloat16 or wider, within the bound.
No kernel may reach another device: no remote copies, remote signals or barrier semaphores. Data moves between devices by JAX's collectives and lax.ppermute only.
A program may use at most 128 MiB of HBM per device.

v0:
```python
import math

import jax
import jax.numpy as jnp
from jax import lax
from jax.sharding import PartitionSpec as P

EXPERTS = 64
TASKS = 3


HIGHEST = lax.Precision.HIGHEST


def split_length(length):
    factor = math.isqrt(length)
    while length % factor:
        factor -= 1
    return factor


def dft_table(points):
    indices = jnp.arange(points, dtype=jnp.int32)
    product = indices[:, None] * indices[None, :] % points
    angles = product.astype(jnp.float32) * (2.0 * math.pi / points)
    return (jnp.cos(angles), jnp.sin(angles))


def twiddle_table(outer_len, inner_len):
    length = outer_len * inner_len
    outer_idx = jnp.arange(outer_len, dtype=jnp.int32)
    inner_idx = jnp.arange(inner_len, dtype=jnp.int32)
    product = outer_idx[:, None] * inner_idx[None, :] % length
    angles = product.astype(jnp.float32) * (2.0 * math.pi / length)
    return (jnp.cos(angles)[:, :, None], jnp.sin(angles)[:, :, None])


def contract(values, matrix):
    return jnp.einsum("amb,mc->acb", values, matrix, precision=HIGHEST)


def spectral_pass(signal, filter_re, filter_im):
    length, col_count = signal.shape
    outer_len = split_length(length)
    inner_len = length // outer_len
    cos_outer, sin_outer = dft_table(outer_len)
    cos_inner, sin_inner = dft_table(inner_len)
    tw_cos, tw_sin = twiddle_table(outer_len, inner_len)
    flat_in = signal.reshape(outer_len, inner_len * col_count)
    part_re = jnp.dot(cos_outer, flat_in, precision=HIGHEST).reshape(
        outer_len, inner_len, col_count
    )
    part_im = -jnp.dot(sin_outer, flat_in, precision=HIGHEST).reshape(
        outer_len, inner_len, col_count
    )
    turn_re = part_re * tw_cos + part_im * tw_sin
    turn_im = part_im * tw_cos - part_re * tw_sin
    spec_re = contract(turn_re, cos_inner) + contract(turn_im, sin_inner)
    spec_im = contract(turn_im, cos_inner) - contract(turn_re, sin_inner)
    prod_re = spec_re * filter_re - spec_im * filter_im
    prod_im = spec_re * filter_im + spec_im * filter_re
    back_re = contract(prod_re, cos_inner) - contract(prod_im, sin_inner)
    back_im = contract(prod_im, cos_inner) + contract(prod_re, sin_inner)
    rot_re = (back_re * tw_cos - back_im * tw_sin).reshape(outer_len, inner_len * col_count)
    rot_im = (back_im * tw_cos + back_re * tw_sin).reshape(outer_len, inner_len * col_count)
    result = jnp.dot(cos_outer, rot_re, precision=HIGHEST) - jnp.dot(
        sin_outer, rot_im, precision=HIGHEST
    )
    return result.reshape(length, col_count) / length


def filter_layout(values, outer_len, inner_len, user_count):
    chan_dev = values.shape[1]
    turned = values.reshape(inner_len, outer_len, chan_dev).transpose(1, 0, 2)
    wide = turned[:, :, None, :]
    return wide.reshape(outer_len, inner_len, user_count * chan_dev)


def layer_norm(summed, gain_vec):
    centre = jnp.mean(summed, -1, keepdims=True, dtype=jnp.float32)
    square_mean = jnp.mean(jnp.square(summed.astype(jnp.float32)), -1, keepdims=True)
    spread_sq = jnp.maximum(square_mean - centre * centre, 0.0)
    return ((summed.astype(jnp.float32) - centre) * lax.rsqrt(spread_sq + 1e-05) * gain_vec).astype(
        jnp.bfloat16
    )


def build_slots(rows, targets, slot_total):
    row_count = rows.shape[0]
    owner_map = (
        jnp.full((slot_total,), row_count, jnp.int32)
        .at[targets]
        .set(jnp.arange(row_count, dtype=jnp.int32))
    )
    padded = jnp.concatenate([rows, jnp.zeros((1, rows.shape[1]), rows.dtype)], 0)
    return padded[owner_map]


def expert_ffn(normed, w_in, w_out):
    part_in = lax.all_gather(w_in, "batch", axis=1, tiled=True)
    part_out = lax.all_gather(w_out, "batch", axis=1, tiled=True)
    hidden = jnp.maximum(
        jnp.einsum("jsc,jhc->jsh", normed, part_in, preferred_element_type=jnp.float32), 0.0
    ).astype(jnp.bfloat16)
    summed = jnp.einsum("jsh,jhc->jsc", hidden, part_out, preferred_element_type=jnp.float32)
    return summed.astype(jnp.bfloat16)


def on_device(
    events, spectral_filter, ln_gain, w_in, w_out, gate_weight, gate_table, routes, gate_index
):
    n_seq = lax.axis_size("seq")
    len_dev = events.shape[1]
    user_count = events.shape[2]
    channels = events.shape[3]
    chan_dev = channels // n_seq
    length = len_dev * n_seq
    tok_count = len_dev * user_count
    capacity = max(2, 2 * tok_count // EXPERTS)
    col_count = user_count * chan_dev
    outer_len = split_length(length)
    inner_len = length // outer_len
    channel_view = lax.all_to_all(events, "seq", split_axis=3, concat_axis=1, tiled=True)
    filter_re = filter_layout(spectral_filter[0], outer_len, inner_len, user_count)
    filter_im = filter_layout(spectral_filter[1], outer_len, inner_len, user_count)
    signal = channel_view.reshape(length, col_count).astype(jnp.float32)
    filtered = spectral_pass(signal, filter_re, filter_im)
    summed_ch = (signal + filtered).astype(jnp.bfloat16).reshape(1, length, user_count, chan_dev)
    expert_ids = routes.reshape(tok_count)
    onehot = (expert_ids[:, None] == jnp.arange(EXPERTS, dtype=jnp.int32)[None, :]).astype(
        jnp.int32
    )
    earlier = jnp.cumsum(onehot, 0) - onehot
    rank_vals = jnp.sum(earlier * onehot, 1)
    slot_index = expert_ids * capacity + rank_vals
    returned = lax.all_to_all(summed_ch, "seq", split_axis=1, concat_axis=3, tiled=True)
    normed = layer_norm(returned, ln_gain).reshape(tok_count, channels)
    outgoing = build_slots(normed, slot_index, EXPERTS * capacity).reshape(
        EXPERTS, capacity, channels
    )
    arrived = lax.all_to_all(outgoing, "seq", split_axis=0, concat_axis=1, tiled=True)
    expert_out = expert_ffn(arrived, w_in, w_out)
    result_slots = lax.all_to_all(expert_out, "seq", split_axis=1, concat_axis=0, tiled=True)
    gate_cols = gate_weight.transpose(1, 0, 2).reshape(channels, TASKS * EXPERTS)
    all_scores = jnp.dot(normed, gate_cols, preferred_element_type=jnp.float32).reshape(
        tok_count, TASKS, EXPERTS
    )
    pick = jnp.broadcast_to(expert_ids[:, None, None], (tok_count, TASKS, 1))
    chosen = jnp.take_along_axis(all_scores, pick, axis=2)[:, :, 0].astype(jnp.bfloat16)
    expert_rows = result_slots.reshape(-1, channels)[slot_index].astype(jnp.float32)
    lookup = gate_index.reshape(tok_count, TASKS)
    matches = lookup[:, :, None] == jnp.arange(gate_table.shape[1], dtype=jnp.int32)[None, None, :]
    table_bias = jnp.sum(jnp.where(matches, gate_table[None], 0.0), -1)
    gate_vals = jax.nn.sigmoid(chosen.astype(jnp.float32) + table_bias)
    task_out = (gate_vals.T[:, :, None] * expert_rows[None]).astype(jnp.bfloat16)
    return task_out.reshape(TASKS, 1, len_dev, user_count, channels)


def solution(mesh):
    in_specs = (
        P("batch", "seq", None, None),
        P(None, None, "seq"),
        P(),
        P("seq", "batch", None),
        P("seq", "batch", None),
        P(),
        P(),
        P("batch", "seq", None, None),
        P("batch", "seq", None, None),
    )
    out_specs = P(None, "batch", "seq", None, None)
    return jax.shard_map(
        on_device, mesh=mesh, in_specs=in_specs, out_specs=out_specs, check_vma=False
    )
```

profile of v0, /device:TPU:1, one launch (start us, length us, event | category | flops | bytes accessed | tf_op | source)
XLA Modules:
  0.0 726.7 jit_solution(15999475889338935902)
XLA Ops:
  5.0 13.0 %all-to-all-start = ((bf16[64,2,1024]{2,1,0:T(2,128)(2,1)}), bf16[64,2,1024]{2,1,0:T(2,128)(2,1)S(1)}, u32[]{:S(2)}, u32[]{:S(2)}) async-start(bf16[64,2,1024]{2,1,0:T(2,128)(2,1)} %reshape.528), calls=%async_computation | async-start | bytes 524288 | tf_op jit(solution)/shard_map/all_to_all | solution.py:123
  22.0 8.0 %all-to-all-done = bf16[64,2,1024]{2,1,0:T(2,128)(2,1)S(1)} async-done(((bf16[64,2,1024]{2,1,0:T(2,128)(2,1)}), bf16[64,2,1024]{2,1,0:T(2,128)(2,1)S(1)}, u32[]{:S(2)}, u32[]{:S(2)}) %all-to-all-start) | async-done | bytes 262176 | tf_op jit(solution)/shard_map/all_to_all | solution.py:123
  31.8 5.5 copy.139
  37.4 17.2 %reshape.469 = bf16[128,1024]{1,0:T(8,128)(2,1)S(1)} reshape(bf16[1,64,512,1,4]{4,2,1,3,0:T(8,128)(2,1)} %copy.139) | data formatting | bytes 524288 | tf_op jit(solution)/shard_map/reshape | solution.py:49
  66.6 2.2 fusion.4
  72.9 18.7 %div.19 = f32[1,32768,1,4]{3,1,2,0:T(8,128)} reshape(f32[128,1024]{1,0:T(8,128)S(1)} %fusion.3) | data formatting | bytes 1048576 | tf_op jit(solution)/shard_map/div | solution.py:69
  91.6 9.5 %copy.153 = f32[1,32768,1,4]{1,3,2,0:T(4,128)S(1)} copy(f32[1,32768,1,4]{3,1,2,0:T(8,128)} %div.19) | data formatting | bytes 1048576 | tf_op jit(solution)/shard_map/div | solution.py:69
  101.2 25.5 %copy.154 = bf16[1,32768,1,4]{3,2,0,1:T(2,128)(2,1)} copy(bf16[1,32768,1,4]{1,3,2,0:T(4,128)(2,1)S(1)} %fusion.10) | data formatting | bytes 524288 | tf_op jit(solution)/shard_map/convert_element_type | solution.py:128
  126.7 179.3 %reduce.16 = bf16[32768,4]{1,0:T(8,128)(2,1)} reduce(bf16[32768,1,1,4]{3,2,1,0:T(2,128)(2,1)} %bitcast.168, bf16[]{:T(256)} %broadcast.438), dimensions={1,2}, to_apply=%bitcast.143.reduce_sub_computation | reduce | bytes 524290
  306.0 16.8 %reshape.530 = bf16[64,2,1024]{2,1,0:T(2,128)(2,1)} reshape(bf16[32768,4]{1,0:T(8,128)(2,1)} %reduce.16) | data formatting | bytes 524288
  322.8 6.0 all-to-all-start.1
  329.0 2.4 scatter_custom_fusion
  331.5 9.4 %all-to-all-done.1 = bf16[64,2,1024]{2,1,0:T(2,128)(2,1)S(1)} async-done(((bf16[64,2,1024]{2,1,0:T(2,128)(2,1)}), bf16[64,2,1024]{2,1,0:T(2,128)(2,1)S(1)}, u32[]{:S(2)}, u32[]{:S(2)}) %all-to-all-start.1) | async-done | bytes 262176 | tf_op jit(solution)/shard_map/all_to_all | solution.py:136
  340.9 34.1 %reshape.531 = bf16[32768,1,1,4]{3,2,1,0:T(2,128)(2,1)} reshape(bf16[64,2,1024]{2,1,0:T(2,128)(2,1)S(1)} %all-to-all-done.1) | data formatting | bytes 524288
  374.9 244.9 %convert_reduce_fusion = (f32[32768]{0:T(1024)S(1)}, f32[32768]{0:T(1024)S(1)}) fusion(bf16[32768,1,1,4]{3,2,1,0:T(2,128)(2,1)} %reshape.531), kind=kLoop, calls=%fused_computation.136 | loop fusion | flops 458752 | bytes 524288 | tf_op jit(solution)/shard_map/reduce_sum | solution.py:80
  619.9 19.8 %bitcast_convert_fusion = f32[1,32768,1,4]{3,2,0,1:T(1,128)} fusion(bf16[32768,1,1,4]{3,2,1,0:T(2,128)(2,1)} %reshape.531), kind=kLoop, calls=%fused_computation.186 | loop fusion | flops 131072 | bytes 786432 | tf_op jit(solution)/shard_map/convert_element_type | solution.py:83
  639.8 9.2 %copy.155 = f32[1,64,512,1,4]{2,4,1,3,0:T(4,128)S(1)} copy(f32[1,64,512,1,4]{4,2,1,3,0:T(8,128)} %bitcast.167) | data formatting | bytes 1048576 | tf_op jit(solution)/shard_map/convert_element_type | solution.py:83
  649.7 5.0 gather_fusion
  654.7 6.0 all-to-all-start.2
  660.7 11.6 %all_gather.6 = bf16[1,1024,256]{2,1,0:T(8,128)(2,1)S(1)} all-gather(bf16[1,256,256]{2,1,0:T(8,128)(2,1)S(1)} %copy-done.1), channel_id=1, replica_groups=mesh['seq'=64,'batch'=4] {'batch'}, dimensions={1}, use_global_device_ids=true | all-gather | bytes 655360 | tf_op jit(solution)/shard_map/all_gather | solution.py:100
  672.3 10.4 %all_gather.7 = bf16[1,1024,256]{2,1,0:T(8,128)(2,1)S(1)} all-gather(bf16[1,256,256]{2,1,0:T(8,128)(2,1)S(1)} %copy-done.2), channel_id=1, replica_groups=mesh['seq'=64,'batch'=4] {'batch'}, dimensions={1}, use_global_device_ids=true | all-gather | bytes 655360 | tf_op jit(solution)/shard_map/all_gather | solution.py:101
  685.0 4.0 reduce.17
  689.9 15.3 %all-to-all-start.3 = ((bf16[64,2,2048]{2,1,0:T(2,128)(2,1)}), bf16[64,2,2048]{2,1,0:T(2,128)(2,1)S(1)}, u32[]{:S(2)}, u32[]{:S(2)}) async-start(bf16[64,2,2048]{2,1,0:T(2,128)(2,1)} %reshape.532), calls=%async_computation.3 | async-start | bytes 1048576 | tf_op jit(solution)/shard_map/all_to_all | solution.py:143
  707.4 14.6 %gather_fusion.2 = bf16[1536]{0:T(1024)(128)(2,1)S(1)} fusion(bf16[512,3,64]{0,2,1:T(8,128)(2,1)S(1)} %fusion.18, s32[1536]{0:T(1024)S(1)} %reshape.502), kind=kCustom, calls=%fused_computation.2 | custom fusion | bytes 24576 | tf_op jit(solution)/shard_map/jit(take_along_axis)/gather | solution.py:149
  (88 shorter events, 37.2 us)
Async XLA Ops:
  0.0 707.0 %copy-start = (bf16[3,256,64]{1,2,0:T(8,128)(2,1)S(1)}, bf16[3,256,64]{1,2,0:T(8,128)(2,1)}, u32[]{:S(2)}) copy-start(bf16[3,256,64]{1,2,0:T(8,128)(2,1)} %param.14) | copy-start | bytes 294916
  5.0 25.0 %all-to-all-start = ((bf16[64,2,1024]{2,1,0:T(2,128)(2,1)}), bf16[64,2,1024]{2,1,0:T(2,128)(2,1)S(1)}, u32[]{:S(2)}, u32[]{:S(2)}) async-start(bf16[64,2,1024]{2,1,0:T(2,128)(2,1)} %reshape.528), calls=%async_computation | async-start | bytes 524288 | tf_op jit(solution)/shard_map/all_to_all | solution.py:123
  20.2 34.4 %copy-start.4 = (s32[64,5]{0,1:T(8,128)}, s32[64,5]{0,1:T(8,128)S(1)}, u32[]{:S(2)}) copy-start(s32[64,5]{0,1:T(8,128)S(1)} %reduce-window.9) | copy-start | bytes 3844
  306.0 22.9 %copy-start.3 = (s32[1,512,1,1]{1,3,2,0:T(1,128)S(1)}, s32[1,512,1,1]{1,3,2,0:T(1,128)}, u32[]{:S(2)}) copy-start(s32[1,512,1,1]{1,3,2,0:T(1,128)} %param.16) | copy-start | bytes 6148
  306.0 22.9 %slice-start = ((s32[64,5]{0,1:T(8,128)}), s32[64,4]{0,1:T(4,128)S(1)}, s32[]{:S(2)}) async-start(s32[64,5]{0,1:T(8,128)} %copy-done.4), calls=%async_computation.4 | async-start | bytes 4096 | tf_op jit(solution)/shard_map/slice.1
  322.8 18.0 %all-to-all-start.1 = ((bf16[64,2,1024]{2,1,0:T(2,128)(2,1)}), bf16[64,2,1024]{2,1,0:T(2,128)(2,1)S(1)}, u32[]{:S(2)}, u32[]{:S(2)}) async-start(bf16[64,2,1024]{2,1,0:T(2,128)(2,1)} %reshape.530), calls=%async_computation.1 | async-start | bytes 524288 | tf_op jit(solution)/shard_map/all_to_all | solution.py:136
  639.8 9.6 %copy-start.6 = (f32[256]{0:T(256)S(1)}, f32[256]{0:T(256)}, u32[]{:S(2)}) copy-start(f32[256]{0:T(256)} %param.11) | copy-start | bytes 3076
  649.0 11.7 %copy-start.1 = (bf16[1,256,256]{2,1,0:T(8,128)(2,1)S(1)}, bf16[1,256,256]{2,1,0:T(8,128)(2,1)}, u32[]{:S(2)}) copy-start(bf16[1,256,256]{2,1,0:T(8,128)(2,1)} %param.12) | copy-start | bytes 393220
  649.0 23.3 %copy-start.2 = (bf16[1,256,256]{2,1,0:T(8,128)(2,1)S(1)}, bf16[1,256,256]{2,1,0:T(8,128)(2,1)}, u32[]{:S(2)}) copy-start(bf16[1,256,256]{2,1,0:T(8,128)(2,1)} %param.13) | copy-start | bytes 393220
  649.7 56.0 %copy-start.5 = (s32[1,512,1,3]{1,2,3,0:T(1,128)S(1)}, s32[1,512,1,3]{1,2,3,0:T(1,128)}, u32[]{:S(2)}) copy-start(s32[1,512,1,3]{1,2,3,0:T(1,128)} %param.17) | copy-start | bytes 18436
  649.7 56.0 %copy-start.7 = (f32[3,16]{1,0:T(4,128)S(1)}, f32[3,16]{1,0:T(4,128)}, u32[]{:S(2)}) copy-start(f32[3,16]{1,0:T(4,128)} %param.15) | copy-start | bytes 580
  654.7 28.1 %all-to-all-start.2 = ((bf16[64,16,256]{2,1,0:T(8,128)(2,1)}), bf16[64,16,256]{2,1,0:T(8,128)(2,1)S(1)}, u32[]{:S(2)}, u32[]{:S(2)}) async-start(bf16[64,16,256]{2,1,0:T(8,128)(2,1)} %bitcast.29), calls=%async_computation.2 | async-start | bytes 1048576 | tf_op jit(solution)/shard_map/all_to_all | solution.py:141
  689.9 32.6 %all-to-all-start.3 = ((bf16[64,2,2048]{2,1,0:T(2,128)(2,1)}), bf16[64,2,2048]{2,1,0:T(2,128)(2,1)S(1)}, u32[]{:S(2)}, u32[]{:S(2)}) async-start(bf16[64,2,2048]{2,1,0:T(2,128)(2,1)} %reshape.532), calls=%async_computation.3 | async-start | bytes 1048576 | tf_op jit(solution)/shard_map/all_to_all | solution.py:143
where the time goes:
time: 733 us; the launch traced here: 727 us
  other arithmetic  455 us (62%)
  local copies, waits for them, and re-layouts  172 us (23%)
  starting transfers between devices  40.3 us (5%)
  blocking collectives  22 us (3%)
  matrix products  19.3 us (3%)
  waiting for transfers between devices  17.5 us (2%)
    reduce_sum x2, other arithmetic, layer_norm(): centre = jnp.mean(summed, -1, keepdims=True, dtype=jnp.float32)  245 us
    unnamed x3, other arithmetic  186 us
    unnamed x30, local copies, waits for them, and re-layouts  56.8 us
    div x2, local copies, waits for them, and re-layouts, spectral_pass(): return result.reshape(length, col_count) / length  28.1 us
    convert_element_type x1, local copies, waits for them, and re-layouts, on_device(): (signal + filtered).astype(jnp.bfloat16)  25.5 us
    convert_element_type x1, other arithmetic, layer_norm(): summed.astype(jnp.float32) - centre  19.8 us
    reshape x1, local copies, waits for them, and re-layouts, spectral_pass(): flat_in = signal.reshape(outer_len, inner_len * col_count)  17.2 us
    gather x5, local copies, waits for them, and re-layouts, on_device(): jnp.take_along_axis(all_scores, pick, axis=2)[:, :, 0].astype(jnp.bfloat16)  15.3 us
  transfers between devices with their start and end apart: 4, of which 3 were waited for; matrix products, arithmetic and copies ran while one was open for 3% of the time, Pallas kernels for 0%

commit v1 on v0

v1 whole, which is shorter than its diff:
```python
import functools

import jax
import jax.numpy as jnp
import ml_dtypes
import numpy as np
from jax import lax
from jax.experimental import pallas as pl
from jax.experimental.pallas import tpu as pltpu
from jax.sharding import PartitionSpec as P

EXPERTS = 64
TASKS = 3
CAP = 16
ROWS = 256
COLS = 128
LENGTH = ROWS * COLS
BF16 = jnp.bfloat16
F32 = jnp.float32

NN = (((1,), (0,)), ((), ()))
NT = (((1,), (1,)), ((), ()))


def dot(a, b, dims):
    return lax.dot_general(a, b, dims, preferred_element_type=F32)


def split(x):
    hi = x.astype(BF16)
    return hi, (x - hi.astype(F32)).astype(BF16)


def np_split(x):
    hi = x.astype(ml_dtypes.bfloat16)
    return hi, (x - hi.astype(np.float64)).astype(ml_dtypes.bfloat16)


def cos_sin(rows, cols, points):
    angle = 2.0 * np.pi * (np.outer(np.arange(rows), np.arange(cols)) % points) / points
    return np.cos(angle), np.sin(angle)


def tables():
    cos_r, sin_r = cos_sin(ROWS, ROWS, ROWS)
    cos_c, sin_c = cos_sin(COLS, COLS, COLS)
    tw_cos, tw_sin = cos_sin(ROWS, COLS, LENGTH)
    first = np.stack(np_split(np.concatenate([cos_r, -sin_r], 0)))
    second = np.stack(np_split(np.block([[cos_c, sin_c], [-sin_c, cos_c]])))
    third = np.stack(np_split(np.block([[cos_c, -sin_c], [sin_c, cos_c]])))
    fourth = np.stack(np_split(np.concatenate([cos_r, -sin_r], 1) / LENGTH))
    turn = np.stack([tw_cos, tw_sin]).astype(np.float32)
    turn_back = np.stack([tw_cos.T, tw_sin.T]).astype(np.float32)
    return first, second, third, fourth, turn, turn_back


def join_lanes(wide, out_ref):
    for half in range(2):
        out_ref[:, half * 128 : (half + 1) * 128] = wide[half].astype(BF16)


def deinterleave(x_ref, wide):
    for half in range(2):
        wide[half] = x_ref[:, half * 128 : (half + 1) * 128].astype(F32)
    return jnp.concatenate(
        [wide[half, pl.ds(odd, 256, stride=2), :] for odd in range(2) for half in range(2)], 1
    )


def prep_kernel(ev_ref, out_ref, mid, wide):
    for pb in range(4):
        mid[...] = ev_ref[pb * 128 : (pb + 1) * 128, :].astype(F32).T
        for ch in range(4):
            chp, chl = ch // 2, ch % 2
            wide[chl, pl.ds(pb * 2 + chp, 64, stride=8), :] = mid[pl.ds(ch, 64, stride=4), :]
    join_lanes(wide, out_ref)


def filter_kernel(
    x_ref, spec_ref, first_ref, second_ref, third_ref, fourth_ref, turn_ref, back_ref,
    out_ref, wide, sums,
):
    sig = deinterleave(x_ref, wide)
    sig16 = sig.astype(BF16)
    spec1 = dot(first_ref[0], sig16, NN) + dot(first_ref[1], sig16, NN)
    tcos, tsin = turn_ref[0], turn_ref[1]
    turned = []
    for ch in range(4):
        re = spec1[:256, ch * 128 : (ch + 1) * 128]
        im = spec1[256:, ch * 128 : (ch + 1) * 128]
        turned.append(jnp.concatenate([re * tcos + im * tsin, im * tcos - re * tsin], 1))
    t_hi, t_lo = split(jnp.concatenate(turned, 0))
    spec2 = (
        dot(second_ref[0], t_hi, NT) + dot(second_ref[0], t_lo, NT) + dot(second_ref[1], t_hi, NT)
    )
    prods = []
    for ch in range(4):
        fr = jnp.concatenate(
            [spec_ref[0, pl.ds(4 * h + ch, 128, stride=8), :] for h in range(2)], 1
        )
        fi = jnp.concatenate(
            [spec_ref[1, pl.ds(4 * h + ch, 128, stride=8), :] for h in range(2)], 1
        )
        zr = spec2[:128, ch * 256 : (ch + 1) * 256]
        zi = spec2[128:, ch * 256 : (ch + 1) * 256]
        prods.append(jnp.concatenate([zr * fr - zi * fi, zr * fi + zi * fr], 0))
    p_hi, p_lo = split(jnp.concatenate(prods, 1))
    back = dot(third_ref[0], p_hi, NN) + dot(third_ref[0], p_lo, NN) + dot(third_ref[1], p_hi, NN)
    bcos, bsin = back_ref[0], back_ref[1]
    turned = []
    for ch in range(4):
        re = back[:128, ch * 256 : (ch + 1) * 256]
        im = back[128:, ch * 256 : (ch + 1) * 256]
        turned.append(jnp.concatenate([re * bcos - im * bsin, im * bcos + re * bsin], 1))
    v_hi, v_lo = split(jnp.concatenate(turned, 0))
    filtered = (
        dot(fourth_ref[0], v_hi, NT) + dot(fourth_ref[0], v_lo, NT) + dot(fourth_ref[1], v_hi, NT)
    )
    summed = sig + filtered
    for ch in range(4):
        sums[ch] = summed[:, ch * 128 : (ch + 1) * 128]
    for pb in range(4):
        for ch in range(4):
            wide[pb % 2, pl.ds(ch * 2 + pb // 2, 64, stride=8), :] = sums[
                ch, pl.ds(pb, 64, stride=4), :
            ]
    join_lanes(wide, out_ref)


def route_kernel(routes_ref, put_ref, take_ref):
    experts = routes_ref[...]
    onehot = (lax.broadcasted_iota(jnp.int32, (EXPERTS, 512), 0) == experts).astype(F32)
    before = lax.broadcasted_iota(jnp.int32, (512, 512), 0) < lax.broadcasted_iota(
        jnp.int32, (512, 512), 1
    )
    earlier = dot(onehot.astype(BF16), before.astype(F32).astype(BF16), NN)
    rank = jnp.sum(earlier * onehot, 0, keepdims=True)
    slot = experts.astype(F32) * CAP + rank
    put_ref[...] = (
        lax.broadcasted_iota(jnp.int32, (EXPERTS * CAP, 512), 0) == slot.astype(jnp.int32)
    ).astype(F32).astype(BF16)
    slot_col = jnp.broadcast_to(slot, (128, 512)).T[:, 0:1].astype(jnp.int32)
    take_ref[...] = (
        lax.broadcasted_iota(jnp.int32, (512, EXPERTS * CAP), 1) == slot_col
    ).astype(F32).astype(BF16)


def norm_kernel(x_ref, gain_ref, put_ref, out_ref, normed_ref, wide):
    vals = deinterleave(x_ref, wide)
    centre = jnp.sum(vals, 0, keepdims=True) * (1.0 / 256)
    off = vals - centre
    spread = jnp.sum(off * off, 0, keepdims=True) * (1.0 / 256)
    normed = (off * lax.rsqrt(spread + 1e-05) * gain_ref[...]).astype(BF16)
    normed_ref[...] = normed
    out_ref[...] = dot(put_ref[...], normed, NT).astype(BF16)


def gate_kernel(normed_ref, weight_ref, routes_ref, index_ref, table_ref, out_ref):
    scores = dot(weight_ref[...], normed_ref[...], NN)
    mask = lax.broadcasted_iota(jnp.int32, (EXPERTS, 512), 0) == routes_ref[...]
    rows = []
    for t in range(TASKS):
        part = scores[t * EXPERTS : (t + 1) * EXPERTS]
        chosen = jnp.sum(jnp.where(mask, part, 0.0), 0, keepdims=True).astype(BF16).astype(F32)
        idx = index_ref[t : t + 1, :]
        bias = jnp.zeros((1, 512), F32)
        for r in range(table_ref.shape[1]):
            bias = jnp.where(idx == r, table_ref[t, r], bias)
        rows.append(jax.nn.sigmoid(chosen + bias))
    rows.append(jnp.zeros((128 - TASKS, 512), F32))
    out_ref[...] = jnp.concatenate(rows, 0).T


def ffn_kernel(x_ref, weights_ref, out_ref):
    w_in = weights_ref[:, 0].reshape(1024, 256)
    w_out = weights_ref[:, 1].reshape(1024, 256)
    hidden = jnp.maximum(dot(x_ref[...], w_in, NT), 0.0).astype(BF16)
    out_ref[...] = dot(hidden, w_out, NN).astype(BF16)


def final_kernel(slots_ref, take_ref, gate_ref, out_ref):
    rows = dot(take_ref[...], slots_ref[...], NN)
    for t in range(TASKS):
        out_ref[t] = (gate_ref[:, t : t + 1] * rows).astype(BF16)


def call(kernel, outs, *args, scratch=(), smem=(), flops=0, name=None):
    specs = [
        pl.BlockSpec(memory_space=pltpu.SMEM if i in smem else pltpu.VMEM)
        for i in range(len(args))
    ]
    many = isinstance(outs, (tuple, list))
    return pl.pallas_call(
        kernel,
        out_shape=outs,
        in_specs=specs,
        out_specs=[pl.BlockSpec(memory_space=pltpu.VMEM)] * len(outs)
        if many
        else pl.BlockSpec(memory_space=pltpu.VMEM),
        scratch_shapes=list(scratch),
        compiler_params=pltpu.CompilerParams(vmem_limit_bytes=32 * 2**20),
        cost_estimate=pl.CostEstimate(flops=flops, bytes_accessed=2**20, transcendentals=0),
        name=name,
    )(*args)


def shape(dims, dtype):
    return jax.ShapeDtypeStruct(dims, dtype)


def swap(values, rows):
    lanes = values.shape[-1]
    chunks = values.reshape(64, rows, lanes)
    return lax.all_to_all(chunks, "seq", split_axis=0, concat_axis=0, tiled=True).reshape(
        64 * rows, lanes
    )


def on_device(
    events, spectral_filter, ln_gain, w_in, w_out, gate_weight, gate_table, routes, gate_index
):
    big = pltpu.VMEM
    chunks = call(
        prep_kernel, shape((512, 256), BF16), events.reshape(512, 256),
        scratch=[big((256, 128), F32), big((2, 512, 128), F32)], name="prep",
    )
    arrived = swap(chunks, 8)
    weights = lax.all_gather(jnp.stack([w_in[0], w_out[0]]), "batch", axis=0, tiled=False)
    route_row = routes.reshape(1, 512)
    put, take = call(
        route_kernel, [shape((1024, 512), BF16), shape((512, 1024), BF16)], route_row, name="route"
    )
    spec = spectral_filter.reshape(2, 256, 128, 4).transpose(0, 1, 3, 2).reshape(2, 1024, 128)
    consts = [jnp.asarray(t) for t in tables()]
    sums = call(
        filter_kernel, shape((512, 256), BF16), arrived, spec, *consts,
        scratch=[big((2, 512, 128), F32), big((4, 256, 128), F32)], name="filter", flops=2 * 10**9,
    )
    returned = swap(sums, 8)
    outgoing, normed = call(
        norm_kernel, [shape((1024, 256), BF16), shape((256, 512), BF16)],
        returned, ln_gain.reshape(256, 1), put, scratch=[big((2, 512, 128), F32)], name="norm",
    )
    slots_in = swap(outgoing, 16)
    gates = call(
        gate_kernel, shape((512, 128), F32), normed,
        gate_weight.transpose(0, 2, 1).reshape(192, 256), route_row,
        gate_index.reshape(512, 3).T, gate_table, smem=(4,), name="gate",
    )
    slots_out = call(ffn_kernel, shape((1024, 256), BF16), slots_in, weights, name="ffn", flops=10**9)
    results = swap(slots_out, 16)
    out = call(final_kernel, shape((3, 512, 256), BF16), results, take, gates, name="final")
    return out.reshape(TASKS, 1, 512, 1, 256)


def solution(mesh):
    in_specs = (
        P("batch", "seq", None, None),
        P(None, None, "seq"),
        P(),
        P("seq", "batch", None),
        P("seq", "batch", None),
        P(),
        P(),
        P("batch", "seq", None, None),
        P("batch", "seq", None, None),
    )
    out_specs = P(None, "batch", "seq", None, None)
    return jax.shard_map(
        on_device, mesh=mesh, in_specs=in_specs, out_specs=out_specs, check_vma=False
    )
```

time: 733 us -> 120 us (0.16)
  other arithmetic: 455 us -> 1.75 us
  local copies, waits for them, and re-layouts: 172 us -> 7.57 us
  waiting for transfers between devices: 17.5 us -> 53.3 us
  blocking collectives: 22 us -> 0 us
  matrix products: 19.3 us -> 0 us
  between operations: 1.04 us -> 13.5 us
  Pallas kernels: 0 us -> 11.3 us
  starting transfers between devices: 40.3 us -> 31.6 us
    reduce_sum x5 -> x0, other arithmetic: 245 us -> none  [the longest x2 245 us: layer_norm(): centre = jnp.mean(summed, -1, keepdims=True, dtype=jnp.float32)]
    unnamed x3 -> x0, other arithmetic: 186 us -> none
    unnamed x30 -> x29, local copies, waits for them, and re-layouts: 56.8 us -> 7.44 us
    convert_element_type x7 -> x0, local copies, waits for them, and re-layouts: 37.1 us -> none  [the longest x1 25.5 us: on_device(): (signal + filtered).astype(jnp.bfloat16)]
    all_to_all x4, waiting for transfers between devices: 17.5 us -> 53.3 us  [swap(): lax.all_to_all(chunks, 'seq', split_axis=0, concat_axis=0, tiled=True)]
    div x2 -> x0, local copies, waits for them, and re-layouts: 28.1 us -> none  [spectral_pass(): return result.reshape(length, col_count) / length]
    gather x7 -> x0, local copies, waits for them, and re-layouts: 22.2 us -> none  [the longest x5 15.3 us: on_device(): jnp.take_along_axis(all_scores, pick, axis=2)[:, :, 0].astype(jnp.bfloat16)]
    convert_element_type x6 -> x0, other arithmetic: 22.1 us -> none  [the longest x1 19.8 us: layer_norm(): summed.astype(jnp.float32) - centre]
  transfers between devices with their start and end apart: 4 -> 5, of which waited for: 3 -> 4; matrix products, arithmetic and copies ran while one was open for 3% -> 2% of each run, Pallas kernels for 0% -> 6%
where the time goes in v1:
time: 120 us; the launch traced here: 119 us
  waiting for transfers between devices  53.3 us (44%)
  starting transfers between devices  31.6 us (26%)
  between operations  13.5 us (11%)
  Pallas kernels  11.3 us (9%)
  local copies, waits for them, and re-layouts  7.57 us (6%)
  other arithmetic  1.75 us (1%)
    all_to_all x4, waiting for transfers between devices, swap(): lax.all_to_all(chunks, 'seq', split_axis=0, concat_axis=0, tiled=True)  53.3 us
    all_to_all x4, starting transfers between devices, swap(): lax.all_to_all(chunks, 'seq', split_axis=0, concat_axis=0, tiled=True)  31.6 us
    pallas_call x7, Pallas kernels, call(): pl.pallas_call(kernel, out_shape=outs, in_specs=specs, out_specs=[pl.Bloc...  11.3 us
    unnamed x29, local copies, waits for them, and re-layouts  7.44 us
  transfers between devices with their start and end apart: 5, of which 4 were waited for; matrix products, arithmetic and copies ran while one was open for 2% of the time, Pallas kernels for 6%

profile of v1, /device:TPU:1, one launch (start us, length us, event | category | flops | bytes accessed | tf_op | source)
XLA Modules:
  0.0 119.0 jit_solution(16214046310241561669)
XLA Ops:
  6.5 0.9 copy-done
  7.5 1.0 prep.1
  8.5 13.0 %all-to-all-start = ((bf16[64,8,256]{2,1,0:T(8,128)(2,1)}), bf16[64,8,256]{2,1,0:T(8,128)(2,1)S(1)}, u32[]{:S(2)}, u32[]{:S(2)}) async-start(bf16[64,8,256]{2,1,0:T(8,128)(2,1)} %bitcast.1), calls=%async_computation | async-start | bytes 524288 | tf_op jit(solution)/shard_map/all_to_all | solution.py:214
  21.5 1.8 %pad_maximum_fusion = bf16[2,256,256]{2,1,0:T(8,128)(2,1)} fusion(bf16[1,256,256]{2,1,0:T(8,128)(2,1)} %param.19, bf16[1,256,256]{2,1,0:T(8,128)(2,1)} %param.18), kind=kLoop, calls=%fused_computation | loop fusion | flops 131072 | bytes 524288 | tf_op jit(solution)/shard_map/stack | solution.py:228
  23.3 10.2 %all-to-all-done = bf16[64,8,256]{2,1,0:T(8,128)(2,1)S(1)} async-done(((bf16[64,8,256]{2,1,0:T(8,128)(2,1)}), bf16[64,8,256]{2,1,0:T(8,128)(2,1)S(1)}, u32[]{:S(2)}, u32[]{:S(2)}) %all-to-all-start) | async-done | bytes 262176 | tf_op jit(solution)/shard_map/all_to_all | solution.py:214
  33.5 1.0 copy-done.7
  34.5 0.9 copy-done.9
  35.5 0.9 copy-done.10
  36.4 1.0 copy-done.11
  37.4 3.4 %filter.1 = bf16[512,256]{1,0:T(8,128)(2,1)} custom-call(bf16[512,256]{1,0:T(8,128)(2,1)S(1)} %bitcast.32, f32[2,1024,128]{2,1,0:T(8,128)S(1)} %bitcast.37, bf16[2,512,256]{2,1,0:T(8,128)(2,1)S(1)} %copy-done.6, bf16[2,256,256]{2,1,0:T(8,128)(2,1)S(1)} %copy-done.8, bf16[2,256,256]{2,1,0:T(8,128)(2,1)S(1)} %copy-done.9, bf16[2,256,512]{2,1,0:T(8,128)(2,1)S(1)} %copy-done.7, ...), custom_call_target="tpu_custom_call" | custom-call | flops 2000000000 | bytes 1048576 | tf_op jit(solution)/shard_map/filter/pallas_call | solution.py:193
  40.7 6.1 %all-to-all-start.1 = ((bf16[64,8,256]{2,1,0:T(8,128)(2,1)}), bf16[64,8,256]{2,1,0:T(8,128)(2,1)S(1)}, u32[]{:S(2)}, u32[]{:S(2)}) async-start(bf16[64,8,256]{2,1,0:T(8,128)(2,1)} %bitcast.6), calls=%async_computation.1 | async-start | bytes 524288 | tf_op jit(solution)/shard_map/all_to_all | solution.py:214
  46.9 1.0 route.1
  47.9 0.7 copy-done.13
  48.7 10.1 %all-to-all-done.1 = bf16[64,8,256]{2,1,0:T(8,128)(2,1)S(1)} async-done(((bf16[64,8,256]{2,1,0:T(8,128)(2,1)}), bf16[64,8,256]{2,1,0:T(8,128)(2,1)S(1)}, u32[]{:S(2)}, u32[]{:S(2)}) %all-to-all-start.1) | async-done | bytes 262176 | tf_op jit(solution)/shard_map/all_to_all | solution.py:214
  58.9 1.5 %norm.1 = (bf16[1024,256]{1,0:T(8,128)(2,1)}, bf16[256,512]{1,0:T(8,128)(2,1)S(1)}) custom-call(bf16[512,256]{1,0:T(8,128)(2,1)S(1)} %bitcast.29, f32[256,1]{1,0:T(8,128)S(1)} %copy.22.gain_ref, bf16[1024,512]{1,0:T(8,128)(2,1)S(1)} %get-tuple-element.9.put_ref), custom_call_target="tpu_custom_call" | custom-call | bytes 1048576 | tf_op jit(solution)/shard_map/norm/pallas_call | solution.py:193
  60.4 6.0 %all-to-all-start.2 = ((bf16[64,16,256]{2,1,0:T(8,128)(2,1)}), bf16[64,16,256]{2,1,0:T(8,128)(2,1)S(1)}, u32[]{:S(2)}, u32[]{:S(2)}) async-start(bf16[64,16,256]{2,1,0:T(8,128)(2,1)} %bitcast.10), calls=%async_computation.2 | async-start | bytes 1048576 | tf_op jit(solution)/shard_map/all_to_all | solution.py:214
  66.4 17.3 %all-to-all-done.2 = bf16[64,16,256]{2,1,0:T(8,128)(2,1)S(1)} async-done(((bf16[64,16,256]{2,1,0:T(8,128)(2,1)}), bf16[64,16,256]{2,1,0:T(8,128)(2,1)S(1)}, u32[]{:S(2)}, u32[]{:S(2)}) %all-to-all-start.2) | async-done | bytes 524320 | tf_op jit(solution)/shard_map/all_to_all | solution.py:214
  83.7 1.2 %copy-done.5 = bf16[8,256,256]{2,1,0:T(8,128)(2,1)S(1)} copy-done((bf16[8,256,256]{2,1,0:T(8,128)(2,1)S(1)}, bf16[8,256,256]{2,1,0:T(8,128)(2,1)}, u32[]{:S(2)}) %copy-start.5) | copy-done | bytes 1048600
  84.9 2.2 %ffn.1 = bf16[1024,256]{1,0:T(8,128)(2,1)} custom-call(bf16[1024,256]{1,0:T(8,128)(2,1)S(1)} %bitcast.30, bf16[4,2,256,256]{3,2,1,0:T(8,128)(2,1)S(1)} %bitcast.38), custom_call_target="tpu_custom_call" | custom-call | flops 1000000000 | bytes 1048576 | tf_op jit(solution)/shard_map/ffn/pallas_call | solution.py:193
  87.1 6.4 %all-to-all-start.3 = ((bf16[64,16,256]{2,1,0:T(8,128)(2,1)}), bf16[64,16,256]{2,1,0:T(8,128)(2,1)S(1)}, u32[]{:S(2)}, u32[]{:S(2)}) async-start(bf16[64,16,256]{2,1,0:T(8,128)(2,1)} %bitcast.13), calls=%async_computation.3 | async-start | bytes 1048576 | tf_op jit(solution)/shard_map/all_to_all | solution.py:214
  93.6 0.7 copy-done.3
  94.3 0.9 gate.1.gate_ref
  95.2 15.7 %all-to-all-done.3 = bf16[64,16,256]{2,1,0:T(8,128)(2,1)S(1)} async-done(((bf16[64,16,256]{2,1,0:T(8,128)(2,1)}), bf16[64,16,256]{2,1,0:T(8,128)(2,1)S(1)}, u32[]{:S(2)}, u32[]{:S(2)}) %all-to-all-start.3) | async-done | bytes 524320 | tf_op jit(solution)/shard_map/all_to_all | solution.py:214
  110.9 1.3 %final.1 = bf16[3,512,256]{2,1,0:T(8,128)(2,1)} custom-call(bf16[1024,256]{1,0:T(8,128)(2,1)S(1)} %bitcast.28, bf16[512,1024]{1,0:T(8,128)(2,1)S(1)} %get-tuple-element.11.take_ref, f32[512,128]{1,0:T(8,128)S(1)} %gate.1.gate_ref), custom_call_target="tpu_custom_call" | custom-call | bytes 1048576 | tf_op jit(solution)/shard_map/final/pallas_call | solution.py:193
  (25 shorter events, 0.3 us)
Async XLA Ops:
  6.5 0.9 copy-start
  7.5 26.0 %copy-start.4 = (f32[2,32768,4]{1,2,0:T(4,128)S(1)}, f32[2,32768,4]{1,2,0:T(4,128)}, u32[]{:S(2)}) copy-start(f32[2,32768,4]{1,2,0:T(4,128)} %param.16) | copy-start | bytes 3145732
  8.5 25.0 %all-to-all-start = ((bf16[64,8,256]{2,1,0:T(8,128)(2,1)}), bf16[64,8,256]{2,1,0:T(8,128)(2,1)S(1)}, u32[]{:S(2)}, u32[]{:S(2)}) async-start(bf16[64,8,256]{2,1,0:T(8,128)(2,1)} %bitcast.1), calls=%async_computation | async-start | bytes 524288 | tf_op jit(solution)/shard_map/all_to_all | solution.py:214
  21.5 12.0 %copy-start.6 = (bf16[2,512,256]{2,1,0:T(8,128)(2,1)S(1)}, bf16[2,512,256]{2,1,0:T(8,128)(2,1)}, u32[]{:S(2)}) copy-start(bf16[2,512,256]{2,1,0:T(8,128)(2,1)} %constant.12.clone.first_ref) | copy-start | bytes 1572868
  21.5 44.9 %all-gather.3.cloned.1.call-start = ((), (), s32[]{:S(2)}) async-start(), calls=%async_computation.4 | async-start | bytes 1310720 | tf_op jit(solution)/shard_map/all_gather | solution.py:228
  23.3 10.2 %copy-start.8 = (bf16[2,256,256]{2,1,0:T(8,128)(2,1)S(1)}, bf16[2,256,256]{2,1,0:T(8,128)(2,1)}, u32[]{:S(2)}) copy-start(bf16[2,256,256]{2,1,0:T(8,128)(2,1)} %constant.13.clone.second_ref) | copy-start | bytes 786436
  33.5 1.0 copy-start.7
  34.5 0.9 copy-start.9
  35.5 0.9 copy-start.10
  36.4 1.0 copy-start.11
  40.7 6.2 %copy-start.2 = (s32[1,512,1,1]{1,3,2,0:T(1,128)S(1)}, s32[1,512,1,1]{1,3,2,0:T(1,128)}, u32[]{:S(2)}) copy-start(s32[1,512,1,1]{1,3,2,0:T(1,128)} %param.22) | copy-start | bytes 6148
  40.7 18.2 %all-to-all-start.1 = ((bf16[64,8,256]{2,1,0:T(8,128)(2,1)}), bf16[64,8,256]{2,1,0:T(8,128)(2,1)S(1)}, u32[]{:S(2)}, u32[]{:S(2)}) async-start(bf16[64,8,256]{2,1,0:T(8,128)(2,1)} %bitcast.6), calls=%async_computation.1 | async-start | bytes 524288 | tf_op jit(solution)/shard_map/all_to_all | solution.py:214
  47.9 0.7 copy-start.13
  60.4 23.4 %all-to-all-start.2 = ((bf16[64,16,256]{2,1,0:T(8,128)(2,1)}), bf16[64,16,256]{2,1,0:T(8,128)(2,1)S(1)}, u32[]{:S(2)}, u32[]{:S(2)}) async-start(bf16[64,16,256]{2,1,0:T(8,128)(2,1)} %bitcast.10), calls=%async_computation.2 | async-start | bytes 1048576 | tf_op jit(solution)/shard_map/all_to_all | solution.py:214
  83.7 1.2 %copy-start.5 = (bf16[8,256,256]{2,1,0:T(8,128)(2,1)S(1)}, bf16[8,256,256]{2,1,0:T(8,128)(2,1)}, u32[]{:S(2)}) copy-start(bf16[8,256,256]{2,1,0:T(8,128)(2,1)} %all-gather.3.cloned.1.call-done) | copy-start | bytes 3145732
  87.1 6.4 %copy-start.12 = (s32[1,512,1,3]{1,2,3,0:T(1,128)S(1)}, s32[1,512,1,3]{1,2,3,0:T(1,128)}, u32[]{:S(2)}) copy-start(s32[1,512,1,3]{1,2,3,0:T(1,128)} %param.23) | copy-start | bytes 18436
  87.1 6.5 %copy-start.1 = (bf16[3,256,64]{1,2,0:T(8,128)(2,1)S(1)}, bf16[3,256,64]{1,2,0:T(8,128)(2,1)}, u32[]{:S(2)}) copy-start(bf16[3,256,64]{1,2,0:T(8,128)(2,1)} %param.20) | copy-start | bytes 294916
  87.1 23.7 %all-to-all-start.3 = ((bf16[64,16,256]{2,1,0:T(8,128)(2,1)}), bf16[64,16,256]{2,1,0:T(8,128)(2,1)S(1)}, u32[]{:S(2)}, u32[]{:S(2)}) async-start(bf16[64,16,256]{2,1,0:T(8,128)(2,1)} %bitcast.13), calls=%async_computation.3 | async-start | bytes 1048576 | tf_op jit(solution)/shard_map/all_to_all | solution.py:214
  93.6 0.7 copy-start.3
Sparse Core Ops, SparseCore 0:
  24.1 26.7 all-gather.2

commit v2 on v1

--- a/solution.py
+++ b/solution.py
@@ -45,13 +45,11 @@
     cos_r, sin_r = cos_sin(ROWS, ROWS, ROWS)
     cos_c, sin_c = cos_sin(COLS, COLS, COLS)
     tw_cos, tw_sin = cos_sin(ROWS, COLS, LENGTH)
-    first = np.stack(np_split(np.concatenate([cos_r, -sin_r], 0)))
-    second = np.stack(np_split(np.block([[cos_c, sin_c], [-sin_c, cos_c]])))
-    third = np.stack(np_split(np.block([[cos_c, -sin_c], [sin_c, cos_c]])))
-    fourth = np.stack(np_split(np.concatenate([cos_r, -sin_r], 1) / LENGTH))
-    turn = np.stack([tw_cos, tw_sin]).astype(np.float32)
-    turn_back = np.stack([tw_cos.T, tw_sin.T]).astype(np.float32)
-    return first, second, third, fourth, turn, turn_back
+    first = np.concatenate([cos_r, -sin_r], 0)
+    second = np.block([[cos_c, sin_c], [-sin_c, cos_c]])
+    factors = np.concatenate([part for m in (first, second) for part in np_split(m)])
+    turns = [t[i : i + 128] for t in (tw_cos, tw_sin) for i in (0, 128)]
+    return factors, np.stack(turns).astype(np.float32)
 
 
 def join_lanes(wide, out_ref):
@@ -67,23 +65,32 @@
     )
 
 
-def prep_kernel(ev_ref, out_ref, mid, wide):
+def prep_kernel(ev_ref, out_ref, landed, mid, wide, sems):
+    copies = [
+        pltpu.make_async_copy(
+            ev_ref.at[pl.ds(pb * 128, 128)], landed.at[pl.ds(pb * 128, 128)], sems.at[pb]
+        )
+        for pb in range(4)
+    ]
+    for copy in copies:
+        copy.start()
     for pb in range(4):
-        mid[...] = ev_ref[pb * 128 : (pb + 1) * 128, :].astype(F32).T
+        copies[pb].wait()
+        mid[...] = landed[pb * 128 : (pb + 1) * 128, :].astype(F32).T
         for ch in range(4):
             chp, chl = ch // 2, ch % 2
             wide[chl, pl.ds(pb * 2 + chp, 64, stride=8), :] = mid[pl.ds(ch, 64, stride=4), :]
     join_lanes(wide, out_ref)
 
 
-def filter_kernel(
-    x_ref, spec_ref, first_ref, second_ref, third_ref, fourth_ref, turn_ref, back_ref,
-    out_ref, wide, sums,
-):
+def filter_kernel(x_ref, spec_ref, factor_ref, turn_ref, out_ref, wide, sums):
+    first = factor_ref[0:512], factor_ref[512:1024]
+    second = factor_ref[1024:1280], factor_ref[1280:1536]
+    fourth = [jnp.concatenate([part[:256], part[256:]], 1) for part in first]
     sig = deinterleave(x_ref, wide)
     sig16 = sig.astype(BF16)
-    spec1 = dot(first_ref[0], sig16, NN) + dot(first_ref[1], sig16, NN)
-    tcos, tsin = turn_ref[0], turn_ref[1]
+    spec1 = dot(first[0], sig16, NN) + dot(first[1], sig16, NN)
+    tcos, tsin = [jnp.concatenate([turn_ref[i], turn_ref[i + 1]], 0) for i in (0, 2)]
     turned = []
     for ch in range(4):
         re = spec1[:256, ch * 128 : (ch + 1) * 128]
@@ -91,32 +98,28 @@
         turned.append(jnp.concatenate([re * tcos + im * tsin, im * tcos - re * tsin], 1))
     t_hi, t_lo = split(jnp.concatenate(turned, 0))
     spec2 = (
-        dot(second_ref[0], t_hi, NT) + dot(second_ref[0], t_lo, NT) + dot(second_ref[1], t_hi, NT)
+        dot(second[0], t_hi, NT) + dot(second[0], t_lo, NT) + dot(second[1], t_hi, NT)
     )
     prods = []
     for ch in range(4):
-        fr = jnp.concatenate(
-            [spec_ref[0, pl.ds(4 * h + ch, 128, stride=8), :] for h in range(2)], 1
-        )
-        fi = jnp.concatenate(
-            [spec_ref[1, pl.ds(4 * h + ch, 128, stride=8), :] for h in range(2)], 1
-        )
+        fr = spec_ref[0, :, ch * 256 : (ch + 1) * 256]
+        fi = spec_ref[1, :, ch * 256 : (ch + 1) * 256]
         zr = spec2[:128, ch * 256 : (ch + 1) * 256]
         zi = spec2[128:, ch * 256 : (ch + 1) * 256]
-        prods.append(jnp.concatenate([zr * fr - zi * fi, zr * fi + zi * fr], 0))
+        prods.append(jnp.concatenate([zr * fi + zi * fr, zr * fr - zi * fi], 0))
     p_hi, p_lo = split(jnp.concatenate(prods, 1))
-    back = dot(third_ref[0], p_hi, NN) + dot(third_ref[0], p_lo, NN) + dot(third_ref[1], p_hi, NN)
-    bcos, bsin = back_ref[0], back_ref[1]
+    back = dot(second[0], p_hi, NN) + dot(second[0], p_lo, NN) + dot(second[1], p_hi, NN)
+    bcos, bsin = [jnp.concatenate([turn_ref[i].T, turn_ref[i + 1].T], 1) for i in (0, 2)]
     turned = []
     for ch in range(4):
-        re = back[:128, ch * 256 : (ch + 1) * 256]
-        im = back[128:, ch * 256 : (ch + 1) * 256]
+        im = back[:128, ch * 256 : (ch + 1) * 256]
+        re = back[128:, ch * 256 : (ch + 1) * 256]
         turned.append(jnp.concatenate([re * bcos - im * bsin, im * bcos + re * bsin], 1))
     v_hi, v_lo = split(jnp.concatenate(turned, 0))
     filtered = (
-        dot(fourth_ref[0], v_hi, NT) + dot(fourth_ref[0], v_lo, NT) + dot(fourth_ref[1], v_hi, NT)
-    )
-    summed = sig + filtered
+        dot(fourth[0], v_hi, NT) + dot(fourth[0], v_lo, NT) + dot(fourth[1], v_hi, NT)
+    )
+    summed = sig + filtered * (1.0 / LENGTH)
     for ch in range(4):
         sums[ch] = summed[:, ch * 128 : (ch + 1) * 128]
     for pb in range(4):
@@ -127,7 +130,28 @@
     join_lanes(wide, out_ref)
 
 
-def route_kernel(routes_ref, put_ref, take_ref):
+def ready_kernel(
+    after_ref, spec_ref, factor_ref, turn_ref, spec_out, factor_out, turn_out, raw, sems
+):
+    copies = [
+        pltpu.make_async_copy(src, dst, sems.at[i])
+        for i, (src, dst) in enumerate(
+            ((spec_ref, raw), (factor_ref, factor_out), (turn_ref, turn_out))
+        )
+    ]
+    for copy in copies:
+        copy.start()
+    copies[0].wait()
+    for part in range(2):
+        for ch in range(4):
+            for half in range(2):
+                at = ch * 256 + half * 128
+                spec_out[part, :, at : at + 128] = raw[part, pl.ds(4 * half + ch, 128, stride=8), :]
+    copies[1].wait()
+    copies[2].wait()
+
+
+def route_kernel(after_ref, routes_ref, put_ref, slot_ref):
     experts = routes_ref[...]
     onehot = (lax.broadcasted_iota(jnp.int32, (EXPERTS, 512), 0) == experts).astype(F32)
     before = lax.broadcasted_iota(jnp.int32, (512, 512), 0) < lax.broadcasted_iota(
@@ -139,10 +163,7 @@
     put_ref[...] = (
         lax.broadcasted_iota(jnp.int32, (EXPERTS * CAP, 512), 0) == slot.astype(jnp.int32)
     ).astype(F32).astype(BF16)
-    slot_col = jnp.broadcast_to(slot, (128, 512)).T[:, 0:1].astype(jnp.int32)
-    take_ref[...] = (
-        lax.broadcasted_iota(jnp.int32, (512, EXPERTS * CAP), 1) == slot_col
-    ).astype(F32).astype(BF16)
+    slot_ref[...] = jnp.broadcast_to(slot, (8, 512))
 
 
 def norm_kernel(x_ref, gain_ref, put_ref, out_ref, normed_ref, wide):
@@ -155,7 +176,13 @@
     out_ref[...] = dot(put_ref[...], normed, NT).astype(BF16)
 
 
-def gate_kernel(normed_ref, weight_ref, routes_ref, index_ref, table_ref, out_ref):
+def gate_kernel(
+    after_ref, normed_ref, weight_ref, routes_ref, index_ref, table_ref, slot_ref, out_ref, take_ref
+):
+    slot_col = jnp.broadcast_to(slot_ref[0:1, :], (128, 512)).T[:, 0:1].astype(jnp.int32)
+    take_ref[...] = (
+        lax.broadcasted_iota(jnp.int32, (512, EXPERTS * CAP), 1) == slot_col
+    ).astype(F32).astype(BF16)
     scores = dot(weight_ref[...], normed_ref[...], NN)
     mask = lax.broadcasted_iota(jnp.int32, (EXPERTS, 512), 0) == routes_ref[...]
     rows = []
@@ -171,11 +198,14 @@
     out_ref[...] = jnp.concatenate(rows, 0).T
 
 
-def ffn_kernel(x_ref, weights_ref, out_ref):
-    w_in = weights_ref[:, 0].reshape(1024, 256)
-    w_out = weights_ref[:, 1].reshape(1024, 256)
-    hidden = jnp.maximum(dot(x_ref[...], w_in, NT), 0.0).astype(BF16)
-    out_ref[...] = dot(hidden, w_out, NN).astype(BF16)
+def ffn_kernel(x_ref, own_ref, one_ref, two_ref, three_ref, out_ref):
+    x = x_ref[...]
+    total = None
+    for part in (own_ref, one_ref, two_ref, three_ref):
+        hidden = jnp.maximum(dot(x, part[0], NT), 0.0).astype(BF16)
+        term = dot(hidden, part[1], NN)
+        total = term if total is None else total + term
+    out_ref[...] = total.astype(BF16)
 
 
 def final_kernel(slots_ref, take_ref, gate_ref, out_ref):
@@ -184,9 +214,9 @@
         out_ref[t] = (gate_ref[:, t : t + 1] * rows).astype(BF16)
 
 
-def call(kernel, outs, *args, scratch=(), smem=(), flops=0, name=None):
+def call(kernel, outs, *args, scratch=(), smem=(), far=(), flops=0, name=None):
     specs = [
-        pl.BlockSpec(memory_space=pltpu.SMEM if i in smem else pltpu.VMEM)
+        pl.BlockSpec(memory_space=pltpu.SMEM if i in smem else pl.ANY if i in far else pltpu.VMEM)
         for i in range(len(args))
     ]
     many = isinstance(outs, (tuple, list))
@@ -222,33 +252,48 @@
     big = pltpu.VMEM
     chunks = call(
         prep_kernel, shape((512, 256), BF16), events.reshape(512, 256),
-        scratch=[big((256, 128), F32), big((2, 512, 128), F32)], name="prep",
+        far=(0,), name="prep",
+        scratch=[
+            big((512, 256), BF16), big((256, 128), F32), big((2, 512, 128), F32),
+            pltpu.SemaphoreType.DMA((4,)),
+        ],
     )
     arrived = swap(chunks, 8)
-    weights = lax.all_gather(jnp.stack([w_in[0], w_out[0]]), "batch", axis=0, tiled=False)
+    own = jnp.stack([w_in[0], w_out[0]])
+    weights = [own] + [
+        lax.ppermute(own, "batch", [(i, (i + d) % 4) for i in range(4)]) for d in (1, 3, 2)
+    ]
     route_row = routes.reshape(1, 512)
-    put, take = call(
-        route_kernel, [shape((1024, 512), BF16), shape((512, 1024), BF16)], route_row, name="route"
-    )
     spec = spectral_filter.reshape(2, 256, 128, 4).transpose(0, 1, 3, 2).reshape(2, 1024, 128)
-    consts = [jnp.asarray(t) for t in tables()]
+    factors, turns = [jnp.asarray(t) for t in tables()]
+    spec, factors, turns = call(
+        ready_kernel,
+        [shape((2, 128, 1024), F32), shape(factors.shape, BF16), shape(turns.shape, F32)],
+        chunks, spec, factors, turns, far=(0, 1, 2, 3), name="ready",
+        scratch=[big((2, 1024, 128), F32), pltpu.SemaphoreType.DMA((3,))], flops=2 * 10**9,
+    )
     sums = call(
-        filter_kernel, shape((512, 256), BF16), arrived, spec, *consts,
+        filter_kernel, shape((512, 256), BF16), arrived, spec, factors, turns,
         scratch=[big((2, 512, 128), F32), big((4, 256, 128), F32)], name="filter", flops=2 * 10**9,
     )
     returned = swap(sums, 8)
+    put, slot = call(
+        route_kernel, [shape((1024, 512), BF16), shape((8, 512), F32)], sums, route_row,
+        far=(0,), name="route", flops=2 * 10**9,
+    )
     outgoing, normed = call(
         norm_kernel, [shape((1024, 256), BF16), shape((256, 512), BF16)],
         returned, ln_gain.reshape(256, 1), put, scratch=[big((2, 512, 128), F32)], name="norm",
     )
     slots_in = swap(outgoing, 16)
-    gates = call(
-        gate_kernel, shape((512, 128), F32), normed,
+    slots_out = call(ffn_kernel, shape((1024, 256), BF16), slots_in, *weights, name="ffn", flops=10**9)
+    results = swap(slots_out, 16)
+    gates, take = call(
+        gate_kernel, [shape((512, 128), F32), shape((512, 1024), BF16)], slots_out, normed,
         gate_weight.transpose(0, 2, 1).reshape(192, 256), route_row,
-        gate_index.reshape(512, 3).T, gate_table, smem=(4,), name="gate",
-    )
-    slots_out = call(ffn_kernel, shape((1024, 256), BF16), slots_in, weights, name="ffn", flops=10**9)
-    results = swap(slots_out, 16)
+        gate_index.reshape(512, 3).T, gate_table, slot, far=(0,), smem=(5,), name="gate",
+        flops=2 * 10**9,
+    )
     out = call(final_kernel, shape((3, 512, 256), BF16), results, take, gates, name="final")
     return out.reshape(TASKS, 1, 512, 1, 256)
 

time: 120 us -> 106 us (0.88)
  between operations: 13.5 us -> 0.17 us
  starting transfers between devices: 31.6 us -> 40.2 us
  waiting for transfers between devices: 53.3 us -> 46.9 us
  other arithmetic: 1.75 us -> 0 us
  local copies, waits for them, and re-layouts: 7.57 us -> 5.96 us
    all_to_all x4, waiting for transfers between devices: 53.3 us -> 35.8 us  [swap(): lax.all_to_all(chunks, 'seq', split_axis=0, concat_axis=0, tiled=True)]
    ppermute x0 -> x3, waiting for transfers between devices: none -> 11.1 us  [on_device(): lax.ppermute(own, 'batch', [(i, (i + d) % 4) for i in range(4)])]
    ppermute x0 -> x3, starting transfers between devices: none -> 4.45 us  [on_device(): lax.ppermute(own, 'batch', [(i, (i + d) % 4) for i in range(4)])]
    all_to_all x4, starting transfers between devices: 31.6 us -> 35.8 us  [swap(): lax.all_to_all(chunks, 'seq', split_axis=0, concat_axis=0, tiled=True)]
    another operation x1 -> x0, other arithmetic: 1.75 us -> none  [on_device(): jnp.stack([w_in[0], w_out[0]])]
    unnamed x29 -> x24, local copies, waits for them, and re-layouts: 7.44 us -> 5.82 us
    pallas_call x7 -> x8, Pallas kernels: 11.3 us -> 12.2 us  [call(): pl.pallas_call(kernel, out_shape=outs, in_specs=specs, out_specs=[pl.Bloc...]
  transfers between devices with their start and end apart: 5 -> 7, of which waited for: 4 -> 6; matrix products, arithmetic and copies ran while one was open for 2% -> 0% of each run, Pallas kernels for 6% -> 2%
where the time goes in v2:
time: 106 us; the launch traced here: 105 us
  waiting for transfers between devices  46.9 us (44%)
  starting transfers between devices  40.2 us (38%)
  Pallas kernels  12.2 us (12%)
  local copies, waits for them, and re-layouts  5.96 us (6%)
    all_to_all x4, waiting for transfers between devices, swap(): lax.all_to_all(chunks, 'seq', split_axis=0, concat_axis=0, tiled=True)  35.8 us
    all_to_all x4, starting transfers between devices, swap(): lax.all_to_all(chunks, 'seq', split_axis=0, concat_axis=0, tiled=True)  35.8 us
    pallas_call x8, Pallas kernels, call(): pl.pallas_call(kernel, out_shape=outs, in_specs=specs, out_specs=[pl.Bloc...  12.2 us
    ppermute x3, waiting for transfers between devices, on_device(): lax.ppermute(own, 'batch', [(i, (i + d) % 4) for i in range(4)])  11.1 us
    unnamed x24, local copies, waits for them, and re-layouts  5.82 us
    ppermute x3, starting transfers between devices, on_device(): lax.ppermute(own, 'batch', [(i, (i + d) % 4) for i in range(4)])  4.45 us
  transfers between devices with their start and end apart: 7, of which 6 were waited for; matrix products, arithmetic and copies ran while one was open for 0% of the time, Pallas kernels for 2%

profile of v2, /device:TPU:1, one launch (start us, length us, event | category | flops | bytes accessed | tf_op | source)
XLA Modules:
  0.0 105.5 jit_solution(5797963685940933072)
XLA Ops:
  0.0 0.9 copy-done
  1.0 1.6 %prep.1.after_ref = bf16[512,256]{1,0:T(8,128)(2,1)} custom-call(bf16[512,256]{1,0:T(8,128)(2,1)S(1)} %bitcast.30), custom_call_target="tpu_custom_call" | custom-call | bytes 1048576 | tf_op jit(solution)/shard_map/prep/pallas_call | solution.py:223
  2.6 13.0 %all-to-all-start = ((bf16[64,8,256]{2,1,0:T(8,128)(2,1)}), bf16[64,8,256]{2,1,0:T(8,128)(2,1)S(1)}, u32[]{:S(2)}, u32[]{:S(2)}) async-start(bf16[64,8,256]{2,1,0:T(8,128)(2,1)} %bitcast.1), calls=%async_computation | async-start | bytes 524288 | tf_op jit(solution)/shard_map/all_to_all | solution.py:244
  15.6 1.1 %copy-done.5 = bf16[1536,256]{1,0:T(8,128)(2,1)S(1)} copy-done((bf16[1536,256]{1,0:T(8,128)(2,1)S(1)}, bf16[1536,256]{1,0:T(8,128)(2,1)}, u32[]{:S(2)}) %copy-start.5) | copy-done | bytes 786456
  16.7 0.9 copy-done.6
  18.0 9.5 %all-to-all-done = bf16[64,8,256]{2,1,0:T(8,128)(2,1)S(1)} async-done(((bf16[64,8,256]{2,1,0:T(8,128)(2,1)}), bf16[64,8,256]{2,1,0:T(8,128)(2,1)S(1)}, u32[]{:S(2)}, u32[]{:S(2)}) %all-to-all-start) | async-done | bytes 262176 | tf_op jit(solution)/shard_map/all_to_all | solution.py:244
  27.6 3.2 %filter.1.after_ref = bf16[512,256]{1,0:T(8,128)(2,1)} custom-call(bf16[512,256]{1,0:T(8,128)(2,1)S(1)} %bitcast.31, f32[2,128,1024]{2,1,0:T(8,128)S(1)} %get-tuple-element.14.spec_ref, bf16[1536,256]{1,0:T(8,128)(2,1)S(1)} %get-tuple-element.15.factor_ref, f32[4,128,128]{2,1,0:T(8,128)S(1)} %get-tuple-element.16.turn_ref), custom_call_target="tpu_custom_call" | custom-call | flops 2000000000 | bytes 1048576 | tf_op jit(solution)/shard_map/filter/pallas_call | solution.py:223
  30.8 6.0 %all-to-all-start.1 = ((bf16[64,8,256]{2,1,0:T(8,128)(2,1)}), bf16[64,8,256]{2,1,0:T(8,128)(2,1)S(1)}, u32[]{:S(2)}, u32[]{:S(2)}) async-start(bf16[64,8,256]{2,1,0:T(8,128)(2,1)} %bitcast.6), calls=%async_computation.1 | async-start | bytes 524288 | tf_op jit(solution)/shard_map/all_to_all | solution.py:244
  36.8 0.7 copy-done.10
  38.9 10.0 %all-to-all-done.1 = bf16[64,8,256]{2,1,0:T(8,128)(2,1)S(1)} async-done(((bf16[64,8,256]{2,1,0:T(8,128)(2,1)}), bf16[64,8,256]{2,1,0:T(8,128)(2,1)S(1)}, u32[]{:S(2)}, u32[]{:S(2)}) %all-to-all-start.1) | async-done | bytes 262176 | tf_op jit(solution)/shard_map/all_to_all | solution.py:244
  48.8 1.5 %norm.1 = (bf16[1024,256]{1,0:T(8,128)(2,1)}, bf16[256,512]{1,0:T(8,128)(2,1)S(1)}) custom-call(bf16[512,256]{1,0:T(8,128)(2,1)S(1)} %bitcast.28, f32[256,1]{1,0:T(8,128)S(1)} %copy.15.gain_ref, bf16[1024,512]{1,0:T(8,128)(2,1)S(1)} %get-tuple-element.17.put_ref), custom_call_target="tpu_custom_call" | custom-call | bytes 1048576 | tf_op jit(solution)/shard_map/norm/pallas_call | solution.py:223
  50.3 6.2 %all-to-all-start.2 = ((bf16[64,16,256]{2,1,0:T(8,128)(2,1)}), bf16[64,16,256]{2,1,0:T(8,128)(2,1)S(1)}, u32[]{:S(2)}, u32[]{:S(2)}) async-start(bf16[64,16,256]{2,1,0:T(8,128)(2,1)} %bitcast.10), calls=%async_computation.2 | async-start | bytes 1048576 | tf_op jit(solution)/shard_map/all_to_all | solution.py:244
  56.5 0.9 copy-done.8
  57.4 1.4 %collective-permute-start = (bf16[2,256,256]{2,1,0:T(8,128)(2,1)S(1)}, bf16[2,256,256]{2,1,0:T(8,128)(2,1)S(1)}, u32[]{:S(2)}, u32[]{:S(2)}) collective-permute-start(bf16[2,256,256]{2,1,0:T(8,128)(2,1)S(1)} %constant_dynamic-update-slice_fusion.own_ref), channel_id=1, source_target_pairs={{0,1},{1,2},{2,3},{3,0},{4,5},{5,6},{6,7},{7,4},{8,9},{9,10},{10,1... | collective-permute-start | bytes 786440 | tf_op jit(solution)/shard_map/ppermute | solution.py:264
  58.8 1.5 %collective-permute-start.1 = (bf16[2,256,256]{2,1,0:T(8,128)(2,1)S(1)}, bf16[2,256,256]{2,1,0:T(8,128)(2,1)S(1)}, u32[]{:S(2)}, u32[]{:S(2)}) collective-permute-start(bf16[2,256,256]{2,1,0:T(8,128)(2,1)S(1)} %constant_dynamic-update-slice_fusion.own_ref), channel_id=1, source_target_pairs={{0,3},{1,0},{2,1},{3,2},{4,7},{5,4},{6,5},{7,6},{8,11},{9,8},{10,9... | collective-permute-start | bytes 786440 | tf_op jit(solution)/shard_map/ppermute | solution.py:264
  60.3 1.6 %collective-permute-start.2 = (bf16[2,256,256]{2,1,0:T(8,128)(2,1)S(1)}, bf16[2,256,256]{2,1,0:T(8,128)(2,1)S(1)}, u32[]{:S(2)}, u32[]{:S(2)}) collective-permute-start(bf16[2,256,256]{2,1,0:T(8,128)(2,1)S(1)} %constant_dynamic-update-slice_fusion.own_ref), channel_id=1, source_target_pairs={{0,2},{1,3},{2,0},{3,1},{4,6},{5,7},{6,4},{7,5},{8,10},{9,11},{10,... | collective-permute-start | bytes 786440 | tf_op jit(solution)/shard_map/ppermute | solution.py:264
  61.9 4.4 %collective-permute-done.one_ref = bf16[2,256,256]{2,1,0:T(8,128)(2,1)S(1)} collective-permute-done((bf16[2,256,256]{2,1,0:T(8,128)(2,1)S(1)}, bf16[2,256,256]{2,1,0:T(8,128)(2,1)S(1)}, u32[]{:S(2)}, u32[]{:S(2)}) %collective-permute-start) | collective-permute-done | bytes 262176 | tf_op jit(solution)/shard_map/ppermute | solution.py:264
  66.2 6.7 %collective-permute-done.2.three_ref = bf16[2,256,256]{2,1,0:T(8,128)(2,1)S(1)} collective-permute-done((bf16[2,256,256]{2,1,0:T(8,128)(2,1)S(1)}, bf16[2,256,256]{2,1,0:T(8,128)(2,1)S(1)}, u32[]{:S(2)}, u32[]{:S(2)}) %collective-permute-start.2) | collective-permute-done | bytes 262176 | tf_op jit(solution)/shard_map/ppermute | solution.py:264
  73.0 0.8 all-to-all-done.2
  73.8 2.5 %ffn.1.after_ref = bf16[1024,256]{1,0:T(8,128)(2,1)} custom-call(bf16[1024,256]{1,0:T(8,128)(2,1)S(1)} %bitcast.29, bf16[2,256,256]{2,1,0:T(8,128)(2,1)S(1)} %constant_dynamic-update-slice_fusion.own_ref, bf16[2,256,256]{2,1,0:T(8,128)(2,1)S(1)} %collective-permute-done.one_ref, bf16[2,256,256]{2,1,0:T(8,128)(2,1)S(1)} %collective-permute-done.1.two_ref, ...), custom_call_target="tpu_custom_call" | custom-call | flops 1000000000 | bytes 1048576 | tf_op jit(solution)/shard_map/ffn/pallas_call | solution.py:223
  76.3 10.6 %all-to-all-start.3 = ((bf16[64,16,256]{2,1,0:T(8,128)(2,1)}), bf16[64,16,256]{2,1,0:T(8,128)(2,1)S(1)}, u32[]{:S(2)}, u32[]{:S(2)}) async-start(bf16[64,16,256]{2,1,0:T(8,128)(2,1)} %bitcast.12), calls=%async_computation.3 | async-start | bytes 1048576 | tf_op jit(solution)/shard_map/all_to_all | solution.py:244
  87.5 1.1 %gate.1 = (f32[512,128]{1,0:T(8,128)S(1)}, bf16[512,1024]{1,0:T(8,128)(2,1)S(1)}) custom-call(bf16[1024,256]{1,0:T(8,128)(2,1)} %ffn.1.after_ref, bf16[256,512]{1,0:T(8,128)(2,1)S(1)} %get-tuple-element.19.normed_ref, bf16[192,256]{1,0:T(8,128)(2,1)S(1)} %bitcast.34, s32[1,512]{1,0:T(1,128)S(1)} %bitcast.36, s32[3,512]{1,0:T(4,128)S(1)} %bitcast.32, ...), custom_call_target="tpu_custom_call" | custom-call | flops 2000000000 | bytes 1048576 | tf_op jit(solution)/shard_map/gate/pallas_call | solution.py:223
  88.7 15.5 %all-to-all-done.3 = bf16[64,16,256]{2,1,0:T(8,128)(2,1)S(1)} async-done(((bf16[64,16,256]{2,1,0:T(8,128)(2,1)}), bf16[64,16,256]{2,1,0:T(8,128)(2,1)S(1)}, u32[]{:S(2)}, u32[]{:S(2)}) %all-to-all-start.3) | async-done | bytes 524320 | tf_op jit(solution)/shard_map/all_to_all | solution.py:244
  104.2 1.3 %final.1 = bf16[3,512,256]{2,1,0:T(8,128)(2,1)} custom-call(bf16[1024,256]{1,0:T(8,128)(2,1)S(1)} %bitcast.27, bf16[512,1024]{1,0:T(8,128)(2,1)S(1)} %get-tuple-element.21.take_ref, f32[512,128]{1,0:T(8,128)S(1)} %get-tuple-element.22.gate_ref), custom_call_target="tpu_custom_call" | custom-call | bytes 1048576 | tf_op jit(solution)/shard_map/final/pallas_call | solution.py:223
  (24 shorter events, 2.4 us)
Async XLA Ops:
  0.0 0.9 copy-start
  1.0 14.6 %copy-start.1 = (f32[2,32768,4]{1,2,0:T(4,128)S(1)}, f32[2,32768,4]{1,2,0:T(4,128)}, u32[]{:S(2)}) copy-start(f32[2,32768,4]{1,2,0:T(4,128)} %param.12) | copy-start | bytes 3145732
  2.6 25.0 %all-to-all-start = ((bf16[64,8,256]{2,1,0:T(8,128)(2,1)}), bf16[64,8,256]{2,1,0:T(8,128)(2,1)S(1)}, u32[]{:S(2)}, u32[]{:S(2)}) async-start(bf16[64,8,256]{2,1,0:T(8,128)(2,1)} %bitcast.1), calls=%async_computation | async-start | bytes 524288 | tf_op jit(solution)/shard_map/all_to_all | solution.py:244
  15.6 1.1 %copy-start.5 = (bf16[1536,256]{1,0:T(8,128)(2,1)S(1)}, bf16[1536,256]{1,0:T(8,128)(2,1)}, u32[]{:S(2)}) copy-start(bf16[1536,256]{1,0:T(8,128)(2,1)} %constant.4.clone.factor_ref) | copy-start | bytes 2359300
  16.7 0.9 copy-start.6
  30.8 18.0 %all-to-all-start.1 = ((bf16[64,8,256]{2,1,0:T(8,128)(2,1)}), bf16[64,8,256]{2,1,0:T(8,128)(2,1)S(1)}, u32[]{:S(2)}, u32[]{:S(2)}) async-start(bf16[64,8,256]{2,1,0:T(8,128)(2,1)} %bitcast.6), calls=%async_computation.1 | async-start | bytes 524288 | tf_op jit(solution)/shard_map/all_to_all | solution.py:244
  36.8 0.7 copy-start.10
  37.5 0.7 copy-start.3
  50.3 6.2 %copy-start.7 = (bf16[1,256,256]{2,1,0:T(8,128)(2,1)S(1)}, bf16[1,256,256]{2,1,0:T(8,128)(2,1)}, u32[]{:S(2)}) copy-start(bf16[1,256,256]{2,1,0:T(8,128)(2,1)} %param.14) | copy-start | bytes 393220
  50.3 23.5 %all-to-all-start.2 = ((bf16[64,16,256]{2,1,0:T(8,128)(2,1)}), bf16[64,16,256]{2,1,0:T(8,128)(2,1)S(1)}, u32[]{:S(2)}, u32[]{:S(2)}) async-start(bf16[64,16,256]{2,1,0:T(8,128)(2,1)} %bitcast.10), calls=%async_computation.2 | async-start | bytes 1048576 | tf_op jit(solution)/shard_map/all_to_all | solution.py:244
  56.5 0.9 copy-start.8
  57.4 8.8 %collective-permute-start = (bf16[2,256,256]{2,1,0:T(8,128)(2,1)S(1)}, bf16[2,256,256]{2,1,0:T(8,128)(2,1)S(1)}, u32[]{:S(2)}, u32[]{:S(2)}) collective-permute-start(bf16[2,256,256]{2,1,0:T(8,128)(2,1)S(1)} %constant_dynamic-update-slice_fusion.own_ref), channel_id=1, source_target_pairs={{0,1},{1,2},{2,3},{3,0},{4,5},{5,6},{6,7},{7,4},{8,9},{9,10},{10,1... | collective-permute-start | bytes 786440 | tf_op jit(solution)/shard_map/ppermute | solution.py:264
  58.8 7.5 %collective-permute-start.1 = (bf16[2,256,256]{2,1,0:T(8,128)(2,1)S(1)}, bf16[2,256,256]{2,1,0:T(8,128)(2,1)S(1)}, u32[]{:S(2)}, u32[]{:S(2)}) collective-permute-start(bf16[2,256,256]{2,1,0:T(8,128)(2,1)S(1)} %constant_dynamic-update-slice_fusion.own_ref), channel_id=1, source_target_pairs={{0,3},{1,0},{2,1},{3,2},{4,7},{5,4},{6,5},{7,6},{8,11},{9,8},{10,9... | collective-permute-start | bytes 786440 | tf_op jit(solution)/shard_map/ppermute | solution.py:264
  60.3 12.7 %collective-permute-start.2 = (bf16[2,256,256]{2,1,0:T(8,128)(2,1)S(1)}, bf16[2,256,256]{2,1,0:T(8,128)(2,1)S(1)}, u32[]{:S(2)}, u32[]{:S(2)}) collective-permute-start(bf16[2,256,256]{2,1,0:T(8,128)(2,1)S(1)} %constant_dynamic-update-slice_fusion.own_ref), channel_id=1, source_target_pairs={{0,2},{1,3},{2,0},{3,1},{4,6},{5,7},{6,4},{7,5},{8,10},{9,11},{10,... | collective-permute-start | bytes 786440 | tf_op jit(solution)/shard_map/ppermute | solution.py:264
  76.3 10.6 %copy-start.9 = (s32[1,512,1,3]{1,2,3,0:T(1,128)S(1)}, s32[1,512,1,3]{1,2,3,0:T(1,128)}, u32[]{:S(2)}) copy-start(s32[1,512,1,3]{1,2,3,0:T(1,128)} %param.19) | copy-start | bytes 18436
  76.3 10.6 %copy-start.2 = (bf16[3,256,64]{1,2,0:T(8,128)(2,1)S(1)}, bf16[3,256,64]{1,2,0:T(8,128)(2,1)}, u32[]{:S(2)}) copy-start(bf16[3,256,64]{1,2,0:T(8,128)(2,1)} %param.16) | copy-start | bytes 294916
  76.3 27.9 %all-to-all-start.3 = ((bf16[64,16,256]{2,1,0:T(8,128)(2,1)}), bf16[64,16,256]{2,1,0:T(8,128)(2,1)S(1)}, u32[]{:S(2)}, u32[]{:S(2)}) async-start(bf16[64,16,256]{2,1,0:T(8,128)(2,1)} %bitcast.12), calls=%async_computation.3 | async-start | bytes 1048576 | tf_op jit(solution)/shard_map/all_to_all | solution.py:244
  86.9 0.7 copy-start.4

commit v3 on v2

v3 whole, which is shorter than its diff:
```python
import functools

import jax
import jax.numpy as jnp
import ml_dtypes
import numpy as np
from jax import lax
from jax.experimental import pallas as pl
from jax.experimental.pallas import tpu as pltpu
from jax.sharding import PartitionSpec as P

EXPERTS = 64
TASKS = 3
CAP = 16
ROWS = 256
COLS = 128
LENGTH = ROWS * COLS
BF16 = jnp.bfloat16
F32 = jnp.float32

NN = (((1,), (0,)), ((), ()))
NT = (((1,), (1,)), ((), ()))


def dot(a, b, dims):
    return lax.dot_general(a, b, dims, preferred_element_type=F32)


def split(x):
    hi = x.astype(BF16)
    return hi, (x - hi.astype(F32)).astype(BF16)


def np_split(x):
    hi = x.astype(ml_dtypes.bfloat16)
    return hi, (x - hi.astype(np.float64)).astype(ml_dtypes.bfloat16)


def cos_sin(rows, cols, points):
    angle = 2.0 * np.pi * (np.outer(np.arange(rows), np.arange(cols)) % points) / points
    return np.cos(angle), np.sin(angle)


def tables():
    order = np.arange(ROWS).reshape(64, 4).T.reshape(-1)
    cos_r, sin_r = cos_sin(ROWS, ROWS, ROWS)
    cos_c, sin_c = cos_sin(COLS, COLS, COLS)
    tw_cos, tw_sin = cos_sin(ROWS, COLS, LENGTH)
    first = np.concatenate([cos_r[:, order], -sin_r[:, order]], 0)
    second = np.block([[cos_c, sin_c], [-sin_c, cos_c]])
    fourth = np.concatenate([cos_r[order], -sin_r[order]], 0)
    factors = np.concatenate([part for m in (first, second, fourth) for part in np_split(m)])
    turns = [t[i : i + 128] for t in (tw_cos, tw_sin) for i in (0, 128)]
    lane = np.arange(512)
    source = (lane // 16 % 8) * 64 + (lane // 128) * 16 + lane % 16
    lanes = (lane[:, None] == source[None, :]).astype(ml_dtypes.bfloat16)
    return factors, np.stack(turns).astype(np.float32), lanes


def prep_kernel(ev_ref, routes_ref, out_ref, slot_ref, landed, named, mid, wide, sems):
    copies = [
        pltpu.make_async_copy(
            ev_ref.at[pl.ds(pb * 128, 128)], landed.at[pl.ds(pb * 128, 128)], sems.at[pb]
        )
        for pb in range(4)
    ]
    copies.append(pltpu.make_async_copy(routes_ref, named, sems.at[4]))
    for copy in copies[::-1]:
        copy.start()
    copies[4].wait()
    experts = named[...]
    onehot = (lax.broadcasted_iota(jnp.int32, (EXPERTS, 512), 0) == experts).astype(F32)
    before = lax.broadcasted_iota(jnp.int32, (512, 512), 0) < lax.broadcasted_iota(
        jnp.int32, (512, 512), 1
    )
    earlier = dot(onehot.astype(BF16), before.astype(F32).astype(BF16), NN)
    rank = jnp.sum(earlier * onehot, 0, keepdims=True)
    experts = experts.astype(F32)
    slot_ref[...] = jnp.broadcast_to(experts * CAP + rank, (8, 512))
    for pb in range(4):
        for i, row in enumerate((experts, rank)):
            wide[pl.ds(16 + i * 4 + pb, 64, stride=24), :] = jnp.broadcast_to(
                row[:, pb * 128 : (pb + 1) * 128], (64, 128)
            )
    for pb in range(4):
        copies[pb].wait()
        mid[...] = landed[pb * 128 : (pb + 1) * 128, :].astype(F32).T
        for ch in range(4):
            chp, chl = ch // 2, ch % 2
            wide[pl.ds(chl * 8 + pb * 2 + chp, 64, stride=24), :] = mid[pl.ds(ch, 64, stride=4), :]
    out_ref[...] = wide[...].astype(BF16)


def filter_kernel(x_ref, spec_ref, factor_ref, turn_ref, out_ref, wide, sums, stage):
    first = factor_ref[0:512], factor_ref[512:1024]
    second = factor_ref[1024:1280], factor_ref[1280:1536]
    fourth = [
        jnp.concatenate([factor_ref[at : at + 256], factor_ref[at + 256 : at + 512]], 1)
        for at in (1536, 2048)
    ]
    wide[...] = x_ref[...].astype(F32)
    sig = jnp.concatenate(
        [
            jnp.concatenate(
                [
                    wide[pl.ds(ch % 2 * 8 + pb * 2 + ch // 2, 64, stride=24), :]
                    for ch in range(4)
                ],
                1,
            )
            for pb in range(4)
        ],
        0,
    )
    sig16 = sig.astype(BF16)
    spec1 = dot(first[0], sig16, NN) + dot(first[1], sig16, NN)
    tcos, tsin = [jnp.concatenate([turn_ref[i], turn_ref[i + 1]], 0) for i in (0, 2)]
    turned = []
    for ch in range(4):
        re = spec1[:256, ch * 128 : (ch + 1) * 128]
        im = spec1[256:, ch * 128 : (ch + 1) * 128]
        turned.append(jnp.concatenate([re * tcos + im * tsin, im * tcos - re * tsin], 1))
    t_hi, t_lo = split(jnp.concatenate(turned, 0))
    spec2 = (
        dot(second[0], t_hi, NT) + dot(second[0], t_lo, NT) + dot(second[1], t_hi, NT)
    )
    prods = []
    for ch in range(4):
        fr = spec_ref[0, :, ch * 256 : (ch + 1) * 256]
        fi = spec_ref[1, :, ch * 256 : (ch + 1) * 256]
        zr = spec2[:128, ch * 256 : (ch + 1) * 256]
        zi = spec2[128:, ch * 256 : (ch + 1) * 256]
        prods.append(jnp.concatenate([zr * fi + zi * fr, zr * fr - zi * fi], 0))
    p_hi, p_lo = split(jnp.concatenate(prods, 1))
    back = dot(second[0], p_hi, NN) + dot(second[0], p_lo, NN) + dot(second[1], p_hi, NN)
    bcos, bsin = [jnp.concatenate([turn_ref[i].T, turn_ref[i + 1].T], 1) for i in (0, 2)]
    turned = []
    for ch in range(4):
        im = back[:128, ch * 256 : (ch + 1) * 256]
        re = back[128:, ch * 256 : (ch + 1) * 256]
        turned.append(jnp.concatenate([re * bcos - im * bsin, im * bcos + re * bsin], 1))
    v_hi, v_lo = split(jnp.concatenate(turned, 0))
    filtered = (
        dot(fourth[0], v_hi, NT) + dot(fourth[0], v_lo, NT) + dot(fourth[1], v_hi, NT)
    )
    summed = sig + filtered * (1.0 / LENGTH)
    for ch in range(4):
        sums[ch] = summed[:, ch * 128 : (ch + 1) * 128]
    low = lax.broadcasted_iota(jnp.int32, (8, 512), 0).astype(F32)

    def spread(ref_rows):
        return jnp.concatenate([jnp.broadcast_to(r, (8, 128)) for r in ref_rows], 1)

    def place(block):
        at = block * 24 + 16
        expert = spread([wide[pl.ds(at + pb, 1), :] for pb in range(4)])
        rank = spread([wide[pl.ds(at + 4 + pb, 1), :] for pb in range(4)])
        to = jnp.concatenate(
            [jnp.where(expert == low + 8.0 * m, 1.0, 0.0) for m in range(8)], 0
        ).astype(BF16)
        here = [rank == low, rank == low + 8.0]
        values = []
        for ch in range(4):
            vals = spread([sums[ch, pl.ds(pb * 64 + block, 1), :] for pb in range(4)])
            values += [jnp.where(m, vals, 0.0) for m in here]
        return dot(to, jnp.concatenate(values, 0).astype(BF16), NT)

    def group(hi, carry):
        for q in range(4):
            pair = [place(hi * 8 + q * 2 + half) for half in range(2)]
            stage[q, pl.ds(hi, 64, stride=8), :] = jnp.concatenate(pair, 1)
        return carry

    lax.fori_loop(0, 8, group, 0)
    for q in range(4):
        out_ref[:, q * 128 : (q + 1) * 128] = stage[q].astype(BF16)


def ready_kernel(
    after_ref, spec_ref, factor_ref, turn_ref, spec_out, factor_out, turn_out, raw, sems
):
    copies = [
        pltpu.make_async_copy(src, dst, sems.at[i])
        for i, (src, dst) in enumerate(
            ((spec_ref, raw), (factor_ref, factor_out), (turn_ref, turn_out))
        )
    ]
    for copy in copies:
        copy.start()
    copies[0].wait()
    for part in range(2):
        for ch in range(4):
            for half in range(2):
                at = ch * 256 + half * 128
                spec_out[part, :, at : at + 128] = raw[part, pl.ds(4 * half + ch, 128, stride=8), :]
    copies[1].wait()
    copies[2].wait()


def expert_kernel(
    x_ref, lanes_ref, gain_ref, gate_ref, own_ref, one_ref, two_ref, three_ref,
    out_ref, turned, slots, full,
):
    moved = dot(x_ref[...], lanes_ref[...], NN)
    for ch in range(4):
        turned[ch] = moved[:, ch * 128 : (ch + 1) * 128]
    normed = []
    for hi in range(8):
        for ch in range(4):
            slots[pl.ds(ch, 64, stride=4), :] = turned[ch, pl.ds(hi, 64, stride=8), :]
        vals = slots[...]
        centre = jnp.sum(vals, 0, keepdims=True) * (1.0 / 256)
        off = vals - centre
        spread = jnp.sum(off * off, 0, keepdims=True) * (1.0 / 256)
        normed.append((off * lax.rsqrt(spread + 1e-05) * gain_ref[...]).T.astype(BF16))
    normed = jnp.concatenate(normed, 0)
    total = None
    for part in (own_ref, one_ref, two_ref, three_ref):
        hidden = jnp.maximum(dot(normed, part[0], NT), 0.0).astype(BF16)
        term = dot(hidden, part[1], NN)
        total = term if total is None else total + term
    full[:, 0:16, :] = total[:, :128].reshape(64, 16, 128)
    full[:, 16:32, :] = total[:, 128:].reshape(64, 16, 128)
    scores = dot(normed, gate_ref[...], NT).reshape(64, 2, 8, 256)
    full[:, 32:40, :] = scores[:, 0, :, :128] + scores[:, 1, :, 128:]
    out_ref[...] = full[...].astype(BF16)


def take_kernel(after_ref, index_ref, table_ref, slot_ref, take_ref, bias_ref):
    slot = slot_ref[0:1, :]
    slot_col = jnp.broadcast_to(slot, (128, 512)).T[:, 0:1].astype(jnp.int32)
    take_ref[...] = (
        lax.broadcasted_iota(jnp.int32, (512, EXPERTS * CAP), 1) == slot_col
    ).astype(F32).astype(BF16)
    rows = []
    for t in range(TASKS):
        idx = index_ref[t : t + 1, :]
        bias = jnp.zeros((1, 512), F32)
        for r in range(table_ref.shape[1]):
            bias = jnp.where(idx == r, table_ref[t, r], bias)
        rows.append(bias)
    rank = slot - CAP * jnp.floor(slot * (1.0 / CAP))
    rows.append(jnp.where(rank >= CAP // 2, 1.0, 0.0))
    rows.append(jnp.zeros((128 - TASKS - 1, 512), F32))
    bias_ref[...] = jnp.concatenate(rows, 0).T


def final_kernel(slots_ref, take_ref, bias_ref, out_ref):
    low = slots_ref[:, 0:16, :].reshape(1024, 128)
    high = slots_ref[:, 16:32, :].reshape(1024, 128)
    score = slots_ref[...].astype(F32)[:, 32:40, :]
    score = jnp.concatenate([score, score], 1).reshape(1024, 128).astype(BF16)
    rows = dot(take_ref[...], jnp.concatenate([low, high, score], 1), NN)
    bias = bias_ref[...]
    both = rows[:, 256:384]
    chosen = jnp.where(
        bias[:, 3:4] > 0.5, jnp.concatenate([both[:, 64:], both[:, :64]], 1), both
    )
    gates = jax.nn.sigmoid(chosen + bias)
    for t in range(TASKS):
        out_ref[t] = (gates[:, t : t + 1] * rows[:, :256]).astype(BF16)


def call(kernel, outs, *args, scratch=(), smem=(), far=(), flops=0, vmem=32, name=None):
    specs = [
        pl.BlockSpec(memory_space=pltpu.SMEM if i in smem else pl.ANY if i in far else pltpu.VMEM)
        for i in range(len(args))
    ]
    many = isinstance(outs, (tuple, list))
    return pl.pallas_call(
        kernel,
        out_shape=outs,
        in_specs=specs,
        out_specs=[pl.BlockSpec(memory_space=pltpu.VMEM)] * len(outs)
        if many
        else pl.BlockSpec(memory_space=pltpu.VMEM),
        scratch_shapes=list(scratch),
        compiler_params=pltpu.CompilerParams(vmem_limit_bytes=vmem * 2**20),
        cost_estimate=pl.CostEstimate(flops=flops, bytes_accessed=2**20, transcendentals=0),
        name=name,
    )(*args)


def shape(dims, dtype):
    return jax.ShapeDtypeStruct(dims, dtype)


def swap(values, rows):
    lanes = values.shape[-1]
    chunks = values.reshape(64, rows, lanes)
    return lax.all_to_all(chunks, "seq", split_axis=0, concat_axis=0, tiled=True).reshape(
        64 * rows, lanes
    )


def on_device(
    events, spectral_filter, ln_gain, w_in, w_out, gate_weight, gate_table, routes, gate_index
):
    big = pltpu.VMEM
    chunks, slot = call(
        prep_kernel, [shape((1536, 128), BF16), shape((8, 512), F32)],
        events.reshape(512, 256), routes.reshape(1, 512), far=(0, 1), name="prep", vmem=60,
        scratch=[
            big((512, 256), BF16), big((1, 512), jnp.int32), big((256, 128), F32),
            big((1536, 128), F32), pltpu.SemaphoreType.DMA((5,)),
        ],
    )
    arrived = swap(chunks, 24)
    own = jnp.stack([w_in[0], w_out[0]])
    weights = [own] + [
        lax.ppermute(own, "batch", [(i, (i + d) % 4) for i in range(4)]) for d in (1, 3, 2)
    ]
    spec = spectral_filter.reshape(2, 256, 128, 4).transpose(0, 1, 3, 2).reshape(2, 1024, 128)
    factors, turns, lanes = [jnp.asarray(t) for t in tables()]
    spec, factors, turns = call(
        ready_kernel,
        [shape((2, 128, 1024), F32), shape(factors.shape, BF16), shape(turns.shape, F32)],
        chunks, spec, factors, turns, far=(0, 1, 2, 3), name="ready",
        scratch=[big((2, 1024, 128), F32), pltpu.SemaphoreType.DMA((3,))], flops=2 * 10**9,
    )
    sums = call(
        filter_kernel, shape((512, 512), BF16), arrived, spec, factors, turns,
        scratch=[big((1536, 128), F32), big((4, 256, 128), F32), big((4, 512, 128), F32)],
        name="filter", flops=2 * 10**9,
    )
    slots_in = swap(sums, 8)
    me = lax.axis_index("seq")
    gate = lax.dynamic_index_in_dim(gate_weight.transpose(0, 2, 1), me, 1, keepdims=False)
    gate = jnp.zeros((256, 256), BF16).at[0:TASKS].set(gate).at[192 : 192 + TASKS].set(gate)
    slots_out = call(
        expert_kernel, shape((64, 40, 128), BF16),
        slots_in, lanes, ln_gain.reshape(256, 1), gate, *weights, name="expert", flops=10**9,
        scratch=[big((4, 512, 128), F32), big((256, 128), F32), big((64, 40, 128), F32)],
    )
    results = lax.all_to_all(slots_out, "seq", split_axis=0, concat_axis=0, tiled=True)
    take, bias = call(
        take_kernel, [shape((512, 1024), BF16), shape((512, 128), F32)], slots_out,
        gate_index.reshape(512, 3).T, gate_table, slot, far=(0,), smem=(2,), name="take",
        flops=2 * 10**9,
    )
    out = call(final_kernel, shape((3, 512, 256), BF16), results, take, bias, name="final")
    return out.reshape(TASKS, 1, 512, 1, 256)


def solution(mesh):
    in_specs = (
        P("batch", "seq", None, None),
        P(None, None, "seq"),
        P(),
        P("seq", "batch", None),
        P("seq", "batch", None),
        P(),
        P(),
        P("batch", "seq", None, None),
        P("batch", "seq", None, None),
    )
    out_specs = P(None, "batch", "seq", None, None)
    return jax.shard_map(
        on_device, mesh=mesh, in_specs=in_specs, out_specs=out_specs, check_vma=False
    )
```

time: 106 us -> 95.5 us (0.901)
  starting transfers between devices: 40.2 us -> 33.5 us
  waiting for transfers between devices: 46.9 us -> 41.3 us
  Pallas kernels: 12.2 us -> 15.1 us
  local copies, waits for them, and re-layouts: 5.96 us -> 4.86 us
    all_to_all x4 -> x2, waiting for transfers between devices: 35.8 us -> 11.4 us  [swap(): lax.all_to_all(chunks, 'seq', split_axis=0, concat_axis=0, tiled=True)]
    all_to_all x0 -> x1, waiting for transfers between devices: none -> 19.1 us  [on_device(): lax.all_to_all(slots_out, 'seq', split_axis=0, concat_axis=0, tiled=True)]
    all_to_all x4 -> x2, starting transfers between devices: 35.8 us -> 19.3 us  [swap(): lax.all_to_all(chunks, 'seq', split_axis=0, concat_axis=0, tiled=True)]
    all_to_all x0 -> x1, starting transfers between devices: none -> 9.7 us  [on_device(): lax.all_to_all(slots_out, 'seq', split_axis=0, concat_axis=0, tiled=True)]
    pallas_call x8 -> x6, Pallas kernels: 12.2 us -> 15.1 us  [call(): pl.pallas_call(kernel, out_shape=outs, in_specs=specs, out_specs=[pl.Bloc...]
    unnamed x24 -> x27, local copies, waits for them, and re-layouts: 5.82 us -> 4.56 us
  transfers between devices with their start and end apart: 7 -> 6, of which waited for: 6 -> 5; matrix products, arithmetic and copies ran while one was open for 0% -> 0% of each run, Pallas kernels for 2% -> 1%
where the time goes in v3:
time: 95.5 us; the launch traced here: 94.9 us
  waiting for transfers between devices  41.3 us (43%)
  starting transfers between devices  33.5 us (35%)
  Pallas kernels  15.1 us (16%)
  local copies, waits for them, and re-layouts  4.86 us (5%)
    all_to_all x2, starting transfers between devices, swap(): lax.all_to_all(chunks, 'seq', split_axis=0, concat_axis=0, tiled=True)  19.3 us
    all_to_all x1, waiting for transfers between devices, on_device(): lax.all_to_all(slots_out, 'seq', split_axis=0, concat_axis=0, tiled=True)  19.1 us
    pallas_call x6, Pallas kernels, call(): pl.pallas_call(kernel, out_shape=outs, in_specs=specs, out_specs=[pl.Bloc...  15.1 us
    all_to_all x2, waiting for transfers between devices, swap(): lax.all_to_all(chunks, 'seq', split_axis=0, concat_axis=0, tiled=True)  11.4 us
    ppermute x3, waiting for transfers between devices, on_device(): lax.ppermute(own, 'batch', [(i, (i + d) % 4) for i in range(4)])  10.8 us
    all_to_all x1, starting transfers between devices, on_device(): lax.all_to_all(slots_out, 'seq', split_axis=0, concat_axis=0, tiled=True)  9.7 us
    unnamed x27, local copies, waits for them, and re-layouts  4.56 us
    ppermute x3, starting transfers between devices, on_device(): lax.ppermute(own, 'batch', [(i, (i + d) % 4) for i in range(4)])  4.45 us
  transfers between devices with their start and end apart: 6, of which 5 were waited for; matrix products, arithmetic and copies ran while one was open for 0% of the time, Pallas kernels for 1%

profile of v3, /device:TPU:1, one launch (start us, length us, event | category | flops | bytes accessed | tf_op | source)
XLA Modules:
  0.0 94.9 jit_solution(16284616037779192690)
XLA Ops:
  0.0 2.3 %prep.1 = (bf16[1536,128]{1,0:T(8,128)(2,1)}, f32[8,512]{1,0:T(8,128)}) custom-call(bf16[512,256]{1,0:T(8,128)(2,1)} %bitcast.28, s32[1,512]{1,0:T(1,128)} %bitcast.31), custom_call_target="tpu_custom_call" | custom-call | bytes 1048576 | tf_op jit(solution)/shard_map/prep/pallas_call | solution.py:270
  2.3 13.0 %all-to-all-start = ((bf16[64,24,128]{2,1,0:T(8,128)(2,1)}), bf16[64,24,128]{2,1,0:T(8,128)(2,1)S(1)}, u32[]{:S(2)}, u32[]{:S(2)}) async-start(bf16[64,24,128]{2,1,0:T(8,128)(2,1)} %bitcast.25), calls=%async_computation | async-start | bytes 786432 | tf_op jit(solution)/shard_map/all_to_all | solution.py:291
  15.3 0.0 copy-start.1
  15.4 1.0 %copy-done.1 = bf16[1536,128]{1,0:T(8,128)(2,1)S(1)} copy-done((bf16[1536,128]{1,0:T(8,128)(2,1)S(1)}, bf16[1536,128]{1,0:T(8,128)(2,1)}, u32[]{:S(2)}) %copy-start.1) | copy-done | bytes 393240
  16.4 1.2 %copy-done.2 = f32[2,32768,4]{1,2,0:T(4,128)S(1)} copy-done((f32[2,32768,4]{1,2,0:T(4,128)S(1)}, f32[2,32768,4]{1,2,0:T(4,128)}, u32[]{:S(2)}) %copy-start.2) | copy-done | bytes 1048600
  17.6 1.3 %copy-done.5 = bf16[2560,256]{1,0:T(8,128)(2,1)S(1)} copy-done((bf16[2560,256]{1,0:T(8,128)(2,1)S(1)}, bf16[2560,256]{1,0:T(8,128)(2,1)}, u32[]{:S(2)}) %copy-start.5) | copy-done | bytes 1310744
  18.9 0.9 copy-done.7
  19.9 0.4 ready.1
  20.3 9.7 %all-to-all-done = bf16[64,24,128]{2,1,0:T(8,128)(2,1)S(1)} async-done(((bf16[64,24,128]{2,1,0:T(8,128)(2,1)}), bf16[64,24,128]{2,1,0:T(8,128)(2,1)S(1)}, u32[]{:S(2)}, u32[]{:S(2)}) %all-to-all-start) | async-done | bytes 393248 | tf_op jit(solution)/shard_map/all_to_all | solution.py:291
  30.0 6.2 %filter.1 = bf16[512,512]{1,0:T(8,128)(2,1)} custom-call(bf16[1536,128]{1,0:T(8,128)(2,1)S(1)} %bitcast.24, f32[2,128,1024]{2,1,0:T(8,128)S(1)} %get-tuple-element.37.spec_ref, bf16[2560,256]{1,0:T(8,128)(2,1)S(1)} %get-tuple-element.38.factor_ref, f32[4,128,128]{2,1,0:T(8,128)S(1)} %get-tuple-element.39.turn_ref), custom_call_target="tpu_custom_call" | custom-call | flops 2000000000 | bytes 1048576 | tf_op jit(solution)/shard_map/filter/pallas_call | solution.py:270
  36.1 6.3 %all-to-all-start.1 = ((bf16[64,8,512]{2,1,0:T(8,128)(2,1)}), bf16[64,8,512]{2,1,0:T(8,128)(2,1)S(1)}, u32[]{:S(2)}, u32[]{:S(2)}) async-start(bf16[64,8,512]{2,1,0:T(8,128)(2,1)} %bitcast.7), calls=%async_computation.1 | async-start | bytes 1048576 | tf_op jit(solution)/shard_map/all_to_all | solution.py:291
  42.5 1.4 %collective-permute-start = (bf16[2,256,256]{2,1,0:T(8,128)(2,1)S(1)}, bf16[2,256,256]{2,1,0:T(8,128)(2,1)S(1)}, u32[]{:S(2)}, u32[]{:S(2)}) collective-permute-start(bf16[2,256,256]{2,1,0:T(8,128)(2,1)S(1)} %constant_dynamic-update-slice_fusion.own_ref), channel_id=1, source_target_pairs={{0,1},{1,2},{2,3},{3,0},{4,5},{5,6},{6,7},{7,4},{8,9},{9,10},{10,1... | collective-permute-start | bytes 786440 | tf_op jit(solution)/shard_map/ppermute | solution.py:311
  43.9 1.5 %collective-permute-start.1 = (bf16[2,256,256]{2,1,0:T(8,128)(2,1)S(1)}, bf16[2,256,256]{2,1,0:T(8,128)(2,1)S(1)}, u32[]{:S(2)}, u32[]{:S(2)}) collective-permute-start(bf16[2,256,256]{2,1,0:T(8,128)(2,1)S(1)} %constant_dynamic-update-slice_fusion.own_ref), channel_id=1, source_target_pairs={{0,3},{1,0},{2,1},{3,2},{4,7},{5,4},{6,5},{7,6},{8,11},{9,8},{10,9... | collective-permute-start | bytes 786440 | tf_op jit(solution)/shard_map/ppermute | solution.py:311
  45.4 1.6 %collective-permute-start.2 = (bf16[2,256,256]{2,1,0:T(8,128)(2,1)S(1)}, bf16[2,256,256]{2,1,0:T(8,128)(2,1)S(1)}, u32[]{:S(2)}, u32[]{:S(2)}) collective-permute-start(bf16[2,256,256]{2,1,0:T(8,128)(2,1)S(1)} %constant_dynamic-update-slice_fusion.own_ref), channel_id=1, source_target_pairs={{0,2},{1,3},{2,0},{3,1},{4,6},{5,7},{6,4},{7,5},{8,10},{9,11},{10,... | collective-permute-start | bytes 786440 | tf_op jit(solution)/shard_map/ppermute | solution.py:311
  47.0 0.1 copy.16.gain_ref
  47.2 0.1 scatter.9.gate_ref
  47.3 4.0 %collective-permute-done.one_ref = bf16[2,256,256]{2,1,0:T(8,128)(2,1)S(1)} collective-permute-done((bf16[2,256,256]{2,1,0:T(8,128)(2,1)S(1)}, bf16[2,256,256]{2,1,0:T(8,128)(2,1)S(1)}, u32[]{:S(2)}, u32[]{:S(2)}) %collective-permute-start) | collective-permute-done | bytes 262176 | tf_op jit(solution)/shard_map/ppermute | solution.py:311
  51.4 6.7 %collective-permute-done.2.three_ref = bf16[2,256,256]{2,1,0:T(8,128)(2,1)S(1)} collective-permute-done((bf16[2,256,256]{2,1,0:T(8,128)(2,1)S(1)}, bf16[2,256,256]{2,1,0:T(8,128)(2,1)S(1)}, u32[]{:S(2)}, u32[]{:S(2)}) %collective-permute-start.2) | collective-permute-done | bytes 262176 | tf_op jit(solution)/shard_map/ppermute | solution.py:311
  58.1 1.7 %all-to-all-done.1 = bf16[64,8,512]{2,1,0:T(8,128)(2,1)S(1)} async-done(((bf16[64,8,512]{2,1,0:T(8,128)(2,1)}), bf16[64,8,512]{2,1,0:T(8,128)(2,1)S(1)}, u32[]{:S(2)}, u32[]{:S(2)}) %all-to-all-start.1) | async-done | bytes 524320 | tf_op jit(solution)/shard_map/all_to_all | solution.py:291
  59.8 3.4 %expert.1.after_ref = bf16[64,40,128]{2,1,0:T(8,128)(2,1)} custom-call(bf16[512,512]{1,0:T(8,128)(2,1)S(1)} %bitcast.23, bf16[512,512]{1,0:T(8,128)(2,1)S(1)} %copy-done.6, f32[256,1]{1,0:T(8,128)S(1)} %copy.16.gain_ref, bf16[256,256]{1,0:T(8,128)(2,1)S(1)} %scatter.9.gate_ref, bf16[2,256,256]{2,1,0:T(8,128)(2,1)S(1)} %constant_dynamic-update-slice_fusion.own_ref, ...), custom_call_target="tpu_custom_call" | custom-call | flops 1000000000 | bytes 1048576 | tf_op jit(solution)/shard_map/expert/pallas_call | solution.py:270
  63.2 9.7 %all-to-all-start.2 = ((bf16[64,40,128]{2,1,0:T(8,128)(2,1)}), bf16[64,40,128]{2,1,0:T(8,128)(2,1)S(1)}, u32[]{:S(2)}, u32[]{:S(2)}) async-start(bf16[64,40,128]{2,1,0:T(8,128)(2,1)} %expert.1.after_ref), calls=%async_computation.2 | async-start | bytes 1310720 | tf_op jit(solution)/shard_map/all_to_all | solution.py:335
  72.9 1.0 %take.1 = (bf16[512,1024]{1,0:T(8,128)(2,1)S(1)}, f32[512,128]{1,0:T(8,128)S(1)}) custom-call(bf16[64,40,128]{2,1,0:T(8,128)(2,1)} %expert.1.after_ref, s32[3,512]{1,0:T(4,128)S(1)} %bitcast.26, f32[3,16]{1,0:T(4,128)S(1)} %copy-done.4, f32[8,512]{1,0:T(8,128)S(1)} %copy-done.3), custom_call_target="tpu_custom_call" | custom-call | flops 2000000000 | bytes 1048576 | tf_op jit(solution)/shard_map/take/pallas_call | solution.py:270
  73.9 19.1 %all-to-all-done.2.slots_ref = bf16[64,40,128]{2,1,0:T(8,128)(2,1)S(1)} async-done(((bf16[64,40,128]{2,1,0:T(8,128)(2,1)}), bf16[64,40,128]{2,1,0:T(8,128)(2,1)S(1)}, u32[]{:S(2)}, u32[]{:S(2)}) %all-to-all-start.2) | async-done | bytes 655392 | tf_op jit(solution)/shard_map/all_to_all | solution.py:335
  93.0 1.9 %final.1 = bf16[3,512,256]{2,1,0:T(8,128)(2,1)} custom-call(bf16[64,40,128]{2,1,0:T(8,128)(2,1)S(1)} %all-to-all-done.2.slots_ref, bf16[512,1024]{1,0:T(8,128)(2,1)S(1)} %get-tuple-element.41.take_ref, f32[512,128]{1,0:T(8,128)S(1)} %get-tuple-element.42.bias_ref), custom_call_target="tpu_custom_call" | custom-call | bytes 1048576 | tf_op jit(solution)/shard_map/final/pallas_call | solution.py:270
  (26 shorter events, 0.1 us)
Async XLA Ops:
  0.0 47.0 %copy-start = (bf16[3,256,64]{1,2,0:T(8,128)(2,1)S(1)}, bf16[3,256,64]{1,2,0:T(8,128)(2,1)}, u32[]{:S(2)}) copy-start(bf16[3,256,64]{1,2,0:T(8,128)(2,1)} %param.21) | copy-start | bytes 294916
  2.3 27.6 %all-to-all-start = ((bf16[64,24,128]{2,1,0:T(8,128)(2,1)}), bf16[64,24,128]{2,1,0:T(8,128)(2,1)S(1)}, u32[]{:S(2)}, u32[]{:S(2)}) async-start(bf16[64,24,128]{2,1,0:T(8,128)(2,1)} %bitcast.25), calls=%async_computation | async-start | bytes 786432 | tf_op jit(solution)/shard_map/all_to_all | solution.py:291
  15.3 1.0 %copy-start.1 = (bf16[1536,128]{1,0:T(8,128)(2,1)S(1)}, bf16[1536,128]{1,0:T(8,128)(2,1)}, u32[]{:S(2)}) copy-start(bf16[1536,128]{1,0:T(8,128)(2,1)} %get-tuple-element.36.after_ref) | copy-start | bytes 1179652
  16.4 1.2 %copy-start.2 = (f32[2,32768,4]{1,2,0:T(4,128)S(1)}, f32[2,32768,4]{1,2,0:T(4,128)}, u32[]{:S(2)}) copy-start(f32[2,32768,4]{1,2,0:T(4,128)} %param.17) | copy-start | bytes 3145732
  17.6 1.3 %copy-start.5 = (bf16[2560,256]{1,0:T(8,128)(2,1)S(1)}, bf16[2560,256]{1,0:T(8,128)(2,1)}, u32[]{:S(2)}) copy-start(bf16[2560,256]{1,0:T(8,128)(2,1)} %constant.74.clone.factor_ref) | copy-start | bytes 3932164
  18.9 0.9 %copy-start.7 = (f32[4,128,128]{2,1,0:T(8,128)S(1)}, f32[4,128,128]{2,1,0:T(8,128)}, u32[]{:S(2)}) copy-start(f32[4,128,128]{2,1,0:T(8,128)} %constant.75.clone.turn_ref) | copy-start | bytes 786436
  29.9 12.5 %copy-start.8 = (bf16[1,256,256]{2,1,0:T(8,128)(2,1)S(1)}, bf16[1,256,256]{2,1,0:T(8,128)(2,1)}, u32[]{:S(2)}) copy-start(bf16[1,256,256]{2,1,0:T(8,128)(2,1)} %param.19) | copy-start | bytes 393220
  36.1 6.4 %copy-start.9 = (bf16[1,256,256]{2,1,0:T(8,128)(2,1)S(1)}, bf16[1,256,256]{2,1,0:T(8,128)(2,1)}, u32[]{:S(2)}) copy-start(bf16[1,256,256]{2,1,0:T(8,128)(2,1)} %param.20) | copy-start | bytes 393220
  36.1 10.9 %copy-start.11 = (f32[256]{0:T(256)S(1)}, f32[256]{0:T(256)}, u32[]{:S(2)}) copy-start(f32[256]{0:T(256)} %param.18) | copy-start | bytes 3076
  36.1 23.7 %copy-start.6 = (bf16[512,512]{1,0:T(8,128)(2,1)S(1)}, bf16[512,512]{1,0:T(8,128)(2,1)}, u32[]{:S(2)}) copy-start(bf16[512,512]{1,0:T(8,128)(2,1)} %constant.76.clone.lanes_ref) | copy-start | bytes 1572868
  36.1 23.7 %all-to-all-start.1 = ((bf16[64,8,512]{2,1,0:T(8,128)(2,1)}), bf16[64,8,512]{2,1,0:T(8,128)(2,1)S(1)}, u32[]{:S(2)}, u32[]{:S(2)}) async-start(bf16[64,8,512]{2,1,0:T(8,128)(2,1)} %bitcast.7), calls=%async_computation.1 | async-start | bytes 1048576 | tf_op jit(solution)/shard_map/all_to_all | solution.py:291
  42.5 8.8 %collective-permute-start = (bf16[2,256,256]{2,1,0:T(8,128)(2,1)S(1)}, bf16[2,256,256]{2,1,0:T(8,128)(2,1)S(1)}, u32[]{:S(2)}, u32[]{:S(2)}) collective-permute-start(bf16[2,256,256]{2,1,0:T(8,128)(2,1)S(1)} %constant_dynamic-update-slice_fusion.own_ref), channel_id=1, source_target_pairs={{0,1},{1,2},{2,3},{3,0},{4,5},{5,6},{6,7},{7,4},{8,9},{9,10},{10,1... | collective-permute-start | bytes 786440 | tf_op jit(solution)/shard_map/ppermute | solution.py:311
  43.9 7.5 %collective-permute-start.1 = (bf16[2,256,256]{2,1,0:T(8,128)(2,1)S(1)}, bf16[2,256,256]{2,1,0:T(8,128)(2,1)S(1)}, u32[]{:S(2)}, u32[]{:S(2)}) collective-permute-start(bf16[2,256,256]{2,1,0:T(8,128)(2,1)S(1)} %constant_dynamic-update-slice_fusion.own_ref), channel_id=1, source_target_pairs={{0,3},{1,0},{2,1},{3,2},{4,7},{5,4},{6,5},{7,6},{8,11},{9,8},{10,9... | collective-permute-start | bytes 786440 | tf_op jit(solution)/shard_map/ppermute | solution.py:311
  45.4 12.7 %collective-permute-start.2 = (bf16[2,256,256]{2,1,0:T(8,128)(2,1)S(1)}, bf16[2,256,256]{2,1,0:T(8,128)(2,1)S(1)}, u32[]{:S(2)}, u32[]{:S(2)}) collective-permute-start(bf16[2,256,256]{2,1,0:T(8,128)(2,1)S(1)} %constant_dynamic-update-slice_fusion.own_ref), channel_id=1, source_target_pairs={{0,2},{1,3},{2,0},{3,1},{4,6},{5,7},{6,4},{7,5},{8,10},{9,11},{10,... | collective-permute-start | bytes 786440 | tf_op jit(solution)/shard_map/ppermute | solution.py:311
  63.2 9.7 %copy-start.10 = (s32[1,512,1,3]{1,2,3,0:T(1,128)S(1)}, s32[1,512,1,3]{1,2,3,0:T(1,128)}, u32[]{:S(2)}) copy-start(s32[1,512,1,3]{1,2,3,0:T(1,128)} %param.24) | copy-start | bytes 18436
  63.2 9.7 %copy-start.3 = (f32[8,512]{1,0:T(8,128)S(1)}, f32[8,512]{1,0:T(8,128)}, u32[]{:S(2)}) copy-start(f32[8,512]{1,0:T(8,128)} %get-tuple-element.40.slot_ref) | copy-start | bytes 49156
  63.2 9.7 %copy-start.4 = (f32[3,16]{1,0:T(4,128)S(1)}, f32[3,16]{1,0:T(4,128)}, u32[]{:S(2)}) copy-start(f32[3,16]{1,0:T(4,128)} %table_ref.1) | copy-start | bytes 580
  63.2 29.8 %all-to-all-start.2 = ((bf16[64,40,128]{2,1,0:T(8,128)(2,1)}), bf16[64,40,128]{2,1,0:T(8,128)(2,1)S(1)}, u32[]{:S(2)}, u32[]{:S(2)}) async-start(bf16[64,40,128]{2,1,0:T(8,128)(2,1)} %expert.1.after_ref), calls=%async_computation.2 | async-start | bytes 1310720 | tf_op jit(solution)/shard_map/all_to_all | solution.py:335

commit v4 on v3

--- a/solution.py
+++ b/solution.py
@@ -171,7 +171,7 @@
             stage[q, pl.ds(hi, 64, stride=8), :] = jnp.concatenate(pair, 1)
         return carry
 
-    lax.fori_loop(0, 8, group, 0)
+    lax.fori_loop(0, 8, group, 0, unroll=8)
     for q in range(4):
         out_ref[:, q * 128 : (q + 1) * 128] = stage[q].astype(BF16)
 
@@ -198,9 +198,9 @@
 
 
 def expert_kernel(
-    x_ref, lanes_ref, gain_ref, gate_ref, own_ref, one_ref, two_ref, three_ref,
-    out_ref, turned, slots, full,
+    x_ref, lanes_ref, gain_ref, gate_ref, *refs
 ):
+    out_ref, turned, slots, full = refs[8:]
     moved = dot(x_ref[...], lanes_ref[...], NN)
     for ch in range(4):
         turned[ch] = moved[:, ch * 128 : (ch + 1) * 128]
@@ -215,9 +215,9 @@
         normed.append((off * lax.rsqrt(spread + 1e-05) * gain_ref[...]).T.astype(BF16))
     normed = jnp.concatenate(normed, 0)
     total = None
-    for part in (own_ref, one_ref, two_ref, three_ref):
-        hidden = jnp.maximum(dot(normed, part[0], NT), 0.0).astype(BF16)
-        term = dot(hidden, part[1], NN)
+    for part_in, part_out in zip(refs[0:8:2], refs[1:8:2]):
+        hidden = jnp.maximum(dot(normed, part_in[...], NT), 0.0).astype(BF16)
+        term = dot(hidden, part_out[...], NN)
         total = term if total is None else total + term
     full[:, 0:16, :] = total[:, :128].reshape(64, 16, 128)
     full[:, 16:32, :] = total[:, 128:].reshape(64, 16, 128)
@@ -306,10 +306,14 @@
         ],
     )
     arrived = swap(chunks, 24)
-    own = jnp.stack([w_in[0], w_out[0]])
-    weights = [own] + [
-        lax.ppermute(own, "batch", [(i, (i + d) % 4) for i in range(4)]) for d in (1, 3, 2)
-    ]
+    ahead, behind = [(i, (i + 1) % 4) for i in range(4)], [(i, (i + 3) % 4) for i in range(4)]
+    own_in, own_out = w_in[0], w_out[0]
+    one_in = lax.ppermute(own_in, "batch", ahead)
+    two_out = lax.ppermute(own_out, "batch", behind)
+    far_in = lax.ppermute(one_in, "batch", ahead)
+    far_out = lax.ppermute(two_out, "batch", behind)
+    one_out = lax.ppermute(own_out, "batch", ahead)
+    two_in = lax.ppermute(own_in, "batch", behind)
     spec = spectral_filter.reshape(2, 256, 128, 4).transpose(0, 1, 3, 2).reshape(2, 1024, 128)
     factors, turns, lanes = [jnp.asarray(t) for t in tables()]
     spec, factors, turns = call(
@@ -329,7 +333,9 @@
     gate = jnp.zeros((256, 256), BF16).at[0:TASKS].set(gate).at[192 : 192 + TASKS].set(gate)
     slots_out = call(
         expert_kernel, shape((64, 40, 128), BF16),
-        slots_in, lanes, ln_gain.reshape(256, 1), gate, *weights, name="expert", flops=10**9,
+        slots_in, lanes, ln_gain.reshape(256, 1), gate,
+        own_in, own_out, one_in, one_out, two_in, two_out, far_in, far_out,
+        name="expert", flops=10**9,
         scratch=[big((4, 512, 128), F32), big((256, 128), F32), big((64, 40, 128), F32)],
     )
     results = lax.all_to_all(slots_out, "seq", split_axis=0, concat_axis=0, tiled=True)

time: 95.5 us -> 90.6 us (0.949)
  waiting for transfers between devices: 41.3 us -> 37.5 us
  Pallas kernels: 15.1 us -> 13.5 us
    ppermute x3 -> x6, waiting for transfers between devices: 10.8 us -> 2.74 us  [the longest x1 2.28 us: on_device(): far_in = lax.ppermute(one_in, 'batch', ahead)]
    all_to_all x2, waiting for transfers between devices: 11.4 us -> 15.6 us  [swap(): lax.all_to_all(chunks, 'seq', split_axis=0, concat_axis=0, tiled=True)]
    ppermute x3 -> x6, starting transfers between devices: 4.45 us -> 8.26 us  [the longest x1 2.67 us: on_device(): far_out = lax.ppermute(two_out, 'batch', behind)]
    all_to_all x1, starting transfers between devices: 9.7 us -> 6.41 us  [on_device(): lax.all_to_all(slots_out, 'seq', split_axis=0, concat_axis=0, tiled=True)]
    pallas_call x6, Pallas kernels: 15.1 us -> 13.5 us  [call(): pl.pallas_call(kernel, out_shape=outs, in_specs=specs, out_specs=[pl.Bloc...]
    unnamed x27 -> x26, local copies, waits for them, and re-layouts: 4.56 us -> 4.55 us
  transfers between devices with their start and end apart: 6 -> 9, of which waited for: 5 -> 5; matrix products, arithmetic and copies ran while one was open for 0% -> 0% of each run, Pallas kernels for 1% -> 1%
where the time goes in v4:
time: 90.6 us; the launch traced here: 90 us
  waiting for transfers between devices  37.5 us (41%)
  starting transfers between devices  34 us (38%)
  Pallas kernels  13.5 us (15%)
  local copies, waits for them, and re-layouts  4.84 us (5%)
    all_to_all x2, starting transfers between devices, swap(): lax.all_to_all(chunks, 'seq', split_axis=0, concat_axis=0, tiled=True)  19.3 us
    all_to_all x1, waiting for transfers between devices, on_device(): lax.all_to_all(slots_out, 'seq', split_axis=0, concat_axis=0, tiled=True)  19.1 us
    all_to_all x2, waiting for transfers between devices, swap(): lax.all_to_all(chunks, 'seq', split_axis=0, concat_axis=0, tiled=True)  15.6 us
    pallas_call x6, Pallas kernels, call(): pl.pallas_call(kernel, out_shape=outs, in_specs=specs, out_specs=[pl.Bloc...  13.5 us
    all_to_all x1, starting transfers between devices, on_device(): lax.all_to_all(slots_out, 'seq', split_axis=0, concat_axis=0, tiled=True)  6.41 us
    unnamed x26, local copies, waits for them, and re-layouts  4.55 us
    ppermute x1, starting transfers between devices, on_device(): far_out = lax.ppermute(two_out, 'batch', behind)  2.67 us
    ppermute x1, starting transfers between devices, on_device(): two_in = lax.ppermute(own_in, 'batch', behind)  2.67 us
  transfers between devices with their start and end apart: 9, of which 5 were waited for; matrix products, arithmetic and copies ran while one was open for 0% of the time, Pallas kernels for 1%

profile of v4, /device:TPU:1, one launch (start us, length us, event | category | flops | bytes accessed | tf_op | source)
XLA Modules:
  0.0 90.0 jit_solution(14068890455815159013)
XLA Ops:
  0.0 2.3 %prep.1 = (bf16[1536,128]{1,0:T(8,128)(2,1)}, f32[8,512]{1,0:T(8,128)}) custom-call(bf16[512,256]{1,0:T(8,128)(2,1)} %bitcast.36, s32[1,512]{1,0:T(1,128)} %bitcast.39), custom_call_target="tpu_custom_call" | custom-call | bytes 1048576 | tf_op jit(solution)/shard_map/prep/pallas_call | solution.py:270
  2.3 13.0 %all-to-all-start = ((bf16[64,24,128]{2,1,0:T(8,128)(2,1)}), bf16[64,24,128]{2,1,0:T(8,128)(2,1)S(1)}, u32[]{:S(2)}, u32[]{:S(2)}) async-start(bf16[64,24,128]{2,1,0:T(8,128)(2,1)} %bitcast.27), calls=%async_computation | async-start | bytes 786432 | tf_op jit(solution)/shard_map/all_to_all | solution.py:291
  15.4 1.0 %copy-done.1 = bf16[1536,128]{1,0:T(8,128)(2,1)S(1)} copy-done((bf16[1536,128]{1,0:T(8,128)(2,1)S(1)}, bf16[1536,128]{1,0:T(8,128)(2,1)}, u32[]{:S(2)}) %copy-start.1) | copy-done | bytes 393240
  16.4 1.2 %copy-done.2 = f32[2,32768,4]{1,2,0:T(4,128)S(1)} copy-done((f32[2,32768,4]{1,2,0:T(4,128)S(1)}, f32[2,32768,4]{1,2,0:T(4,128)}, u32[]{:S(2)}) %copy-start.2) | copy-done | bytes 1048600
  17.6 1.3 %copy-done.7 = bf16[2560,256]{1,0:T(8,128)(2,1)S(1)} copy-done((bf16[2560,256]{1,0:T(8,128)(2,1)S(1)}, bf16[2560,256]{1,0:T(8,128)(2,1)}, u32[]{:S(2)}) %copy-start.7) | copy-done | bytes 1310744
  18.9 0.9 %copy-done.9 = f32[4,128,128]{2,1,0:T(8,128)S(1)} copy-done((f32[4,128,128]{2,1,0:T(8,128)S(1)}, f32[4,128,128]{2,1,0:T(8,128)}, u32[]{:S(2)}) %copy-start.9) | copy-done | bytes 262168
  19.9 0.4 ready.1
  20.3 9.7 %all-to-all-done = bf16[64,24,128]{2,1,0:T(8,128)(2,1)S(1)} async-done(((bf16[64,24,128]{2,1,0:T(8,128)(2,1)}), bf16[64,24,128]{2,1,0:T(8,128)(2,1)S(1)}, u32[]{:S(2)}, u32[]{:S(2)}) %all-to-all-start) | async-done | bytes 393248 | tf_op jit(solution)/shard_map/all_to_all | solution.py:291
  30.0 4.6 %filter.1 = bf16[512,512]{1,0:T(8,128)(2,1)} custom-call(bf16[1536,128]{1,0:T(8,128)(2,1)S(1)} %bitcast.26, f32[2,128,1024]{2,1,0:T(8,128)S(1)} %get-tuple-element.37.spec_ref, bf16[2560,256]{1,0:T(8,128)(2,1)S(1)} %get-tuple-element.38.factor_ref, f32[4,128,128]{2,1,0:T(8,128)S(1)} %get-tuple-element.39.turn_ref), custom_call_target="tpu_custom_call" | custom-call | flops 2000000000 | bytes 1048576 | tf_op jit(solution)/shard_map/filter/pallas_call | solution.py:270
  34.5 6.3 %all-to-all-start.1 = ((bf16[64,8,512]{2,1,0:T(8,128)(2,1)}), bf16[64,8,512]{2,1,0:T(8,128)(2,1)S(1)}, u32[]{:S(2)}, u32[]{:S(2)}) async-start(bf16[64,8,512]{2,1,0:T(8,128)(2,1)} %bitcast.7), calls=%async_computation.1 | async-start | bytes 1048576 | tf_op jit(solution)/shard_map/all_to_all | solution.py:291
  40.9 1.4 %collective-permute-start = (bf16[256,256]{1,0:T(8,128)(2,1)S(1)}, bf16[256,256]{1,0:T(8,128)(2,1)S(1)}, u32[]{:S(2)}, u32[]{:S(2)}) collective-permute-start(bf16[256,256]{1,0:T(8,128)(2,1)S(1)} %bitcast.30), channel_id=1, source_target_pairs={{0,1},{1,2},{2,3},{3,0},{4,5},{5,6},{6,7},{7,4},{8,9},{9,10},{10,1... | collective-permute-start | bytes 393224 | tf_op jit(solution)/shard_map/ppermute | solution.py:311
  42.3 1.5 %collective-permute-start.3 = (bf16[256,256]{1,0:T(8,128)(2,1)S(1)}, bf16[256,256]{1,0:T(8,128)(2,1)S(1)}, u32[]{:S(2)}, u32[]{:S(2)}) collective-permute-start(bf16[256,256]{1,0:T(8,128)(2,1)S(1)} %bitcast.33), channel_id=1, source_target_pairs={{0,3},{1,0},{2,1},{3,2},{4,7},{5,4},{6,5},{7,6},{8,11},{9,8},{10,9... | collective-permute-start | bytes 393224 | tf_op jit(solution)/shard_map/ppermute | solution.py:312
  43.8 2.7 %collective-permute-start.2 = (bf16[256,256]{1,0:T(8,128)(2,1)S(1)}, bf16[256,256]{1,0:T(8,128)(2,1)S(1)}, u32[]{:S(2)}, u32[]{:S(2)}) collective-permute-start(bf16[256,256]{1,0:T(8,128)(2,1)S(1)} %bitcast.31), channel_id=1, source_target_pairs={{0,3},{1,0},{2,1},{3,2},{4,7},{5,4},{6,5},{7,6},{8,11},{9,8},{10,9... | collective-permute-start | bytes 393224 | tf_op jit(solution)/shard_map/ppermute | solution.py:316
  46.5 0.4 collective-permute-done.refs_2_
  46.9 2.7 %collective-permute-start.5 = (bf16[256,256]{1,0:T(8,128)(2,1)S(1)}, bf16[256,256]{1,0:T(8,128)(2,1)S(1)}, u32[]{:S(2)}, u32[]{:S(2)}) collective-permute-start(bf16[256,256]{1,0:T(8,128)(2,1)S(1)} %collective-permute-done.3.refs_5_), channel_id=1, source_target_pairs={{0,3},{1,0},{2,1},{3,2},{4,7},{5,4},{6,5},{7,6},{8,11},{9,8},{10,9... | collective-permute-start | bytes 393224 | tf_op jit(solution)/shard_map/ppermute | solution.py:314
  49.6 0.1 copy.16.gain_ref
  49.8 0.1 scatter.9.gate_ref
  50.0 2.3 %collective-permute-done.4.refs_6_ = bf16[256,256]{1,0:T(8,128)(2,1)S(1)} collective-permute-done((bf16[256,256]{1,0:T(8,128)(2,1)S(1)}, bf16[256,256]{1,0:T(8,128)(2,1)S(1)}, u32[]{:S(2)}, u32[]{:S(2)}) %collective-permute-start.4) | collective-permute-done | bytes 131104 | tf_op jit(solution)/shard_map/ppermute | solution.py:313
  52.2 6.0 %all-to-all-done.1 = bf16[64,8,512]{2,1,0:T(8,128)(2,1)S(1)} async-done(((bf16[64,8,512]{2,1,0:T(8,128)(2,1)}), bf16[64,8,512]{2,1,0:T(8,128)(2,1)S(1)}, u32[]{:S(2)}, u32[]{:S(2)}) %all-to-all-start.1) | async-done | bytes 524320 | tf_op jit(solution)/shard_map/all_to_all | solution.py:291
  58.2 3.4 %expert.1.after_ref = bf16[64,40,128]{2,1,0:T(8,128)(2,1)} custom-call(bf16[512,512]{1,0:T(8,128)(2,1)S(1)} %bitcast.25, bf16[512,512]{1,0:T(8,128)(2,1)S(1)} %copy-done.8, f32[256,1]{1,0:T(8,128)S(1)} %copy.16.gain_ref, bf16[256,256]{1,0:T(8,128)(2,1)S(1)} %scatter.9.gate_ref, bf16[256,256]{1,0:T(8,128)(2,1)S(1)} %bitcast.32, ...), custom_call_target="tpu_custom_call" | custom-call | flops 1000000000 | bytes 1048576 | tf_op jit(solution)/shard_map/expert/pallas_call | solution.py:270
  61.6 6.4 %all-to-all-start.2 = ((bf16[64,40,128]{2,1,0:T(8,128)(2,1)}), bf16[64,40,128]{2,1,0:T(8,128)(2,1)S(1)}, u32[]{:S(2)}, u32[]{:S(2)}) async-start(bf16[64,40,128]{2,1,0:T(8,128)(2,1)} %expert.1.after_ref), calls=%async_computation.2 | async-start | bytes 1310720 | tf_op jit(solution)/shard_map/all_to_all | solution.py:341
  68.0 1.0 %take.1 = (bf16[512,1024]{1,0:T(8,128)(2,1)S(1)}, f32[512,128]{1,0:T(8,128)S(1)}) custom-call(bf16[64,40,128]{2,1,0:T(8,128)(2,1)} %expert.1.after_ref, s32[3,512]{1,0:T(4,128)S(1)} %bitcast.28, f32[3,16]{1,0:T(4,128)S(1)} %copy-done.6, f32[8,512]{1,0:T(8,128)S(1)} %copy-done.5), custom_call_target="tpu_custom_call" | custom-call | flops 2000000000 | bytes 1048576 | tf_op jit(solution)/shard_map/take/pallas_call | solution.py:270
  69.0 19.1 %all-to-all-done.2.slots_ref = bf16[64,40,128]{2,1,0:T(8,128)(2,1)S(1)} async-done(((bf16[64,40,128]{2,1,0:T(8,128)(2,1)}), bf16[64,40,128]{2,1,0:T(8,128)(2,1)S(1)}, u32[]{:S(2)}, u32[]{:S(2)}) %all-to-all-start.2) | async-done | bytes 655392 | tf_op jit(solution)/shard_map/all_to_all | solution.py:341
  88.1 1.9 %final.1 = bf16[3,512,256]{2,1,0:T(8,128)(2,1)} custom-call(bf16[64,40,128]{2,1,0:T(8,128)(2,1)S(1)} %all-to-all-done.2.slots_ref, bf16[512,1024]{1,0:T(8,128)(2,1)S(1)} %get-tuple-element.41.take_ref, f32[512,128]{1,0:T(8,128)S(1)} %get-tuple-element.42.bias_ref), custom_call_target="tpu_custom_call" | custom-call | bytes 1048576 | tf_op jit(solution)/shard_map/final/pallas_call | solution.py:270
  (30 shorter events, 0.1 us)
Async XLA Ops:
  0.0 49.6 %copy-start = (bf16[3,256,64]{1,2,0:T(8,128)(2,1)S(1)}, bf16[3,256,64]{1,2,0:T(8,128)(2,1)}, u32[]{:S(2)}) copy-start(bf16[3,256,64]{1,2,0:T(8,128)(2,1)} %param.21) | copy-start | bytes 294916
  2.3 27.6 %all-to-all-start = ((bf16[64,24,128]{2,1,0:T(8,128)(2,1)}), bf16[64,24,128]{2,1,0:T(8,128)(2,1)S(1)}, u32[]{:S(2)}, u32[]{:S(2)}) async-start(bf16[64,24,128]{2,1,0:T(8,128)(2,1)} %bitcast.27), calls=%async_computation | async-start | bytes 786432 | tf_op jit(solution)/shard_map/all_to_all | solution.py:291
  15.3 1.0 %copy-start.1 = (bf16[1536,128]{1,0:T(8,128)(2,1)S(1)}, bf16[1536,128]{1,0:T(8,128)(2,1)}, u32[]{:S(2)}) copy-start(bf16[1536,128]{1,0:T(8,128)(2,1)} %get-tuple-element.36.after_ref) | copy-start | bytes 1179652
  16.4 1.2 %copy-start.2 = (f32[2,32768,4]{1,2,0:T(4,128)S(1)}, f32[2,32768,4]{1,2,0:T(4,128)}, u32[]{:S(2)}) copy-start(f32[2,32768,4]{1,2,0:T(4,128)} %param.17) | copy-start | bytes 3145732
  17.6 1.3 %copy-start.7 = (bf16[2560,256]{1,0:T(8,128)(2,1)S(1)}, bf16[2560,256]{1,0:T(8,128)(2,1)}, u32[]{:S(2)}) copy-start(bf16[2560,256]{1,0:T(8,128)(2,1)} %constant.74.clone.factor_ref) | copy-start | bytes 3932164
  18.9 0.9 %copy-start.9 = (f32[4,128,128]{2,1,0:T(8,128)S(1)}, f32[4,128,128]{2,1,0:T(8,128)}, u32[]{:S(2)}) copy-start(f32[4,128,128]{2,1,0:T(8,128)} %constant.75.clone.turn_ref) | copy-start | bytes 786436
  29.9 10.9 %copy-start.3 = (bf16[1,256,256]{2,1,0:T(8,128)(2,1)S(1)}, bf16[1,256,256]{2,1,0:T(8,128)(2,1)}, u32[]{:S(2)}) copy-start(bf16[1,256,256]{2,1,0:T(8,128)(2,1)} %param.19) | copy-start | bytes 393220
  30.0 12.3 %copy-start.4 = (bf16[1,256,256]{2,1,0:T(8,128)(2,1)S(1)}, bf16[1,256,256]{2,1,0:T(8,128)(2,1)}, u32[]{:S(2)}) copy-start(bf16[1,256,256]{2,1,0:T(8,128)(2,1)} %param.20) | copy-start | bytes 393220
  30.0 19.7 %copy-start.11 = (f32[256]{0:T(256)S(1)}, f32[256]{0:T(256)}, u32[]{:S(2)}) copy-start(f32[256]{0:T(256)} %param.18) | copy-start | bytes 3076
  34.5 23.7 %copy-start.8 = (bf16[512,512]{1,0:T(8,128)(2,1)S(1)}, bf16[512,512]{1,0:T(8,128)(2,1)}, u32[]{:S(2)}) copy-start(bf16[512,512]{1,0:T(8,128)(2,1)} %constant.76.clone.lanes_ref) | copy-start | bytes 1572868
  34.5 23.7 %all-to-all-start.1 = ((bf16[64,8,512]{2,1,0:T(8,128)(2,1)}), bf16[64,8,512]{2,1,0:T(8,128)(2,1)S(1)}, u32[]{:S(2)}, u32[]{:S(2)}) async-start(bf16[64,8,512]{2,1,0:T(8,128)(2,1)} %bitcast.7), calls=%async_computation.1 | async-start | bytes 1048576 | tf_op jit(solution)/shard_map/all_to_all | solution.py:291
  40.9 6.0 %collective-permute-start = (bf16[256,256]{1,0:T(8,128)(2,1)S(1)}, bf16[256,256]{1,0:T(8,128)(2,1)S(1)}, u32[]{:S(2)}, u32[]{:S(2)}) collective-permute-start(bf16[256,256]{1,0:T(8,128)(2,1)S(1)} %bitcast.30), channel_id=1, source_target_pairs={{0,1},{1,2},{2,3},{3,0},{4,5},{5,6},{6,7},{7,4},{8,9},{9,10},{10,1... | collective-permute-start | bytes 393224 | tf_op jit(solution)/shard_map/ppermute | solution.py:311
  42.3 4.7 %collective-permute-start.3 = (bf16[256,256]{1,0:T(8,128)(2,1)S(1)}, bf16[256,256]{1,0:T(8,128)(2,1)S(1)}, u32[]{:S(2)}, u32[]{:S(2)}) collective-permute-start(bf16[256,256]{1,0:T(8,128)(2,1)S(1)} %bitcast.33), channel_id=1, source_target_pairs={{0,3},{1,0},{2,1},{3,2},{4,7},{5,4},{6,5},{7,6},{8,11},{9,8},{10,9... | collective-permute-start | bytes 393224 | tf_op jit(solution)/shard_map/ppermute | solution.py:312
  43.8 6.1 %collective-permute-start.1 = (bf16[256,256]{1,0:T(8,128)(2,1)S(1)}, bf16[256,256]{1,0:T(8,128)(2,1)S(1)}, u32[]{:S(2)}, u32[]{:S(2)}) collective-permute-start(bf16[256,256]{1,0:T(8,128)(2,1)S(1)} %bitcast.34), channel_id=1, source_target_pairs={{0,1},{1,2},{2,3},{3,0},{4,5},{5,6},{6,7},{7,4},{8,9},{9,10},{10,1... | collective-permute-start | bytes 393224 | tf_op jit(solution)/shard_map/ppermute | solution.py:315
  43.8 6.2 %collective-permute-start.2 = (bf16[256,256]{1,0:T(8,128)(2,1)S(1)}, bf16[256,256]{1,0:T(8,128)(2,1)S(1)}, u32[]{:S(2)}, u32[]{:S(2)}) collective-permute-start(bf16[256,256]{1,0:T(8,128)(2,1)S(1)} %bitcast.31), channel_id=1, source_target_pairs={{0,3},{1,0},{2,1},{3,2},{4,7},{5,4},{6,5},{7,6},{8,11},{9,8},{10,9... | collective-permute-start | bytes 393224 | tf_op jit(solution)/shard_map/ppermute | solution.py:316
  46.9 5.3 %collective-permute-start.4 = (bf16[256,256]{1,0:T(8,128)(2,1)S(1)}, bf16[256,256]{1,0:T(8,128)(2,1)S(1)}, u32[]{:S(2)}, u32[]{:S(2)}) collective-permute-start(bf16[256,256]{1,0:T(8,128)(2,1)S(1)} %collective-permute-done.refs_2_), channel_id=1, source_target_pairs={{0,1},{1,2},{2,3},{3,0},{4,5},{5,6},{6,7},{7,4},{8,9},{9,10},{10,1... | collective-permute-start | bytes 393224 | tf_op jit(solution)/shard_map/ppermute | solution.py:313
  46.9 5.3 %collective-permute-start.5 = (bf16[256,256]{1,0:T(8,128)(2,1)S(1)}, bf16[256,256]{1,0:T(8,128)(2,1)S(1)}, u32[]{:S(2)}, u32[]{:S(2)}) collective-permute-start(bf16[256,256]{1,0:T(8,128)(2,1)S(1)} %collective-permute-done.3.refs_5_), channel_id=1, source_target_pairs={{0,3},{1,0},{2,1},{3,2},{4,7},{5,4},{6,5},{7,6},{8,11},{9,8},{10,9... | collective-permute-start | bytes 393224 | tf_op jit(solution)/shard_map/ppermute | solution.py:314
  61.6 6.4 %copy-start.10 = (s32[1,512,1,3]{1,2,3,0:T(1,128)S(1)}, s32[1,512,1,3]{1,2,3,0:T(1,128)}, u32[]{:S(2)}) copy-start(s32[1,512,1,3]{1,2,3,0:T(1,128)} %param.24) | copy-start | bytes 18436
  61.6 6.4 %copy-start.5 = (f32[8,512]{1,0:T(8,128)S(1)}, f32[8,512]{1,0:T(8,128)}, u32[]{:S(2)}) copy-start(f32[8,512]{1,0:T(8,128)} %get-tuple-element.40.slot_ref) | copy-start | bytes 49156
  61.6 6.5 %copy-start.6 = (f32[3,16]{1,0:T(4,128)S(1)}, f32[3,16]{1,0:T(4,128)}, u32[]{:S(2)}) copy-start(f32[3,16]{1,0:T(4,128)} %table_ref.1) | copy-start | bytes 580
  61.6 26.5 %all-to-all-start.2 = ((bf16[64,40,128]{2,1,0:T(8,128)(2,1)}), bf16[64,40,128]{2,1,0:T(8,128)(2,1)S(1)}, u32[]{:S(2)}, u32[]{:S(2)}) async-start(bf16[64,40,128]{2,1,0:T(8,128)(2,1)} %expert.1.after_ref), calls=%async_computation.2 | async-start | bytes 1310720 | tf_op jit(solution)/shard_map/all_to_all | solution.py:341

commit v5 on v4

--- a/solution.py
+++ b/solution.py
@@ -42,14 +42,12 @@
 
 
 def tables():
-    order = np.arange(ROWS).reshape(64, 4).T.reshape(-1)
     cos_r, sin_r = cos_sin(ROWS, ROWS, ROWS)
     cos_c, sin_c = cos_sin(COLS, COLS, COLS)
     tw_cos, tw_sin = cos_sin(ROWS, COLS, LENGTH)
-    first = np.concatenate([cos_r[:, order], -sin_r[:, order]], 0)
+    first = np.concatenate([cos_r, -sin_r], 0)
     second = np.block([[cos_c, sin_c], [-sin_c, cos_c]])
-    fourth = np.concatenate([cos_r[order], -sin_r[order]], 0)
-    factors = np.concatenate([part for m in (first, second, fourth) for part in np_split(m)])
+    factors = np.concatenate([part for m in (first, second) for part in np_split(m)])
     turns = [t[i : i + 128] for t in (tw_cos, tw_sin) for i in (0, 128)]
     lane = np.arange(512)
     source = (lane // 16 % 8) * 64 + (lane // 128) * 16 + lane % 16
@@ -94,24 +92,14 @@
 def filter_kernel(x_ref, spec_ref, factor_ref, turn_ref, out_ref, wide, sums, stage):
     first = factor_ref[0:512], factor_ref[512:1024]
     second = factor_ref[1024:1280], factor_ref[1280:1536]
-    fourth = [
-        jnp.concatenate([factor_ref[at : at + 256], factor_ref[at + 256 : at + 512]], 1)
-        for at in (1536, 2048)
-    ]
+    fourth = [jnp.concatenate([part[:256], part[256:]], 1) for part in first]
     wide[...] = x_ref[...].astype(F32)
-    sig = jnp.concatenate(
-        [
-            jnp.concatenate(
-                [
-                    wide[pl.ds(ch % 2 * 8 + pb * 2 + ch // 2, 64, stride=24), :]
-                    for ch in range(4)
-                ],
-                1,
-            )
-            for pb in range(4)
-        ],
-        0,
-    )
+    for ch in range(4):
+        for pb in range(4):
+            sums[ch, pl.ds(pb, 64, stride=4), :] = wide[
+                pl.ds(ch % 2 * 8 + pb * 2 + ch // 2, 64, stride=24), :
+            ]
+    sig = jnp.concatenate([sums[ch] for ch in range(4)], 1)
     sig16 = sig.astype(BF16)
     spec1 = dot(first[0], sig16, NN) + dot(first[1], sig16, NN)
     tcos, tsin = [jnp.concatenate([turn_ref[i], turn_ref[i + 1]], 0) for i in (0, 2)]
@@ -161,7 +149,7 @@
         here = [rank == low, rank == low + 8.0]
         values = []
         for ch in range(4):
-            vals = spread([sums[ch, pl.ds(pb * 64 + block, 1), :] for pb in range(4)])
+            vals = spread([sums[ch, pl.ds(block * 4 + pb, 1), :] for pb in range(4)])
             values += [jnp.where(m, vals, 0.0) for m in here]
         return dot(to, jnp.concatenate(values, 0).astype(BF16), NT)
 
@@ -219,19 +207,39 @@
         hidden = jnp.maximum(dot(normed, part_in[...], NT), 0.0).astype(BF16)
         term = dot(hidden, part_out[...], NN)
         total = term if total is None else total + term
-    full[:, 0:16, :] = total[:, :128].reshape(64, 16, 128)
-    full[:, 16:32, :] = total[:, 128:].reshape(64, 16, 128)
-    scores = dot(normed, gate_ref[...], NT).reshape(64, 2, 8, 256)
-    full[:, 32:40, :] = scores[:, 0, :, :128] + scores[:, 1, :, 128:]
+    for block in range(64):
+        rows = total[block * 16 : (block + 1) * 16]
+        full[block * 34 : block * 34 + 16, :] = rows[:, :128]
+        full[block * 34 + 16 : block * 34 + 32, :] = rows[:, 128:]
+    scores = dot(normed, gate_ref[...], NT)
+    own_lanes = lax.broadcasted_iota(jnp.int32, (1024, 128), 1) // 16 == (
+        lax.broadcasted_iota(jnp.int32, (1024, 128), 0) % 8
+    )
+    row = lax.broadcasted_iota(jnp.int32, (128, 1024), 0)
+    gather = lax.broadcasted_iota(jnp.int32, (128, 1024), 1) // 8 == row % 64 * 2 + row // 64
+    packed = dot(
+        jnp.where(gather, 1.0, 0.0).astype(BF16), jnp.where(own_lanes, scores, 0.0).astype(BF16), NN
+    )
+    for half in range(2):
+        full[pl.ds(32 + half, 64, stride=34), :] = packed[half * 64 : (half + 1) * 64]
     out_ref[...] = full[...].astype(BF16)
 
 
-def take_kernel(after_ref, index_ref, table_ref, slot_ref, take_ref, bias_ref):
+def take_kernel(
+    after_ref, index_ref, table_ref, slot_ref, take_ref, score_ref, lanes_ref, bias_ref
+):
     slot = slot_ref[0:1, :]
-    slot_col = jnp.broadcast_to(slot, (128, 512)).T[:, 0:1].astype(jnp.int32)
+    expert = jnp.floor(slot * (1.0 / CAP))
+    rank = slot - CAP * expert
+    half = jnp.where(rank >= CAP // 2, 1.0, 0.0)
+    codes = [rank * 64 + expert, half * 64 + expert, rank - CAP // 2 * half]
+    codes = jnp.concatenate(codes + [jnp.zeros((125, 512), F32)], 0).T.astype(jnp.int32)
     take_ref[...] = (
-        lax.broadcasted_iota(jnp.int32, (512, EXPERTS * CAP), 1) == slot_col
+        lax.broadcasted_iota(jnp.int32, (512, EXPERTS * CAP), 1) == codes[:, 0:1]
     ).astype(F32).astype(BF16)
+    lane = lax.broadcasted_iota(jnp.int32, (512, 128), 1)
+    score_ref[...] = (lane == codes[:, 1:2]).astype(F32).astype(BF16)
+    lanes_ref[...] = (lane // 16 == codes[:, 2:3]).astype(F32)
     rows = []
     for t in range(TASKS):
         idx = index_ref[t : t + 1, :]
@@ -239,26 +247,25 @@
         for r in range(table_ref.shape[1]):
             bias = jnp.where(idx == r, table_ref[t, r], bias)
         rows.append(bias)
-    rank = slot - CAP * jnp.floor(slot * (1.0 / CAP))
-    rows.append(jnp.where(rank >= CAP // 2, 1.0, 0.0))
-    rows.append(jnp.zeros((128 - TASKS - 1, 512), F32))
+    rows.append(jnp.zeros((128 - TASKS, 512), F32))
     bias_ref[...] = jnp.concatenate(rows, 0).T
 
 
-def final_kernel(slots_ref, take_ref, bias_ref, out_ref):
-    low = slots_ref[:, 0:16, :].reshape(1024, 128)
-    high = slots_ref[:, 16:32, :].reshape(1024, 128)
-    score = slots_ref[...].astype(F32)[:, 32:40, :]
-    score = jnp.concatenate([score, score], 1).reshape(1024, 128).astype(BF16)
-    rows = dot(take_ref[...], jnp.concatenate([low, high, score], 1), NN)
-    bias = bias_ref[...]
-    both = rows[:, 256:384]
-    chosen = jnp.where(
-        bias[:, 3:4] > 0.5, jnp.concatenate([both[:, 64:], both[:, :64]], 1), both
-    )
-    gates = jax.nn.sigmoid(chosen + bias)
+def final_kernel(slots_ref, take_ref, score_ref, lanes_ref, bias_ref, out_ref, wide):
+    wide[...] = slots_ref[...].astype(F32)
+
+    def rows_of(at, count):
+        return jnp.concatenate(
+            [wide[pl.ds(at + r, 64, stride=34), :] for r in range(count)], 0
+        ).astype(BF16)
+
+    gates = dot(score_ref[...], rows_of(32, 2), NN) * lanes_ref[...]
+    for shift in (64, 32, 16):
+        gates = gates + pltpu.roll(gates, shift, 1)
+    gates = jax.nn.sigmoid(gates + bias_ref[...])
+    rows = dot(take_ref[...], jnp.concatenate([rows_of(0, 16), rows_of(16, 16)], 1), NN)
     for t in range(TASKS):
-        out_ref[t] = (gates[:, t : t + 1] * rows[:, :256]).astype(BF16)
+        out_ref[t] = (gates[:, t : t + 1] * rows).astype(BF16)
 
 
 def call(kernel, outs, *args, scratch=(), smem=(), far=(), flops=0, vmem=32, name=None):
@@ -330,21 +337,30 @@
     slots_in = swap(sums, 8)
     me = lax.axis_index("seq")
     gate = lax.dynamic_index_in_dim(gate_weight.transpose(0, 2, 1), me, 1, keepdims=False)
-    gate = jnp.zeros((256, 256), BF16).at[0:TASKS].set(gate).at[192 : 192 + TASKS].set(gate)
+    gate = jnp.tile(jnp.pad(gate, ((0, 16 - TASKS), (0, 0))), (8, 1))
     slots_out = call(
-        expert_kernel, shape((64, 40, 128), BF16),
+        expert_kernel, shape((64 * 34, 128), BF16),
         slots_in, lanes, ln_gain.reshape(256, 1), gate,
         own_in, own_out, one_in, one_out, two_in, two_out, far_in, far_out,
         name="expert", flops=10**9,
-        scratch=[big((4, 512, 128), F32), big((256, 128), F32), big((64, 40, 128), F32)],
-    )
-    results = lax.all_to_all(slots_out, "seq", split_axis=0, concat_axis=0, tiled=True)
-    take, bias = call(
-        take_kernel, [shape((512, 1024), BF16), shape((512, 128), F32)], slots_out,
-        gate_index.reshape(512, 3).T, gate_table, slot, far=(0,), smem=(2,), name="take",
-        flops=2 * 10**9,
-    )
-    out = call(final_kernel, shape((3, 512, 256), BF16), results, take, bias, name="final")
+        scratch=[big((4, 512, 128), F32), big((256, 128), F32), big((64 * 34, 128), F32)],
+    )
+    results = lax.all_to_all(
+        slots_out.reshape(64, 17, 2, 128), "seq", split_axis=0, concat_axis=0, tiled=True
+    ).reshape(64 * 34, 128)
+    take, score, score_lanes, bias = call(
+        take_kernel,
+        [
+            shape((512, 1024), BF16), shape((512, 128), BF16), shape((512, 128), F32),
+            shape((512, 128), F32),
+        ],
+        slots_out, gate_index.reshape(512, 3).T, gate_table, slot, far=(0,), smem=(2,),
+        name="take", flops=2 * 10**9,
+    )
+    out = call(
+        final_kernel, shape((3, 512, 256), BF16), results, take, score, score_lanes, bias,
+        scratch=[big((64 * 34, 128), F32)], name="final",
+    )
     return out.reshape(TASKS, 1, 512, 1, 256)
 
 

time: 90.6 us -> 88.4 us (0.976)
  waiting for transfers between devices: 37.5 us -> 36.2 us
  local copies, waits for them, and re-layouts: 4.84 us -> 3.91 us
    all_to_all x1, waiting for transfers between devices: 19.1 us -> 16.1 us  [on_device(): lax.all_to_all(slots_out.reshape(64, 17, 2, 128), 'seq', split_axis=0, co...]
    all_to_all x2, waiting for transfers between devices: 15.6 us -> 17.8 us  [swap(): lax.all_to_all(chunks, 'seq', split_axis=0, concat_axis=0, tiled=True)]
  transfers between devices with their start and end apart: 9 -> 9, of which waited for: 5 -> 5; matrix products, arithmetic and copies ran while one was open for 0% -> 0% of each run, Pallas kernels for 1% -> 2%
where the time goes in v5:
time: 88.4 us; the launch traced here: 87.8 us
  waiting for transfers between devices  36.2 us (41%)
  starting transfers between devices  34.1 us (39%)
  Pallas kernels  13.4 us (15%)
  local copies, waits for them, and re-layouts  3.91 us (4%)
    all_to_all x2, starting transfers between devices, swap(): lax.all_to_all(chunks, 'seq', split_axis=0, concat_axis=0, tiled=True)  19.5 us
    all_to_all x2, waiting for transfers between devices, swap(): lax.all_to_all(chunks, 'seq', split_axis=0, concat_axis=0, tiled=True)  17.8 us
    all_to_all x1, waiting for transfers between devices, on_device(): lax.all_to_all(slots_out.reshape(64, 17, 2, 128), 'seq', split_axis=0, co...  16.1 us
    pallas_call x6, Pallas kernels, call(): pl.pallas_call(kernel, out_shape=outs, in_specs=specs, out_specs=[pl.Bloc...  13.4 us
    all_to_all x1, starting transfers between devices, on_device(): lax.all_to_all(slots_out.reshape(64, 17, 2, 128), 'seq', split_axis=0, co...  6.41 us
    unnamed x26, local copies, waits for them, and re-layouts  3.76 us
    ppermute x1, starting transfers between devices, on_device(): far_out = lax.ppermute(two_out, 'batch', behind)  2.67 us
    ppermute x1, starting transfers between devices, on_device(): two_in = lax.ppermute(own_in, 'batch', behind)  2.67 us
  transfers between devices with their start and end apart: 9, of which 5 were waited for; matrix products, arithmetic and copies ran while one was open for 0% of the time, Pallas kernels for 2%

profile of v5, /device:TPU:1, one launch (start us, length us, event | category | flops | bytes accessed | tf_op | source)
XLA Modules:
  0.0 87.8 jit_solution(13361672148751300924)
XLA Ops:
  0.0 2.3 %prep.1 = (bf16[1536,128]{1,0:T(8,128)(2,1)}, f32[8,512]{1,0:T(8,128)}) custom-call(bf16[512,256]{1,0:T(8,128)(2,1)} %bitcast.41, s32[1,512]{1,0:T(1,128)} %bitcast.43), custom_call_target="tpu_custom_call" | custom-call | bytes 1048576 | tf_op jit(solution)/shard_map/prep/pallas_call | solution.py:277
  2.3 0.0 copy-start.9
  2.4 13.1 %all-to-all-start = ((bf16[64,24,128]{2,1,0:T(8,128)(2,1)}), bf16[64,24,128]{2,1,0:T(8,128)(2,1)S(1)}, u32[]{:S(2)}, u32[]{:S(2)}) async-start(bf16[64,24,128]{2,1,0:T(8,128)(2,1)} %bitcast.31), calls=%async_computation | async-start | bytes 786432 | tf_op jit(solution)/shard_map/all_to_all | solution.py:298
  15.5 1.2 %copy-done.2 = f32[2,32768,4]{1,2,0:T(4,128)S(1)} copy-done((f32[2,32768,4]{1,2,0:T(4,128)S(1)}, f32[2,32768,4]{1,2,0:T(4,128)}, u32[]{:S(2)}) %copy-start.2) | copy-done | bytes 1048600
  16.7 1.1 %copy-done.7 = bf16[1536,256]{1,0:T(8,128)(2,1)S(1)} copy-done((bf16[1536,256]{1,0:T(8,128)(2,1)S(1)}, bf16[1536,256]{1,0:T(8,128)(2,1)}, u32[]{:S(2)}) %copy-start.7) | copy-done | bytes 786456
  17.9 0.4 ready.1
  18.2 11.9 %all-to-all-done = bf16[64,24,128]{2,1,0:T(8,128)(2,1)S(1)} async-done(((bf16[64,24,128]{2,1,0:T(8,128)(2,1)}), bf16[64,24,128]{2,1,0:T(8,128)(2,1)S(1)}, u32[]{:S(2)}, u32[]{:S(2)}) %all-to-all-start) | async-done | bytes 393248 | tf_op jit(solution)/shard_map/all_to_all | solution.py:298
  30.1 4.6 %filter.1 = bf16[512,512]{1,0:T(8,128)(2,1)} custom-call(bf16[1536,128]{1,0:T(8,128)(2,1)S(1)} %bitcast.30, f32[2,128,1024]{2,1,0:T(8,128)S(1)} %get-tuple-element.15.spec_ref, bf16[1536,256]{1,0:T(8,128)(2,1)S(1)} %get-tuple-element.16.factor_ref, f32[4,128,128]{2,1,0:T(8,128)S(1)} %get-tuple-element.17.turn_ref), custom_call_target="tpu_custom_call" | custom-call | flops 2000000000 | bytes 1048576 | tf_op jit(solution)/shard_map/filter/pallas_call | solution.py:277
  34.7 6.3 %all-to-all-start.1 = ((bf16[64,8,512]{2,1,0:T(8,128)(2,1)}), bf16[64,8,512]{2,1,0:T(8,128)(2,1)S(1)}, u32[]{:S(2)}, u32[]{:S(2)}) async-start(bf16[64,8,512]{2,1,0:T(8,128)(2,1)} %bitcast.7), calls=%async_computation.1 | async-start | bytes 1048576 | tf_op jit(solution)/shard_map/all_to_all | solution.py:298
  41.1 1.4 %collective-permute-start = (bf16[256,256]{1,0:T(8,128)(2,1)S(1)}, bf16[256,256]{1,0:T(8,128)(2,1)S(1)}, u32[]{:S(2)}, u32[]{:S(2)}) collective-permute-start(bf16[256,256]{1,0:T(8,128)(2,1)S(1)} %bitcast.35), channel_id=1, source_target_pairs={{0,1},{1,2},{2,3},{3,0},{4,5},{5,6},{6,7},{7,4},{8,9},{9,10},{10,1... | collective-permute-start | bytes 393224 | tf_op jit(solution)/shard_map/ppermute | solution.py:318
  42.4 1.5 %collective-permute-start.3 = (bf16[256,256]{1,0:T(8,128)(2,1)S(1)}, bf16[256,256]{1,0:T(8,128)(2,1)S(1)}, u32[]{:S(2)}, u32[]{:S(2)}) collective-permute-start(bf16[256,256]{1,0:T(8,128)(2,1)S(1)} %bitcast.38), channel_id=1, source_target_pairs={{0,3},{1,0},{2,1},{3,2},{4,7},{5,4},{6,5},{7,6},{8,11},{9,8},{10,9... | collective-permute-start | bytes 393224 | tf_op jit(solution)/shard_map/ppermute | solution.py:319
  44.0 2.7 %collective-permute-start.2 = (bf16[256,256]{1,0:T(8,128)(2,1)S(1)}, bf16[256,256]{1,0:T(8,128)(2,1)S(1)}, u32[]{:S(2)}, u32[]{:S(2)}) collective-permute-start(bf16[256,256]{1,0:T(8,128)(2,1)S(1)} %bitcast.36), channel_id=1, source_target_pairs={{0,3},{1,0},{2,1},{3,2},{4,7},{5,4},{6,5},{7,6},{8,11},{9,8},{10,9... | collective-permute-start | bytes 393224 | tf_op jit(solution)/shard_map/ppermute | solution.py:323
  46.6 0.4 collective-permute-done.refs_2_
  47.1 2.7 %collective-permute-start.5 = (bf16[256,256]{1,0:T(8,128)(2,1)S(1)}, bf16[256,256]{1,0:T(8,128)(2,1)S(1)}, u32[]{:S(2)}, u32[]{:S(2)}) collective-permute-start(bf16[256,256]{1,0:T(8,128)(2,1)S(1)} %collective-permute-done.3.refs_5_), channel_id=1, source_target_pairs={{0,3},{1,0},{2,1},{3,2},{4,7},{5,4},{6,5},{7,6},{8,11},{9,8},{10,9... | collective-permute-start | bytes 393224 | tf_op jit(solution)/shard_map/ppermute | solution.py:321
  49.8 0.7 copy-done.11
  50.5 0.1 copy.16.gain_ref
  50.6 1.8 %collective-permute-done.4.refs_6_ = bf16[256,256]{1,0:T(8,128)(2,1)S(1)} collective-permute-done((bf16[256,256]{1,0:T(8,128)(2,1)S(1)}, bf16[256,256]{1,0:T(8,128)(2,1)S(1)}, u32[]{:S(2)}, u32[]{:S(2)}) %collective-permute-start.4) | collective-permute-done | bytes 131104 | tf_op jit(solution)/shard_map/ppermute | solution.py:320
  52.4 6.0 %all-to-all-done.1 = bf16[64,8,512]{2,1,0:T(8,128)(2,1)S(1)} async-done(((bf16[64,8,512]{2,1,0:T(8,128)(2,1)}), bf16[64,8,512]{2,1,0:T(8,128)(2,1)S(1)}, u32[]{:S(2)}, u32[]{:S(2)}) %all-to-all-start.1) | async-done | bytes 524320 | tf_op jit(solution)/shard_map/all_to_all | solution.py:298
  58.4 3.4 %expert.1.after_ref = bf16[2176,128]{1,0:T(8,128)(2,1)} custom-call(bf16[512,512]{1,0:T(8,128)(2,1)S(1)} %bitcast.29, bf16[512,512]{1,0:T(8,128)(2,1)S(1)} %copy-done.8, f32[256,1]{1,0:T(8,128)S(1)} %copy.16.gain_ref, bf16[128,256]{1,0:T(8,128)(2,1)S(1)} %bitcast.32, bf16[256,256]{1,0:T(8,128)(2,1)S(1)} %bitcast.37, bf16[256,256]{1,0:T(8,128)(2,1)S(1)} %bitcast.40, ...), custom_call_target="tpu_custom_call" | custom-call | flops 1000000000 | bytes 1048576 | tf_op jit(solution)/shard_map/expert/pallas_call | solution.py:277
  61.7 6.4 %all-to-all-start.2 = ((bf16[64,17,2,128]{3,2,1,0:T(2,128)(2,1)}), bf16[64,17,2,128]{3,2,1,0:T(2,128)(2,1)S(1)}, u32[]{:S(2)}, u32[]{:S(2)}) async-start(bf16[64,17,2,128]{3,2,1,0:T(2,128)(2,1)} %bitcast.13), calls=%async_computation.2 | async-start | bytes 1114112 | tf_op jit(solution)/shard_map/all_to_all | solution.py:348
  68.2 0.7 copy-done.5
  68.9 1.2 %take.1 = (bf16[512,1024]{1,0:T(8,128)(2,1)S(1)}, bf16[512,128]{1,0:T(8,128)(2,1)S(1)}, f32[512,128]{1,0:T(8,128)S(1)}, f32[512,128]{1,0:T(8,128)S(1)}) custom-call(bf16[2176,128]{1,0:T(8,128)(2,1)} %expert.1.after_ref, s32[3,512]{1,0:T(4,128)S(1)} %bitcast.33, f32[3,16]{1,0:T(4,128)S(1)} %copy-done.6, f32[8,512]{1,0:T(8,128)S(1)} %copy-done.5), custom_call_target="tpu_custom_call" | custom-call | flops 2000000000 | bytes 1048576 | tf_op jit(solution)/shard_map/take/pallas_call | solution.py:277
  70.1 16.1 %all-to-all-done.2 = bf16[64,17,2,128]{3,2,1,0:T(2,128)(2,1)S(1)} async-done(((bf16[64,17,2,128]{3,2,1,0:T(2,128)(2,1)}), bf16[64,17,2,128]{3,2,1,0:T(2,128)(2,1)S(1)}, u32[]{:S(2)}, u32[]{:S(2)}) %all-to-all-start.2) | async-done | bytes 557088 | tf_op jit(solution)/shard_map/all_to_all | solution.py:348
  86.2 1.6 %final.1 = bf16[3,512,256]{2,1,0:T(8,128)(2,1)} custom-call(bf16[2176,128]{1,0:T(8,128)(2,1)S(1)} %bitcast.28, bf16[512,1024]{1,0:T(8,128)(2,1)S(1)} %get-tuple-element.19.take_ref, bf16[512,128]{1,0:T(8,128)(2,1)S(1)} %get-tuple-element.20.score_ref, f32[512,128]{1,0:T(8,128)S(1)} %get-tuple-element.21.lanes_ref, f32[512,128]{1,0:T(8,128)S(1)} %get-tuple-element.22.bias_ref), custom_call_target="tpu_custom_call" | custom-call | bytes 1048576 | tf_op jit(solution)/shard_map/final/pallas_call | solution.py:277
  (30 shorter events, 0.1 us)
Async XLA Ops:
  0.0 49.8 %copy-start = (bf16[3,256,64]{1,2,0:T(8,128)(2,1)S(1)}, bf16[3,256,64]{1,2,0:T(8,128)(2,1)}, u32[]{:S(2)}) copy-start(bf16[3,256,64]{1,2,0:T(8,128)(2,1)} %param.17) | copy-start | bytes 294916
  2.3 13.2 %copy-start.1 = (bf16[1536,128]{1,0:T(8,128)(2,1)S(1)}, bf16[1536,128]{1,0:T(8,128)(2,1)}, u32[]{:S(2)}) copy-start(bf16[1536,128]{1,0:T(8,128)(2,1)} %get-tuple-element.14.after_ref) | copy-start | bytes 1179652
  2.3 13.2 %copy-start.9 = (f32[4,128,128]{2,1,0:T(8,128)S(1)}, f32[4,128,128]{2,1,0:T(8,128)}, u32[]{:S(2)}) copy-start(f32[4,128,128]{2,1,0:T(8,128)} %constant.22.clone.turn_ref) | copy-start | bytes 786436
  2.4 27.7 %all-to-all-start = ((bf16[64,24,128]{2,1,0:T(8,128)(2,1)}), bf16[64,24,128]{2,1,0:T(8,128)(2,1)S(1)}, u32[]{:S(2)}, u32[]{:S(2)}) async-start(bf16[64,24,128]{2,1,0:T(8,128)(2,1)} %bitcast.31), calls=%async_computation | async-start | bytes 786432 | tf_op jit(solution)/shard_map/all_to_all | solution.py:298
  15.5 1.2 %copy-start.2 = (f32[2,32768,4]{1,2,0:T(4,128)S(1)}, f32[2,32768,4]{1,2,0:T(4,128)}, u32[]{:S(2)}) copy-start(f32[2,32768,4]{1,2,0:T(4,128)} %param.13) | copy-start | bytes 3145732
  16.7 1.1 %copy-start.7 = (bf16[1536,256]{1,0:T(8,128)(2,1)S(1)}, bf16[1536,256]{1,0:T(8,128)(2,1)}, u32[]{:S(2)}) copy-start(bf16[1536,256]{1,0:T(8,128)(2,1)} %constant.21.clone.factor_ref) | copy-start | bytes 2359300
  34.7 6.4 %copy-start.3 = (bf16[1,256,256]{2,1,0:T(8,128)(2,1)S(1)}, bf16[1,256,256]{2,1,0:T(8,128)(2,1)}, u32[]{:S(2)}) copy-start(bf16[1,256,256]{2,1,0:T(8,128)(2,1)} %param.15) | copy-start | bytes 393220
  34.7 7.7 %copy-start.4 = (bf16[1,256,256]{2,1,0:T(8,128)(2,1)S(1)}, bf16[1,256,256]{2,1,0:T(8,128)(2,1)}, u32[]{:S(2)}) copy-start(bf16[1,256,256]{2,1,0:T(8,128)(2,1)} %param.16) | copy-start | bytes 393220
  34.7 23.7 %copy-start.8 = (bf16[512,512]{1,0:T(8,128)(2,1)S(1)}, bf16[512,512]{1,0:T(8,128)(2,1)}, u32[]{:S(2)}) copy-start(bf16[512,512]{1,0:T(8,128)(2,1)} %constant.23.clone.lanes_ref) | copy-start | bytes 1572868
  34.7 23.7 %all-to-all-start.1 = ((bf16[64,8,512]{2,1,0:T(8,128)(2,1)}), bf16[64,8,512]{2,1,0:T(8,128)(2,1)S(1)}, u32[]{:S(2)}, u32[]{:S(2)}) async-start(bf16[64,8,512]{2,1,0:T(8,128)(2,1)} %bitcast.7), calls=%async_computation.1 | async-start | bytes 1048576 | tf_op jit(solution)/shard_map/all_to_all | solution.py:298
  41.1 6.0 %collective-permute-start = (bf16[256,256]{1,0:T(8,128)(2,1)S(1)}, bf16[256,256]{1,0:T(8,128)(2,1)S(1)}, u32[]{:S(2)}, u32[]{:S(2)}) collective-permute-start(bf16[256,256]{1,0:T(8,128)(2,1)S(1)} %bitcast.35), channel_id=1, source_target_pairs={{0,1},{1,2},{2,3},{3,0},{4,5},{5,6},{6,7},{7,4},{8,9},{9,10},{10,1... | collective-permute-start | bytes 393224 | tf_op jit(solution)/shard_map/ppermute | solution.py:318
  42.4 4.7 %collective-permute-start.3 = (bf16[256,256]{1,0:T(8,128)(2,1)S(1)}, bf16[256,256]{1,0:T(8,128)(2,1)S(1)}, u32[]{:S(2)}, u32[]{:S(2)}) collective-permute-start(bf16[256,256]{1,0:T(8,128)(2,1)S(1)} %bitcast.38), channel_id=1, source_target_pairs={{0,3},{1,0},{2,1},{3,2},{4,7},{5,4},{6,5},{7,6},{8,11},{9,8},{10,9... | collective-permute-start | bytes 393224 | tf_op jit(solution)/shard_map/ppermute | solution.py:319
  44.0 6.7 %collective-permute-start.1 = (bf16[256,256]{1,0:T(8,128)(2,1)S(1)}, bf16[256,256]{1,0:T(8,128)(2,1)S(1)}, u32[]{:S(2)}, u32[]{:S(2)}) collective-permute-start(bf16[256,256]{1,0:T(8,128)(2,1)S(1)} %bitcast.39), channel_id=1, source_target_pairs={{0,1},{1,2},{2,3},{3,0},{4,5},{5,6},{6,7},{7,4},{8,9},{9,10},{10,1... | collective-permute-start | bytes 393224 | tf_op jit(solution)/shard_map/ppermute | solution.py:322
  44.0 6.7 %collective-permute-start.2 = (bf16[256,256]{1,0:T(8,128)(2,1)S(1)}, bf16[256,256]{1,0:T(8,128)(2,1)S(1)}, u32[]{:S(2)}, u32[]{:S(2)}) collective-permute-start(bf16[256,256]{1,0:T(8,128)(2,1)S(1)} %bitcast.36), channel_id=1, source_target_pairs={{0,3},{1,0},{2,1},{3,2},{4,7},{5,4},{6,5},{7,6},{8,11},{9,8},{10,9... | collective-permute-start | bytes 393224 | tf_op jit(solution)/shard_map/ppermute | solution.py:323
  47.1 5.3 %collective-permute-start.4 = (bf16[256,256]{1,0:T(8,128)(2,1)S(1)}, bf16[256,256]{1,0:T(8,128)(2,1)S(1)}, u32[]{:S(2)}, u32[]{:S(2)}) collective-permute-start(bf16[256,256]{1,0:T(8,128)(2,1)S(1)} %collective-permute-done.refs_2_), channel_id=1, source_target_pairs={{0,1},{1,2},{2,3},{3,0},{4,5},{5,6},{6,7},{7,4},{8,9},{9,10},{10,1... | collective-permute-start | bytes 393224 | tf_op jit(solution)/shard_map/ppermute | solution.py:320
  47.1 5.3 %collective-permute-start.5 = (bf16[256,256]{1,0:T(8,128)(2,1)S(1)}, bf16[256,256]{1,0:T(8,128)(2,1)S(1)}, u32[]{:S(2)}, u32[]{:S(2)}) collective-permute-start(bf16[256,256]{1,0:T(8,128)(2,1)S(1)} %collective-permute-done.3.refs_5_), channel_id=1, source_target_pairs={{0,3},{1,0},{2,1},{3,2},{4,7},{5,4},{6,5},{7,6},{8,11},{9,8},{10,9... | collective-permute-start | bytes 393224 | tf_op jit(solution)/shard_map/ppermute | solution.py:321
  49.8 0.7 copy-start.11
  61.7 6.4 %copy-start.10 = (s32[1,512,1,3]{1,2,3,0:T(1,128)S(1)}, s32[1,512,1,3]{1,2,3,0:T(1,128)}, u32[]{:S(2)}) copy-start(s32[1,512,1,3]{1,2,3,0:T(1,128)} %param.20) | copy-start | bytes 18436
  61.7 6.5 %copy-start.6 = (f32[3,16]{1,0:T(4,128)S(1)}, f32[3,16]{1,0:T(4,128)}, u32[]{:S(2)}) copy-start(f32[3,16]{1,0:T(4,128)} %table_ref.1) | copy-start | bytes 580
  61.7 24.5 %all-to-all-start.2 = ((bf16[64,17,2,128]{3,2,1,0:T(2,128)(2,1)}), bf16[64,17,2,128]{3,2,1,0:T(2,128)(2,1)S(1)}, u32[]{:S(2)}, u32[]{:S(2)}) async-start(bf16[64,17,2,128]{3,2,1,0:T(2,128)(2,1)} %bitcast.13), calls=%async_computation.2 | async-start | bytes 1114112 | tf_op jit(solution)/shard_map/all_to_all | solution.py:348
  68.2 0.7 copy-start.5

commit v6 on v5

--- a/solution.py
+++ b/solution.py
@@ -55,7 +55,7 @@
     return factors, np.stack(turns).astype(np.float32), lanes
 
 
-def prep_kernel(ev_ref, routes_ref, out_ref, slot_ref, landed, named, mid, wide, sems):
+def prep_kernel(ev_ref, routes_ref, out_ref, slot_ref, landed, named, before, mid, wide, sems):
     copies = [
         pltpu.make_async_copy(
             ev_ref.at[pl.ds(pb * 128, 128)], landed.at[pl.ds(pb * 128, 128)], sems.at[pb]
@@ -65,13 +65,14 @@
     copies.append(pltpu.make_async_copy(routes_ref, named, sems.at[4]))
     for copy in copies[::-1]:
         copy.start()
+    before[...] = (
+        lax.broadcasted_iota(jnp.int32, (512, 512), 0)
+        < lax.broadcasted_iota(jnp.int32, (512, 512), 1)
+    ).astype(F32).astype(BF16)
     copies[4].wait()
     experts = named[...]
     onehot = (lax.broadcasted_iota(jnp.int32, (EXPERTS, 512), 0) == experts).astype(F32)
-    before = lax.broadcasted_iota(jnp.int32, (512, 512), 0) < lax.broadcasted_iota(
-        jnp.int32, (512, 512), 1
-    )
-    earlier = dot(onehot.astype(BF16), before.astype(F32).astype(BF16), NN)
+    earlier = dot(onehot.astype(BF16), before[...], NN)
     rank = jnp.sum(earlier * onehot, 0, keepdims=True)
     experts = experts.astype(F32)
     slot_ref[...] = jnp.broadcast_to(experts * CAP + rank, (8, 512))
@@ -82,7 +83,7 @@
             )
     for pb in range(4):
         copies[pb].wait()
-        mid[...] = landed[pb * 128 : (pb + 1) * 128, :].astype(F32).T
+        mid[...] = landed[pb * 128 : (pb + 1) * 128, :].T.astype(F32)
         for ch in range(4):
             chp, chl = ch // 2, ch % 2
             wide[pl.ds(chl * 8 + pb * 2 + chp, 64, stride=24), :] = mid[pl.ds(ch, 64, stride=4), :]
@@ -200,13 +201,12 @@
         centre = jnp.sum(vals, 0, keepdims=True) * (1.0 / 256)
         off = vals - centre
         spread = jnp.sum(off * off, 0, keepdims=True) * (1.0 / 256)
-        normed.append((off * lax.rsqrt(spread + 1e-05) * gain_ref[...]).T.astype(BF16))
+        normed.append((off * lax.rsqrt(spread + 1e-05) * gain_ref[...]).astype(BF16).T)
     normed = jnp.concatenate(normed, 0)
-    total = None
-    for part_in, part_out in zip(refs[0:8:2], refs[1:8:2]):
-        hidden = jnp.maximum(dot(normed, part_in[...], NT), 0.0).astype(BF16)
-        term = dot(hidden, part_out[...], NN)
-        total = term if total is None else total + term
+    all_in = jnp.concatenate([ref[...] for ref in refs[0:8:2]], 0)
+    all_out = jnp.concatenate([ref[...] for ref in refs[1:8:2]], 0)
+    hidden = jnp.maximum(dot(normed, all_in, NT), 0.0).astype(BF16)
+    total = dot(hidden, all_out, NN)
     for block in range(64):
         rows = total[block * 16 : (block + 1) * 16]
         full[block * 34 : block * 34 + 16, :] = rows[:, :128]
@@ -308,7 +308,8 @@
         prep_kernel, [shape((1536, 128), BF16), shape((8, 512), F32)],
         events.reshape(512, 256), routes.reshape(1, 512), far=(0, 1), name="prep", vmem=60,
         scratch=[
-            big((512, 256), BF16), big((1, 512), jnp.int32), big((256, 128), F32),
+            big((512, 256), BF16), big((1, 512), jnp.int32), big((512, 512), BF16),
+            big((256, 128), F32),
             big((1536, 128), F32), pltpu.SemaphoreType.DMA((5,)),
         ],
     )

time: 88.4 us -> 88.1 us (level)
  no operation moved by 1% of the time
where the time goes in v6:
time: 88.1 us; the launch traced here: 87.6 us
  waiting for transfers between devices  36.2 us (41%)
  starting transfers between devices  34.1 us (39%)
  Pallas kernels  13.2 us (15%)
  local copies, waits for them, and re-layouts  3.91 us (4%)
    all_to_all x2, starting transfers between devices, swap(): lax.all_to_all(chunks, 'seq', split_axis=0, concat_axis=0, tiled=True)  19.5 us
    all_to_all x2, waiting for transfers between devices, swap(): lax.all_to_all(chunks, 'seq', split_axis=0, concat_axis=0, tiled=True)  17.8 us
    all_to_all x1, waiting for transfers between devices, on_device(): lax.all_to_all(slots_out.reshape(64, 17, 2, 128), 'seq', split_axis=0, co...  16.1 us
    pallas_call x6, Pallas kernels, call(): pl.pallas_call(kernel, out_shape=outs, in_specs=specs, out_specs=[pl.Bloc...  13.2 us
    all_to_all x1, starting transfers between devices, on_device(): lax.all_to_all(slots_out.reshape(64, 17, 2, 128), 'seq', split_axis=0, co...  6.41 us
    unnamed x26, local copies, waits for them, and re-layouts  3.76 us
    ppermute x1, starting transfers between devices, on_device(): far_out = lax.ppermute(two_out, 'batch', behind)  2.67 us
    ppermute x1, starting transfers between devices, on_device(): two_in = lax.ppermute(own_in, 'batch', behind)  2.67 us
  transfers between devices with their start and end apart: 9, of which 5 were waited for; matrix products, arithmetic and copies ran while one was open for 0% of the time, Pallas kernels for 2%

profile of v6, /device:TPU:1, one launch (start us, length us, event | category | flops | bytes accessed | tf_op | source)
XLA Modules:
  0.0 87.6 jit_solution(5790191502877762426)
XLA Ops:
  0.0 2.2 %prep.1 = (bf16[1536,128]{1,0:T(8,128)(2,1)}, f32[8,512]{1,0:T(8,128)}) custom-call(bf16[512,256]{1,0:T(8,128)(2,1)} %bitcast.41, s32[1,512]{1,0:T(1,128)} %bitcast.43), custom_call_target="tpu_custom_call" | custom-call | bytes 1048576 | tf_op jit(solution)/shard_map/prep/pallas_call | solution.py:277
  2.2 0.0 copy-start.9
  2.2 13.1 %all-to-all-start = ((bf16[64,24,128]{2,1,0:T(8,128)(2,1)}), bf16[64,24,128]{2,1,0:T(8,128)(2,1)S(1)}, u32[]{:S(2)}, u32[]{:S(2)}) async-start(bf16[64,24,128]{2,1,0:T(8,128)(2,1)} %bitcast.31), calls=%async_computation | async-start | bytes 786432 | tf_op jit(solution)/shard_map/all_to_all | solution.py:298
  15.4 1.2 %copy-done.2 = f32[2,32768,4]{1,2,0:T(4,128)S(1)} copy-done((f32[2,32768,4]{1,2,0:T(4,128)S(1)}, f32[2,32768,4]{1,2,0:T(4,128)}, u32[]{:S(2)}) %copy-start.2) | copy-done | bytes 1048600
  16.6 1.1 %copy-done.7 = bf16[1536,256]{1,0:T(8,128)(2,1)S(1)} copy-done((bf16[1536,256]{1,0:T(8,128)(2,1)S(1)}, bf16[1536,256]{1,0:T(8,128)(2,1)}, u32[]{:S(2)}) %copy-start.7) | copy-done | bytes 786456
  17.7 0.4 ready.1
  18.1 11.9 %all-to-all-done = bf16[64,24,128]{2,1,0:T(8,128)(2,1)S(1)} async-done(((bf16[64,24,128]{2,1,0:T(8,128)(2,1)}), bf16[64,24,128]{2,1,0:T(8,128)(2,1)S(1)}, u32[]{:S(2)}, u32[]{:S(2)}) %all-to-all-start) | async-done | bytes 393248 | tf_op jit(solution)/shard_map/all_to_all | solution.py:298
  30.0 4.6 %filter.1 = bf16[512,512]{1,0:T(8,128)(2,1)} custom-call(bf16[1536,128]{1,0:T(8,128)(2,1)S(1)} %bitcast.30, f32[2,128,1024]{2,1,0:T(8,128)S(1)} %get-tuple-element.15.spec_ref, bf16[1536,256]{1,0:T(8,128)(2,1)S(1)} %get-tuple-element.16.factor_ref, f32[4,128,128]{2,1,0:T(8,128)S(1)} %get-tuple-element.17.turn_ref), custom_call_target="tpu_custom_call" | custom-call | flops 2000000000 | bytes 1048576 | tf_op jit(solution)/shard_map/filter/pallas_call | solution.py:277
  34.6 6.3 %all-to-all-start.1 = ((bf16[64,8,512]{2,1,0:T(8,128)(2,1)}), bf16[64,8,512]{2,1,0:T(8,128)(2,1)S(1)}, u32[]{:S(2)}, u32[]{:S(2)}) async-start(bf16[64,8,512]{2,1,0:T(8,128)(2,1)} %bitcast.7), calls=%async_computation.1 | async-start | bytes 1048576 | tf_op jit(solution)/shard_map/all_to_all | solution.py:298
  40.9 1.4 %collective-permute-start = (bf16[256,256]{1,0:T(8,128)(2,1)S(1)}, bf16[256,256]{1,0:T(8,128)(2,1)S(1)}, u32[]{:S(2)}, u32[]{:S(2)}) collective-permute-start(bf16[256,256]{1,0:T(8,128)(2,1)S(1)} %bitcast.35), channel_id=1, source_target_pairs={{0,1},{1,2},{2,3},{3,0},{4,5},{5,6},{6,7},{7,4},{8,9},{9,10},{10,1... | collective-permute-start | bytes 393224 | tf_op jit(solution)/shard_map/ppermute | solution.py:319
  42.3 1.5 %collective-permute-start.3 = (bf16[256,256]{1,0:T(8,128)(2,1)S(1)}, bf16[256,256]{1,0:T(8,128)(2,1)S(1)}, u32[]{:S(2)}, u32[]{:S(2)}) collective-permute-start(bf16[256,256]{1,0:T(8,128)(2,1)S(1)} %bitcast.38), channel_id=1, source_target_pairs={{0,3},{1,0},{2,1},{3,2},{4,7},{5,4},{6,5},{7,6},{8,11},{9,8},{10,9... | collective-permute-start | bytes 393224 | tf_op jit(solution)/shard_map/ppermute | solution.py:320
  43.8 2.7 %collective-permute-start.2 = (bf16[256,256]{1,0:T(8,128)(2,1)S(1)}, bf16[256,256]{1,0:T(8,128)(2,1)S(1)}, u32[]{:S(2)}, u32[]{:S(2)}) collective-permute-start(bf16[256,256]{1,0:T(8,128)(2,1)S(1)} %bitcast.36), channel_id=1, source_target_pairs={{0,3},{1,0},{2,1},{3,2},{4,7},{5,4},{6,5},{7,6},{8,11},{9,8},{10,9... | collective-permute-start | bytes 393224 | tf_op jit(solution)/shard_map/ppermute | solution.py:324
  46.5 0.5 collective-permute-done.refs_2_
  47.0 2.7 %collective-permute-start.5 = (bf16[256,256]{1,0:T(8,128)(2,1)S(1)}, bf16[256,256]{1,0:T(8,128)(2,1)S(1)}, u32[]{:S(2)}, u32[]{:S(2)}) collective-permute-start(bf16[256,256]{1,0:T(8,128)(2,1)S(1)} %collective-permute-done.3.refs_5_), channel_id=1, source_target_pairs={{0,3},{1,0},{2,1},{3,2},{4,7},{5,4},{6,5},{7,6},{8,11},{9,8},{10,9... | collective-permute-start | bytes 393224 | tf_op jit(solution)/shard_map/ppermute | solution.py:322
  49.7 0.7 copy-done.11
  50.4 0.1 copy.16.gain_ref
  50.5 1.8 %collective-permute-done.4.refs_6_ = bf16[256,256]{1,0:T(8,128)(2,1)S(1)} collective-permute-done((bf16[256,256]{1,0:T(8,128)(2,1)S(1)}, bf16[256,256]{1,0:T(8,128)(2,1)S(1)}, u32[]{:S(2)}, u32[]{:S(2)}) %collective-permute-start.4) | collective-permute-done | bytes 131104 | tf_op jit(solution)/shard_map/ppermute | solution.py:321
  52.3 5.9 %all-to-all-done.1 = bf16[64,8,512]{2,1,0:T(8,128)(2,1)S(1)} async-done(((bf16[64,8,512]{2,1,0:T(8,128)(2,1)}), bf16[64,8,512]{2,1,0:T(8,128)(2,1)S(1)}, u32[]{:S(2)}, u32[]{:S(2)}) %all-to-all-start.1) | async-done | bytes 524320 | tf_op jit(solution)/shard_map/all_to_all | solution.py:298
  58.2 3.2 %expert.1.after_ref = bf16[2176,128]{1,0:T(8,128)(2,1)} custom-call(bf16[512,512]{1,0:T(8,128)(2,1)S(1)} %bitcast.29, bf16[512,512]{1,0:T(8,128)(2,1)S(1)} %copy-done.8, f32[256,1]{1,0:T(8,128)S(1)} %copy.16.gain_ref, bf16[128,256]{1,0:T(8,128)(2,1)S(1)} %bitcast.32, bf16[256,256]{1,0:T(8,128)(2,1)S(1)} %bitcast.37, bf16[256,256]{1,0:T(8,128)(2,1)S(1)} %bitcast.40, ...), custom_call_target="tpu_custom_call" | custom-call | flops 1000000000 | bytes 1048576 | tf_op jit(solution)/shard_map/expert/pallas_call | solution.py:277
  61.5 6.4 %all-to-all-start.2 = ((bf16[64,17,2,128]{3,2,1,0:T(2,128)(2,1)}), bf16[64,17,2,128]{3,2,1,0:T(2,128)(2,1)S(1)}, u32[]{:S(2)}, u32[]{:S(2)}) async-start(bf16[64,17,2,128]{3,2,1,0:T(2,128)(2,1)} %bitcast.13), calls=%async_computation.2 | async-start | bytes 1114112 | tf_op jit(solution)/shard_map/all_to_all | solution.py:349
  68.0 0.7 copy-done.5
  68.6 1.2 %take.1 = (bf16[512,1024]{1,0:T(8,128)(2,1)S(1)}, bf16[512,128]{1,0:T(8,128)(2,1)S(1)}, f32[512,128]{1,0:T(8,128)S(1)}, f32[512,128]{1,0:T(8,128)S(1)}) custom-call(bf16[2176,128]{1,0:T(8,128)(2,1)} %expert.1.after_ref, s32[3,512]{1,0:T(4,128)S(1)} %bitcast.33, f32[3,16]{1,0:T(4,128)S(1)} %copy-done.6, f32[8,512]{1,0:T(8,128)S(1)} %copy-done.5), custom_call_target="tpu_custom_call" | custom-call | flops 2000000000 | bytes 1048576 | tf_op jit(solution)/shard_map/take/pallas_call | solution.py:277
  69.8 16.1 %all-to-all-done.2 = bf16[64,17,2,128]{3,2,1,0:T(2,128)(2,1)S(1)} async-done(((bf16[64,17,2,128]{3,2,1,0:T(2,128)(2,1)}), bf16[64,17,2,128]{3,2,1,0:T(2,128)(2,1)S(1)}, u32[]{:S(2)}, u32[]{:S(2)}) %all-to-all-start.2) | async-done | bytes 557088 | tf_op jit(solution)/shard_map/all_to_all | solution.py:349
  86.0 1.6 %final.1 = bf16[3,512,256]{2,1,0:T(8,128)(2,1)} custom-call(bf16[2176,128]{1,0:T(8,128)(2,1)S(1)} %bitcast.28, bf16[512,1024]{1,0:T(8,128)(2,1)S(1)} %get-tuple-element.19.take_ref, bf16[512,128]{1,0:T(8,128)(2,1)S(1)} %get-tuple-element.20.score_ref, f32[512,128]{1,0:T(8,128)S(1)} %get-tuple-element.21.lanes_ref, f32[512,128]{1,0:T(8,128)S(1)} %get-tuple-element.22.bias_ref), custom_call_target="tpu_custom_call" | custom-call | bytes 1048576 | tf_op jit(solution)/shard_map/final/pallas_call | solution.py:277
  (30 shorter events, 0.1 us)
Async XLA Ops:
  0.0 49.6 %copy-start = (bf16[3,256,64]{1,2,0:T(8,128)(2,1)S(1)}, bf16[3,256,64]{1,2,0:T(8,128)(2,1)}, u32[]{:S(2)}) copy-start(bf16[3,256,64]{1,2,0:T(8,128)(2,1)} %param.17) | copy-start | bytes 294916
  2.2 13.2 %copy-start.1 = (bf16[1536,128]{1,0:T(8,128)(2,1)S(1)}, bf16[1536,128]{1,0:T(8,128)(2,1)}, u32[]{:S(2)}) copy-start(bf16[1536,128]{1,0:T(8,128)(2,1)} %get-tuple-element.14.after_ref) | copy-start | bytes 1179652
  2.2 13.2 %copy-start.9 = (f32[4,128,128]{2,1,0:T(8,128)S(1)}, f32[4,128,128]{2,1,0:T(8,128)}, u32[]{:S(2)}) copy-start(f32[4,128,128]{2,1,0:T(8,128)} %constant.22.clone.turn_ref) | copy-start | bytes 786436
  2.2 27.7 %all-to-all-start = ((bf16[64,24,128]{2,1,0:T(8,128)(2,1)}), bf16[64,24,128]{2,1,0:T(8,128)(2,1)S(1)}, u32[]{:S(2)}, u32[]{:S(2)}) async-start(bf16[64,24,128]{2,1,0:T(8,128)(2,1)} %bitcast.31), calls=%async_computation | async-start | bytes 786432 | tf_op jit(solution)/shard_map/all_to_all | solution.py:298
  15.4 1.2 %copy-start.2 = (f32[2,32768,4]{1,2,0:T(4,128)S(1)}, f32[2,32768,4]{1,2,0:T(4,128)}, u32[]{:S(2)}) copy-start(f32[2,32768,4]{1,2,0:T(4,128)} %param.13) | copy-start | bytes 3145732
  16.6 1.1 %copy-start.7 = (bf16[1536,256]{1,0:T(8,128)(2,1)S(1)}, bf16[1536,256]{1,0:T(8,128)(2,1)}, u32[]{:S(2)}) copy-start(bf16[1536,256]{1,0:T(8,128)(2,1)} %constant.21.clone.factor_ref) | copy-start | bytes 2359300
  34.6 6.3 %copy-start.3 = (bf16[1,256,256]{2,1,0:T(8,128)(2,1)S(1)}, bf16[1,256,256]{2,1,0:T(8,128)(2,1)}, u32[]{:S(2)}) copy-start(bf16[1,256,256]{2,1,0:T(8,128)(2,1)} %param.15) | copy-start | bytes 393220
  34.6 7.7 %copy-start.4 = (bf16[1,256,256]{2,1,0:T(8,128)(2,1)S(1)}, bf16[1,256,256]{2,1,0:T(8,128)(2,1)}, u32[]{:S(2)}) copy-start(bf16[1,256,256]{2,1,0:T(8,128)(2,1)} %param.16) | copy-start | bytes 393220
  34.6 23.7 %copy-start.8 = (bf16[512,512]{1,0:T(8,128)(2,1)S(1)}, bf16[512,512]{1,0:T(8,128)(2,1)}, u32[]{:S(2)}) copy-start(bf16[512,512]{1,0:T(8,128)(2,1)} %constant.23.clone.lanes_ref) | copy-start | bytes 1572868
  34.6 23.7 %all-to-all-start.1 = ((bf16[64,8,512]{2,1,0:T(8,128)(2,1)}), bf16[64,8,512]{2,1,0:T(8,128)(2,1)S(1)}, u32[]{:S(2)}, u32[]{:S(2)}) async-start(bf16[64,8,512]{2,1,0:T(8,128)(2,1)} %bitcast.7), calls=%async_computation.1 | async-start | bytes 1048576 | tf_op jit(solution)/shard_map/all_to_all | solution.py:298
  40.9 6.0 %collective-permute-start = (bf16[256,256]{1,0:T(8,128)(2,1)S(1)}, bf16[256,256]{1,0:T(8,128)(2,1)S(1)}, u32[]{:S(2)}, u32[]{:S(2)}) collective-permute-start(bf16[256,256]{1,0:T(8,128)(2,1)S(1)} %bitcast.35), channel_id=1, source_target_pairs={{0,1},{1,2},{2,3},{3,0},{4,5},{5,6},{6,7},{7,4},{8,9},{9,10},{10,1... | collective-permute-start | bytes 393224 | tf_op jit(solution)/shard_map/ppermute | solution.py:319
  42.3 4.7 %collective-permute-start.3 = (bf16[256,256]{1,0:T(8,128)(2,1)S(1)}, bf16[256,256]{1,0:T(8,128)(2,1)S(1)}, u32[]{:S(2)}, u32[]{:S(2)}) collective-permute-start(bf16[256,256]{1,0:T(8,128)(2,1)S(1)} %bitcast.38), channel_id=1, source_target_pairs={{0,3},{1,0},{2,1},{3,2},{4,7},{5,4},{6,5},{7,6},{8,11},{9,8},{10,9... | collective-permute-start | bytes 393224 | tf_op jit(solution)/shard_map/ppermute | solution.py:320
  43.8 6.7 %collective-permute-start.1 = (bf16[256,256]{1,0:T(8,128)(2,1)S(1)}, bf16[256,256]{1,0:T(8,128)(2,1)S(1)}, u32[]{:S(2)}, u32[]{:S(2)}) collective-permute-start(bf16[256,256]{1,0:T(8,128)(2,1)S(1)} %bitcast.39), channel_id=1, source_target_pairs={{0,1},{1,2},{2,3},{3,0},{4,5},{5,6},{6,7},{7,4},{8,9},{9,10},{10,1... | collective-permute-start | bytes 393224 | tf_op jit(solution)/shard_map/ppermute | solution.py:323
  43.8 6.7 %collective-permute-start.2 = (bf16[256,256]{1,0:T(8,128)(2,1)S(1)}, bf16[256,256]{1,0:T(8,128)(2,1)S(1)}, u32[]{:S(2)}, u32[]{:S(2)}) collective-permute-start(bf16[256,256]{1,0:T(8,128)(2,1)S(1)} %bitcast.36), channel_id=1, source_target_pairs={{0,3},{1,0},{2,1},{3,2},{4,7},{5,4},{6,5},{7,6},{8,11},{9,8},{10,9... | collective-permute-start | bytes 393224 | tf_op jit(solution)/shard_map/ppermute | solution.py:324
  47.0 5.3 %collective-permute-start.4 = (bf16[256,256]{1,0:T(8,128)(2,1)S(1)}, bf16[256,256]{1,0:T(8,128)(2,1)S(1)}, u32[]{:S(2)}, u32[]{:S(2)}) collective-permute-start(bf16[256,256]{1,0:T(8,128)(2,1)S(1)} %collective-permute-done.refs_2_), channel_id=1, source_target_pairs={{0,1},{1,2},{2,3},{3,0},{4,5},{5,6},{6,7},{7,4},{8,9},{9,10},{10,1... | collective-permute-start | bytes 393224 | tf_op jit(solution)/shard_map/ppermute | solution.py:321
  47.0 5.3 %collective-permute-start.5 = (bf16[256,256]{1,0:T(8,128)(2,1)S(1)}, bf16[256,256]{1,0:T(8,128)(2,1)S(1)}, u32[]{:S(2)}, u32[]{:S(2)}) collective-permute-start(bf16[256,256]{1,0:T(8,128)(2,1)S(1)} %collective-permute-done.3.refs_5_), channel_id=1, source_target_pairs={{0,3},{1,0},{2,1},{3,2},{4,7},{5,4},{6,5},{7,6},{8,11},{9,8},{10,9... | collective-permute-start | bytes 393224 | tf_op jit(solution)/shard_map/ppermute | solution.py:322
  49.7 0.7 copy-start.11
  61.5 6.4 %copy-start.10 = (s32[1,512,1,3]{1,2,3,0:T(1,128)S(1)}, s32[1,512,1,3]{1,2,3,0:T(1,128)}, u32[]{:S(2)}) copy-start(s32[1,512,1,3]{1,2,3,0:T(1,128)} %param.20) | copy-start | bytes 18436
  61.5 6.5 %copy-start.6 = (f32[3,16]{1,0:T(4,128)S(1)}, f32[3,16]{1,0:T(4,128)}, u32[]{:S(2)}) copy-start(f32[3,16]{1,0:T(4,128)} %table_ref.1) | copy-start | bytes 580
  61.5 24.5 %all-to-all-start.2 = ((bf16[64,17,2,128]{3,2,1,0:T(2,128)(2,1)}), bf16[64,17,2,128]{3,2,1,0:T(2,128)(2,1)S(1)}, u32[]{:S(2)}, u32[]{:S(2)}) async-start(bf16[64,17,2,128]{3,2,1,0:T(2,128)(2,1)} %bitcast.13), calls=%async_computation.2 | async-start | bytes 1114112 | tf_op jit(solution)/shard_map/all_to_all | solution.py:349
  67.9 0.7 copy-start.5

commit v7 on v6

--- a/solution.py
+++ b/solution.py
@@ -211,7 +211,7 @@
         rows = total[block * 16 : (block + 1) * 16]
         full[block * 34 : block * 34 + 16, :] = rows[:, :128]
         full[block * 34 + 16 : block * 34 + 32, :] = rows[:, 128:]
-    scores = dot(normed, gate_ref[...], NT)
+    scores = dot(normed, jnp.concatenate([gate_ref[...]] * 8, 0), NT)
     own_lanes = lax.broadcasted_iota(jnp.int32, (1024, 128), 1) // 16 == (
         lax.broadcasted_iota(jnp.int32, (1024, 128), 0) % 8
     )
@@ -338,7 +338,7 @@
     slots_in = swap(sums, 8)
     me = lax.axis_index("seq")
     gate = lax.dynamic_index_in_dim(gate_weight.transpose(0, 2, 1), me, 1, keepdims=False)
-    gate = jnp.tile(jnp.pad(gate, ((0, 16 - TASKS), (0, 0))), (8, 1))
+    gate = jnp.pad(gate, ((0, 16 - TASKS), (0, 0)))
     slots_out = call(
         expert_kernel, shape((64 * 34, 128), BF16),
         slots_in, lanes, ln_gain.reshape(256, 1), gate,

time: 88.1 us -> 88.1 us (level)
  no operation moved by 1% of the time
where the time goes in v7:
time: 88.1 us; the launch traced here: 87.6 us
  waiting for transfers between devices  36.2 us (41%)
  starting transfers between devices  34.1 us (39%)
  Pallas kernels  13.2 us (15%)
  local copies, waits for them, and re-layouts  3.91 us (4%)
    all_to_all x2, starting transfers between devices, swap(): lax.all_to_all(chunks, 'seq', split_axis=0, concat_axis=0, tiled=True)  19.5 us
    all_to_all x2, waiting for transfers between devices, swap(): lax.all_to_all(chunks, 'seq', split_axis=0, concat_axis=0, tiled=True)  17.8 us
    all_to_all x1, waiting for transfers between devices, on_device(): lax.all_to_all(slots_out.reshape(64, 17, 2, 128), 'seq', split_axis=0, co...  16.1 us
    pallas_call x6, Pallas kernels, call(): pl.pallas_call(kernel, out_shape=outs, in_specs=specs, out_specs=[pl.Bloc...  13.2 us
    all_to_all x1, starting transfers between devices, on_device(): lax.all_to_all(slots_out.reshape(64, 17, 2, 128), 'seq', split_axis=0, co...  6.41 us
    unnamed x26, local copies, waits for them, and re-layouts  3.76 us
    ppermute x1, starting transfers between devices, on_device(): far_out = lax.ppermute(two_out, 'batch', behind)  2.67 us
    ppermute x1, starting transfers between devices, on_device(): two_in = lax.ppermute(own_in, 'batch', behind)  2.67 us
  transfers between devices with their start and end apart: 9, of which 5 were waited for; matrix products, arithmetic and copies ran while one was open for 0% of the time, Pallas kernels for 2%

profile of v7, /device:TPU:1, one launch (start us, length us, event | category | flops | bytes accessed | tf_op | source)
XLA Modules:
  0.0 87.6 jit_solution(11268205991748189069)
XLA Ops:
  0.0 2.2 %prep.1 = (bf16[1536,128]{1,0:T(8,128)(2,1)}, f32[8,512]{1,0:T(8,128)}) custom-call(bf16[512,256]{1,0:T(8,128)(2,1)} %bitcast.39, s32[1,512]{1,0:T(1,128)} %bitcast.41), custom_call_target="tpu_custom_call" | custom-call | bytes 1048576 | tf_op jit(solution)/shard_map/prep/pallas_call | solution.py:277
  2.2 0.0 copy-start.9
  2.2 13.1 %all-to-all-start = ((bf16[64,24,128]{2,1,0:T(8,128)(2,1)}), bf16[64,24,128]{2,1,0:T(8,128)(2,1)S(1)}, u32[]{:S(2)}, u32[]{:S(2)}) async-start(bf16[64,24,128]{2,1,0:T(8,128)(2,1)} %bitcast.30), calls=%async_computation | async-start | bytes 786432 | tf_op jit(solution)/shard_map/all_to_all | solution.py:298
  15.4 1.2 %copy-done.2 = f32[2,32768,4]{1,2,0:T(4,128)S(1)} copy-done((f32[2,32768,4]{1,2,0:T(4,128)S(1)}, f32[2,32768,4]{1,2,0:T(4,128)}, u32[]{:S(2)}) %copy-start.2) | copy-done | bytes 1048600
  16.6 1.1 %copy-done.7 = bf16[1536,256]{1,0:T(8,128)(2,1)S(1)} copy-done((bf16[1536,256]{1,0:T(8,128)(2,1)S(1)}, bf16[1536,256]{1,0:T(8,128)(2,1)}, u32[]{:S(2)}) %copy-start.7) | copy-done | bytes 786456
  17.7 0.4 ready.1
  18.1 11.9 %all-to-all-done = bf16[64,24,128]{2,1,0:T(8,128)(2,1)S(1)} async-done(((bf16[64,24,128]{2,1,0:T(8,128)(2,1)}), bf16[64,24,128]{2,1,0:T(8,128)(2,1)S(1)}, u32[]{:S(2)}, u32[]{:S(2)}) %all-to-all-start) | async-done | bytes 393248 | tf_op jit(solution)/shard_map/all_to_all | solution.py:298
  30.0 4.6 %filter.1 = bf16[512,512]{1,0:T(8,128)(2,1)} custom-call(bf16[1536,128]{1,0:T(8,128)(2,1)S(1)} %bitcast.29, f32[2,128,1024]{2,1,0:T(8,128)S(1)} %get-tuple-element.15.spec_ref, bf16[1536,256]{1,0:T(8,128)(2,1)S(1)} %get-tuple-element.16.factor_ref, f32[4,128,128]{2,1,0:T(8,128)S(1)} %get-tuple-element.17.turn_ref), custom_call_target="tpu_custom_call" | custom-call | flops 2000000000 | bytes 1048576 | tf_op jit(solution)/shard_map/filter/pallas_call | solution.py:277
  34.6 6.3 %all-to-all-start.1 = ((bf16[64,8,512]{2,1,0:T(8,128)(2,1)}), bf16[64,8,512]{2,1,0:T(8,128)(2,1)S(1)}, u32[]{:S(2)}, u32[]{:S(2)}) async-start(bf16[64,8,512]{2,1,0:T(8,128)(2,1)} %bitcast.7), calls=%async_computation.1 | async-start | bytes 1048576 | tf_op jit(solution)/shard_map/all_to_all | solution.py:298
  40.9 1.4 %collective-permute-start = (bf16[256,256]{1,0:T(8,128)(2,1)S(1)}, bf16[256,256]{1,0:T(8,128)(2,1)S(1)}, u32[]{:S(2)}, u32[]{:S(2)}) collective-permute-start(bf16[256,256]{1,0:T(8,128)(2,1)S(1)} %bitcast.33), channel_id=1, source_target_pairs={{0,1},{1,2},{2,3},{3,0},{4,5},{5,6},{6,7},{7,4},{8,9},{9,10},{10,1... | collective-permute-start | bytes 393224 | tf_op jit(solution)/shard_map/ppermute | solution.py:319
  42.3 1.5 %collective-permute-start.3 = (bf16[256,256]{1,0:T(8,128)(2,1)S(1)}, bf16[256,256]{1,0:T(8,128)(2,1)S(1)}, u32[]{:S(2)}, u32[]{:S(2)}) collective-permute-start(bf16[256,256]{1,0:T(8,128)(2,1)S(1)} %bitcast.36), channel_id=1, source_target_pairs={{0,3},{1,0},{2,1},{3,2},{4,7},{5,4},{6,5},{7,6},{8,11},{9,8},{10,9... | collective-permute-start | bytes 393224 | tf_op jit(solution)/shard_map/ppermute | solution.py:320
  43.8 2.7 %collective-permute-start.2 = (bf16[256,256]{1,0:T(8,128)(2,1)S(1)}, bf16[256,256]{1,0:T(8,128)(2,1)S(1)}, u32[]{:S(2)}, u32[]{:S(2)}) collective-permute-start(bf16[256,256]{1,0:T(8,128)(2,1)S(1)} %bitcast.34), channel_id=1, source_target_pairs={{0,3},{1,0},{2,1},{3,2},{4,7},{5,4},{6,5},{7,6},{8,11},{9,8},{10,9... | collective-permute-start | bytes 393224 | tf_op jit(solution)/shard_map/ppermute | solution.py:324
  46.5 0.5 collective-permute-done.refs_2_
  47.0 2.7 %collective-permute-start.5 = (bf16[256,256]{1,0:T(8,128)(2,1)S(1)}, bf16[256,256]{1,0:T(8,128)(2,1)S(1)}, u32[]{:S(2)}, u32[]{:S(2)}) collective-permute-start(bf16[256,256]{1,0:T(8,128)(2,1)S(1)} %collective-permute-done.3.refs_5_), channel_id=1, source_target_pairs={{0,3},{1,0},{2,1},{3,2},{4,7},{5,4},{6,5},{7,6},{8,11},{9,8},{10,9... | collective-permute-start | bytes 393224 | tf_op jit(solution)/shard_map/ppermute | solution.py:322
  49.7 0.7 copy-done.11
  50.4 0.1 copy.16.gain_ref
  50.5 1.8 %collective-permute-done.4.refs_6_ = bf16[256,256]{1,0:T(8,128)(2,1)S(1)} collective-permute-done((bf16[256,256]{1,0:T(8,128)(2,1)S(1)}, bf16[256,256]{1,0:T(8,128)(2,1)S(1)}, u32[]{:S(2)}, u32[]{:S(2)}) %collective-permute-start.4) | collective-permute-done | bytes 131104 | tf_op jit(solution)/shard_map/ppermute | solution.py:321
  52.3 5.9 %all-to-all-done.1 = bf16[64,8,512]{2,1,0:T(8,128)(2,1)S(1)} async-done(((bf16[64,8,512]{2,1,0:T(8,128)(2,1)}), bf16[64,8,512]{2,1,0:T(8,128)(2,1)S(1)}, u32[]{:S(2)}, u32[]{:S(2)}) %all-to-all-start.1) | async-done | bytes 524320 | tf_op jit(solution)/shard_map/all_to_all | solution.py:298
  58.2 3.3 %expert.1.after_ref = bf16[2176,128]{1,0:T(8,128)(2,1)} custom-call(bf16[512,512]{1,0:T(8,128)(2,1)S(1)} %bitcast.28, bf16[512,512]{1,0:T(8,128)(2,1)S(1)} %copy-done.8, f32[256,1]{1,0:T(8,128)S(1)} %copy.16.gain_ref, bf16[16,256]{1,0:T(8,128)(2,1)S(1)} %pad.4.gate_ref, bf16[256,256]{1,0:T(8,128)(2,1)S(1)} %bitcast.35, bf16[256,256]{1,0:T(8,128)(2,1)S(1)} %bitcast.38, ...), custom_call_target="tpu_custom_call" | custom-call | flops 1000000000 | bytes 1048576 | tf_op jit(solution)/shard_map/expert/pallas_call | solution.py:277
  61.5 6.4 %all-to-all-start.2 = ((bf16[64,17,2,128]{3,2,1,0:T(2,128)(2,1)}), bf16[64,17,2,128]{3,2,1,0:T(2,128)(2,1)S(1)}, u32[]{:S(2)}, u32[]{:S(2)}) async-start(bf16[64,17,2,128]{3,2,1,0:T(2,128)(2,1)} %bitcast.12), calls=%async_computation.2 | async-start | bytes 1114112 | tf_op jit(solution)/shard_map/all_to_all | solution.py:349
  68.0 0.7 copy-done.5
  68.7 1.2 %take.1 = (bf16[512,1024]{1,0:T(8,128)(2,1)S(1)}, bf16[512,128]{1,0:T(8,128)(2,1)S(1)}, f32[512,128]{1,0:T(8,128)S(1)}, f32[512,128]{1,0:T(8,128)S(1)}) custom-call(bf16[2176,128]{1,0:T(8,128)(2,1)} %expert.1.after_ref, s32[3,512]{1,0:T(4,128)S(1)} %bitcast.31, f32[3,16]{1,0:T(4,128)S(1)} %copy-done.6, f32[8,512]{1,0:T(8,128)S(1)} %copy-done.5), custom_call_target="tpu_custom_call" | custom-call | flops 2000000000 | bytes 1048576 | tf_op jit(solution)/shard_map/take/pallas_call | solution.py:277
  69.8 16.1 %all-to-all-done.2 = bf16[64,17,2,128]{3,2,1,0:T(2,128)(2,1)S(1)} async-done(((bf16[64,17,2,128]{3,2,1,0:T(2,128)(2,1)}), bf16[64,17,2,128]{3,2,1,0:T(2,128)(2,1)S(1)}, u32[]{:S(2)}, u32[]{:S(2)}) %all-to-all-start.2) | async-done | bytes 557088 | tf_op jit(solution)/shard_map/all_to_all | solution.py:349
  86.0 1.6 %final.1 = bf16[3,512,256]{2,1,0:T(8,128)(2,1)} custom-call(bf16[2176,128]{1,0:T(8,128)(2,1)S(1)} %bitcast.27, bf16[512,1024]{1,0:T(8,128)(2,1)S(1)} %get-tuple-element.19.take_ref, bf16[512,128]{1,0:T(8,128)(2,1)S(1)} %get-tuple-element.20.score_ref, f32[512,128]{1,0:T(8,128)S(1)} %get-tuple-element.21.lanes_ref, f32[512,128]{1,0:T(8,128)S(1)} %get-tuple-element.22.bias_ref), custom_call_target="tpu_custom_call" | custom-call | bytes 1048576 | tf_op jit(solution)/shard_map/final/pallas_call | solution.py:277
  (29 shorter events, 0.1 us)
Async XLA Ops:
  0.0 49.6 %copy-start = (bf16[3,256,64]{1,2,0:T(8,128)(2,1)S(1)}, bf16[3,256,64]{1,2,0:T(8,128)(2,1)}, u32[]{:S(2)}) copy-start(bf16[3,256,64]{1,2,0:T(8,128)(2,1)} %param.17) | copy-start | bytes 294916
  2.2 13.2 %copy-start.1 = (bf16[1536,128]{1,0:T(8,128)(2,1)S(1)}, bf16[1536,128]{1,0:T(8,128)(2,1)}, u32[]{:S(2)}) copy-start(bf16[1536,128]{1,0:T(8,128)(2,1)} %get-tuple-element.14.after_ref) | copy-start | bytes 1179652
  2.2 13.2 %copy-start.9 = (f32[4,128,128]{2,1,0:T(8,128)S(1)}, f32[4,128,128]{2,1,0:T(8,128)}, u32[]{:S(2)}) copy-start(f32[4,128,128]{2,1,0:T(8,128)} %constant.22.clone.turn_ref) | copy-start | bytes 786436
  2.2 27.7 %all-to-all-start = ((bf16[64,24,128]{2,1,0:T(8,128)(2,1)}), bf16[64,24,128]{2,1,0:T(8,128)(2,1)S(1)}, u32[]{:S(2)}, u32[]{:S(2)}) async-start(bf16[64,24,128]{2,1,0:T(8,128)(2,1)} %bitcast.30), calls=%async_computation | async-start | bytes 786432 | tf_op jit(solution)/shard_map/all_to_all | solution.py:298
  15.4 1.2 %copy-start.2 = (f32[2,32768,4]{1,2,0:T(4,128)S(1)}, f32[2,32768,4]{1,2,0:T(4,128)}, u32[]{:S(2)}) copy-start(f32[2,32768,4]{1,2,0:T(4,128)} %param.13) | copy-start | bytes 3145732
  16.6 1.1 %copy-start.7 = (bf16[1536,256]{1,0:T(8,128)(2,1)S(1)}, bf16[1536,256]{1,0:T(8,128)(2,1)}, u32[]{:S(2)}) copy-start(bf16[1536,256]{1,0:T(8,128)(2,1)} %constant.21.clone.factor_ref) | copy-start | bytes 2359300
  34.6 6.3 %copy-start.3 = (bf16[1,256,256]{2,1,0:T(8,128)(2,1)S(1)}, bf16[1,256,256]{2,1,0:T(8,128)(2,1)}, u32[]{:S(2)}) copy-start(bf16[1,256,256]{2,1,0:T(8,128)(2,1)} %param.15) | copy-start | bytes 393220
  34.6 7.7 %copy-start.4 = (bf16[1,256,256]{2,1,0:T(8,128)(2,1)S(1)}, bf16[1,256,256]{2,1,0:T(8,128)(2,1)}, u32[]{:S(2)}) copy-start(bf16[1,256,256]{2,1,0:T(8,128)(2,1)} %param.16) | copy-start | bytes 393220
  34.6 23.7 %copy-start.8 = (bf16[512,512]{1,0:T(8,128)(2,1)S(1)}, bf16[512,512]{1,0:T(8,128)(2,1)}, u32[]{:S(2)}) copy-start(bf16[512,512]{1,0:T(8,128)(2,1)} %constant.23.clone.lanes_ref) | copy-start | bytes 1572868
  34.6 23.7 %all-to-all-start.1 = ((bf16[64,8,512]{2,1,0:T(8,128)(2,1)}), bf16[64,8,512]{2,1,0:T(8,128)(2,1)S(1)}, u32[]{:S(2)}, u32[]{:S(2)}) async-start(bf16[64,8,512]{2,1,0:T(8,128)(2,1)} %bitcast.7), calls=%async_computation.1 | async-start | bytes 1048576 | tf_op jit(solution)/shard_map/all_to_all | solution.py:298
  40.9 6.0 %collective-permute-start = (bf16[256,256]{1,0:T(8,128)(2,1)S(1)}, bf16[256,256]{1,0:T(8,128)(2,1)S(1)}, u32[]{:S(2)}, u32[]{:S(2)}) collective-permute-start(bf16[256,256]{1,0:T(8,128)(2,1)S(1)} %bitcast.33), channel_id=1, source_target_pairs={{0,1},{1,2},{2,3},{3,0},{4,5},{5,6},{6,7},{7,4},{8,9},{9,10},{10,1... | collective-permute-start | bytes 393224 | tf_op jit(solution)/shard_map/ppermute | solution.py:319
  42.3 4.7 %collective-permute-start.3 = (bf16[256,256]{1,0:T(8,128)(2,1)S(1)}, bf16[256,256]{1,0:T(8,128)(2,1)S(1)}, u32[]{:S(2)}, u32[]{:S(2)}) collective-permute-start(bf16[256,256]{1,0:T(8,128)(2,1)S(1)} %bitcast.36), channel_id=1, source_target_pairs={{0,3},{1,0},{2,1},{3,2},{4,7},{5,4},{6,5},{7,6},{8,11},{9,8},{10,9... | collective-permute-start | bytes 393224 | tf_op jit(solution)/shard_map/ppermute | solution.py:320
  43.8 6.7 %collective-permute-start.1 = (bf16[256,256]{1,0:T(8,128)(2,1)S(1)}, bf16[256,256]{1,0:T(8,128)(2,1)S(1)}, u32[]{:S(2)}, u32[]{:S(2)}) collective-permute-start(bf16[256,256]{1,0:T(8,128)(2,1)S(1)} %bitcast.37), channel_id=1, source_target_pairs={{0,1},{1,2},{2,3},{3,0},{4,5},{5,6},{6,7},{7,4},{8,9},{9,10},{10,1... | collective-permute-start | bytes 393224 | tf_op jit(solution)/shard_map/ppermute | solution.py:323
  43.8 6.7 %collective-permute-start.2 = (bf16[256,256]{1,0:T(8,128)(2,1)S(1)}, bf16[256,256]{1,0:T(8,128)(2,1)S(1)}, u32[]{:S(2)}, u32[]{:S(2)}) collective-permute-start(bf16[256,256]{1,0:T(8,128)(2,1)S(1)} %bitcast.34), channel_id=1, source_target_pairs={{0,3},{1,0},{2,1},{3,2},{4,7},{5,4},{6,5},{7,6},{8,11},{9,8},{10,9... | collective-permute-start | bytes 393224 | tf_op jit(solution)/shard_map/ppermute | solution.py:324
  47.0 5.3 %collective-permute-start.4 = (bf16[256,256]{1,0:T(8,128)(2,1)S(1)}, bf16[256,256]{1,0:T(8,128)(2,1)S(1)}, u32[]{:S(2)}, u32[]{:S(2)}) collective-permute-start(bf16[256,256]{1,0:T(8,128)(2,1)S(1)} %collective-permute-done.refs_2_), channel_id=1, source_target_pairs={{0,1},{1,2},{2,3},{3,0},{4,5},{5,6},{6,7},{7,4},{8,9},{9,10},{10,1... | collective-permute-start | bytes 393224 | tf_op jit(solution)/shard_map/ppermute | solution.py:321
  47.0 5.3 %collective-permute-start.5 = (bf16[256,256]{1,0:T(8,128)(2,1)S(1)}, bf16[256,256]{1,0:T(8,128)(2,1)S(1)}, u32[]{:S(2)}, u32[]{:S(2)}) collective-permute-start(bf16[256,256]{1,0:T(8,128)(2,1)S(1)} %collective-permute-done.3.refs_5_), channel_id=1, source_target_pairs={{0,3},{1,0},{2,1},{3,2},{4,7},{5,4},{6,5},{7,6},{8,11},{9,8},{10,9... | collective-permute-start | bytes 393224 | tf_op jit(solution)/shard_map/ppermute | solution.py:322
  49.7 0.7 copy-start.11
  61.5 6.4 %copy-start.10 = (s32[1,512,1,3]{1,2,3,0:T(1,128)S(1)}, s32[1,512,1,3]{1,2,3,0:T(1,128)}, u32[]{:S(2)}) copy-start(s32[1,512,1,3]{1,2,3,0:T(1,128)} %param.20) | copy-start | bytes 18436
  61.5 6.5 %copy-start.6 = (f32[3,16]{1,0:T(4,128)S(1)}, f32[3,16]{1,0:T(4,128)}, u32[]{:S(2)}) copy-start(f32[3,16]{1,0:T(4,128)} %table_ref.1) | copy-start | bytes 580
  61.5 24.5 %all-to-all-start.2 = ((bf16[64,17,2,128]{3,2,1,0:T(2,128)(2,1)}), bf16[64,17,2,128]{3,2,1,0:T(2,128)(2,1)S(1)}, u32[]{:S(2)}, u32[]{:S(2)}) async-start(bf16[64,17,2,128]{3,2,1,0:T(2,128)(2,1)} %bitcast.12), calls=%async_computation.2 | async-start | bytes 1114112 | tf_op jit(solution)/shard_map/all_to_all | solution.py:349
  67.9 0.7 copy-start.5

commit v8 on v7

--- a/solution.py
+++ b/solution.py
@@ -327,7 +327,7 @@
     spec, factors, turns = call(
         ready_kernel,
         [shape((2, 128, 1024), F32), shape(factors.shape, BF16), shape(turns.shape, F32)],
-        chunks, spec, factors, turns, far=(0, 1, 2, 3), name="ready",
+        slot, spec, factors, turns, far=(0, 1, 2, 3), name="ready",
         scratch=[big((2, 1024, 128), F32), pltpu.SemaphoreType.DMA((3,))], flops=2 * 10**9,
     )
     sums = call(

time: 88.1 us -> 89 us (1.010)
  local copies, waits for them, and re-layouts: 3.91 us -> 5.96 us
  waiting for transfers between devices: 36.2 us -> 35 us
    unnamed x26 -> x30, local copies, waits for them, and re-layouts: 3.76 us -> 5.81 us
    all_to_all x2, waiting for transfers between devices: 17.8 us -> 16.7 us  [swap(): lax.all_to_all(chunks, 'seq', split_axis=0, concat_axis=0, tiled=True)]
where the time goes in v8:
time: 89 us; the launch traced here: 88.4 us
  waiting for transfers between devices  35 us (39%)
  starting transfers between devices  34 us (38%)
  Pallas kernels  13.2 us (15%)
  local copies, waits for them, and re-layouts  5.96 us (7%)
    all_to_all x2, starting transfers between devices, swap(): lax.all_to_all(chunks, 'seq', split_axis=0, concat_axis=0, tiled=True)  19.3 us
    all_to_all x2, waiting for transfers between devices, swap(): lax.all_to_all(chunks, 'seq', split_axis=0, concat_axis=0, tiled=True)  16.7 us
    all_to_all x1, waiting for transfers between devices, on_device(): lax.all_to_all(slots_out.reshape(64, 17, 2, 128), 'seq', split_axis=0, co...  16.2 us
    pallas_call x6, Pallas kernels, call(): pl.pallas_call(kernel, out_shape=outs, in_specs=specs, out_specs=[pl.Bloc...  13.2 us
    all_to_all x1, starting transfers between devices, on_device(): lax.all_to_all(slots_out.reshape(64, 17, 2, 128), 'seq', split_axis=0, co...  6.41 us
    unnamed x30, local copies, waits for them, and re-layouts  5.81 us
    ppermute x1, starting transfers between devices, on_device(): far_out = lax.ppermute(two_out, 'batch', behind)  2.67 us
    ppermute x1, starting transfers between devices, on_device(): two_in = lax.ppermute(own_in, 'batch', behind)  2.67 us
  transfers between devices with their start and end apart: 9, of which 5 were waited for; matrix products, arithmetic and copies ran while one was open for 0% of the time, Pallas kernels for 2%

profile of v8, /device:TPU:1, one launch (start us, length us, event | category | flops | bytes accessed | tf_op | source)
XLA Modules:
  0.0 88.4 jit_solution(24403119478913482)
XLA Ops:
  0.0 2.3 %prep.1 = (bf16[1536,128]{1,0:T(8,128)(2,1)}, f32[8,512]{1,0:T(8,128)}) custom-call(bf16[512,256]{1,0:T(8,128)(2,1)} %bitcast.39, s32[1,512]{1,0:T(1,128)} %bitcast.41), custom_call_target="tpu_custom_call" | custom-call | bytes 1048576 | tf_op jit(solution)/shard_map/prep/pallas_call | solution.py:277
  2.3 13.0 %all-to-all-start = ((bf16[64,24,128]{2,1,0:T(8,128)(2,1)}), bf16[64,24,128]{2,1,0:T(8,128)(2,1)S(1)}, u32[]{:S(2)}, u32[]{:S(2)}) async-start(bf16[64,24,128]{2,1,0:T(8,128)(2,1)} %bitcast.38), calls=%async_computation | async-start | bytes 786432 | tf_op jit(solution)/shard_map/all_to_all | solution.py:298
  15.3 0.7 copy-done.4
  16.0 1.1 %copy-done.7 = bf16[1536,256]{1,0:T(8,128)(2,1)S(1)} copy-done((bf16[1536,256]{1,0:T(8,128)(2,1)S(1)}, bf16[1536,256]{1,0:T(8,128)(2,1)}, u32[]{:S(2)}) %copy-start.7) | copy-done | bytes 786456
  17.1 0.9 %copy-done.9 = f32[4,128,128]{2,1,0:T(8,128)S(1)} copy-done((f32[4,128,128]{2,1,0:T(8,128)S(1)}, f32[4,128,128]{2,1,0:T(8,128)}, u32[]{:S(2)}) %copy-start.9) | copy-done | bytes 262168
  18.5 0.7 copy-done.10
  19.2 10.7 %all-to-all-done = bf16[64,24,128]{2,1,0:T(8,128)(2,1)S(1)} async-done(((bf16[64,24,128]{2,1,0:T(8,128)(2,1)}), bf16[64,24,128]{2,1,0:T(8,128)(2,1)S(1)}, u32[]{:S(2)}, u32[]{:S(2)}) %all-to-all-start) | async-done | bytes 393248 | tf_op jit(solution)/shard_map/all_to_all | solution.py:298
  29.9 0.9 %copy-done.11 = f32[4,128,128]{2,1,0:T(8,128)S(1)} copy-done((f32[4,128,128]{2,1,0:T(8,128)S(1)}, f32[4,128,128]{2,1,0:T(8,128)}, u32[]{:S(2)}) %copy-start.11) | copy-done | bytes 262168
  30.8 4.6 %filter.1 = bf16[512,512]{1,0:T(8,128)(2,1)} custom-call(bf16[1536,128]{1,0:T(8,128)(2,1)S(1)} %bitcast.29, f32[2,128,1024]{2,1,0:T(8,128)S(1)} %get-tuple-element.16.spec_ref, bf16[1536,256]{1,0:T(8,128)(2,1)S(1)} %get-tuple-element.17.factor_ref, f32[4,128,128]{2,1,0:T(8,128)S(1)} %copy-done.11), custom_call_target="tpu_custom_call" | custom-call | flops 2000000000 | bytes 1048576 | tf_op jit(solution)/shard_map/filter/pallas_call | solution.py:277
  35.4 6.3 %all-to-all-start.1 = ((bf16[64,8,512]{2,1,0:T(8,128)(2,1)}), bf16[64,8,512]{2,1,0:T(8,128)(2,1)S(1)}, u32[]{:S(2)}, u32[]{:S(2)}) async-start(bf16[64,8,512]{2,1,0:T(8,128)(2,1)} %bitcast.7), calls=%async_computation.1 | async-start | bytes 1048576 | tf_op jit(solution)/shard_map/all_to_all | solution.py:298
  41.8 1.4 %collective-permute-start = (bf16[256,256]{1,0:T(8,128)(2,1)S(1)}, bf16[256,256]{1,0:T(8,128)(2,1)S(1)}, u32[]{:S(2)}, u32[]{:S(2)}) collective-permute-start(bf16[256,256]{1,0:T(8,128)(2,1)S(1)} %bitcast.32), channel_id=1, source_target_pairs={{0,1},{1,2},{2,3},{3,0},{4,5},{5,6},{6,7},{7,4},{8,9},{9,10},{10,1... | collective-permute-start | bytes 393224 | tf_op jit(solution)/shard_map/ppermute | solution.py:319
  43.2 1.5 %collective-permute-start.3 = (bf16[256,256]{1,0:T(8,128)(2,1)S(1)}, bf16[256,256]{1,0:T(8,128)(2,1)S(1)}, u32[]{:S(2)}, u32[]{:S(2)}) collective-permute-start(bf16[256,256]{1,0:T(8,128)(2,1)S(1)} %bitcast.35), channel_id=1, source_target_pairs={{0,3},{1,0},{2,1},{3,2},{4,7},{5,4},{6,5},{7,6},{8,11},{9,8},{10,9... | collective-permute-start | bytes 393224 | tf_op jit(solution)/shard_map/ppermute | solution.py:320
  44.7 2.7 %collective-permute-start.2 = (bf16[256,256]{1,0:T(8,128)(2,1)S(1)}, bf16[256,256]{1,0:T(8,128)(2,1)S(1)}, u32[]{:S(2)}, u32[]{:S(2)}) collective-permute-start(bf16[256,256]{1,0:T(8,128)(2,1)S(1)} %bitcast.33), channel_id=1, source_target_pairs={{0,3},{1,0},{2,1},{3,2},{4,7},{5,4},{6,5},{7,6},{8,11},{9,8},{10,9... | collective-permute-start | bytes 393224 | tf_op jit(solution)/shard_map/ppermute | solution.py:324
  47.4 0.5 collective-permute-done.refs_2_
  47.8 2.7 %collective-permute-start.5 = (bf16[256,256]{1,0:T(8,128)(2,1)S(1)}, bf16[256,256]{1,0:T(8,128)(2,1)S(1)}, u32[]{:S(2)}, u32[]{:S(2)}) collective-permute-start(bf16[256,256]{1,0:T(8,128)(2,1)S(1)} %collective-permute-done.3.refs_5_), channel_id=1, source_target_pairs={{0,3},{1,0},{2,1},{3,2},{4,7},{5,4},{6,5},{7,6},{8,11},{9,8},{10,9... | collective-permute-start | bytes 393224 | tf_op jit(solution)/shard_map/ppermute | solution.py:322
  50.5 0.7 copy-done.13
  51.4 1.8 %collective-permute-done.4.refs_6_ = bf16[256,256]{1,0:T(8,128)(2,1)S(1)} collective-permute-done((bf16[256,256]{1,0:T(8,128)(2,1)S(1)}, bf16[256,256]{1,0:T(8,128)(2,1)S(1)}, u32[]{:S(2)}, u32[]{:S(2)}) %collective-permute-start.4) | collective-permute-done | bytes 131104 | tf_op jit(solution)/shard_map/ppermute | solution.py:321
  53.1 5.9 %all-to-all-done.1 = bf16[64,8,512]{2,1,0:T(8,128)(2,1)S(1)} async-done(((bf16[64,8,512]{2,1,0:T(8,128)(2,1)}), bf16[64,8,512]{2,1,0:T(8,128)(2,1)S(1)}, u32[]{:S(2)}, u32[]{:S(2)}) %all-to-all-start.1) | async-done | bytes 524320 | tf_op jit(solution)/shard_map/all_to_all | solution.py:298
  59.1 3.2 %expert.1.after_ref = bf16[2176,128]{1,0:T(8,128)(2,1)} custom-call(bf16[512,512]{1,0:T(8,128)(2,1)S(1)} %bitcast.28, bf16[512,512]{1,0:T(8,128)(2,1)S(1)} %copy-done.8, f32[256,1]{1,0:T(8,128)S(1)} %copy.16.gain_ref, bf16[16,256]{1,0:T(8,128)(2,1)S(1)} %pad.4.gate_ref, bf16[256,256]{1,0:T(8,128)(2,1)S(1)} %bitcast.34, bf16[256,256]{1,0:T(8,128)(2,1)S(1)} %bitcast.37, ...), custom_call_target="tpu_custom_call" | custom-call | flops 1000000000 | bytes 1048576 | tf_op jit(solution)/shard_map/expert/pallas_call | solution.py:277
  62.3 6.4 %all-to-all-start.2 = ((bf16[64,17,2,128]{3,2,1,0:T(2,128)(2,1)}), bf16[64,17,2,128]{3,2,1,0:T(2,128)(2,1)S(1)}, u32[]{:S(2)}, u32[]{:S(2)}) async-start(bf16[64,17,2,128]{3,2,1,0:T(2,128)(2,1)} %bitcast.12), calls=%async_computation.2 | async-start | bytes 1114112 | tf_op jit(solution)/shard_map/all_to_all | solution.py:349
  68.8 0.7 copy-done.6
  69.4 1.2 %take.1 = (bf16[512,1024]{1,0:T(8,128)(2,1)S(1)}, bf16[512,128]{1,0:T(8,128)(2,1)S(1)}, f32[512,128]{1,0:T(8,128)S(1)}, f32[512,128]{1,0:T(8,128)S(1)}) custom-call(bf16[2176,128]{1,0:T(8,128)(2,1)} %expert.1.after_ref, s32[3,512]{1,0:T(4,128)S(1)} %bitcast.30, f32[3,16]{1,0:T(4,128)S(1)} %copy-done.6, f32[8,512]{1,0:T(8,128)S(1)} %copy-done.5), custom_call_target="tpu_custom_call" | custom-call | flops 2000000000 | bytes 1048576 | tf_op jit(solution)/shard_map/take/pallas_call | solution.py:277
  70.6 16.2 %all-to-all-done.2 = bf16[64,17,2,128]{3,2,1,0:T(2,128)(2,1)S(1)} async-done(((bf16[64,17,2,128]{3,2,1,0:T(2,128)(2,1)}), bf16[64,17,2,128]{3,2,1,0:T(2,128)(2,1)S(1)}, u32[]{:S(2)}, u32[]{:S(2)}) %all-to-all-start.2) | async-done | bytes 557088 | tf_op jit(solution)/shard_map/all_to_all | solution.py:349
  86.8 1.6 %final.1 = bf16[3,512,256]{2,1,0:T(8,128)(2,1)} custom-call(bf16[2176,128]{1,0:T(8,128)(2,1)S(1)} %bitcast.27, bf16[512,1024]{1,0:T(8,128)(2,1)S(1)} %get-tuple-element.19.take_ref, bf16[512,128]{1,0:T(8,128)(2,1)S(1)} %get-tuple-element.20.score_ref, f32[512,128]{1,0:T(8,128)S(1)} %get-tuple-element.21.lanes_ref, f32[512,128]{1,0:T(8,128)S(1)} %get-tuple-element.22.bias_ref), custom_call_target="tpu_custom_call" | custom-call | bytes 1048576 | tf_op jit(solution)/shard_map/final/pallas_call | solution.py:277
  (33 shorter events, 0.6 us)
Async XLA Ops:
  0.0 50.5 %copy-start = (bf16[3,256,64]{1,2,0:T(8,128)(2,1)S(1)}, bf16[3,256,64]{1,2,0:T(8,128)(2,1)}, u32[]{:S(2)}) copy-start(bf16[3,256,64]{1,2,0:T(8,128)(2,1)} %param.17) | copy-start | bytes 294916
  0.0 15.3 %copy-start.1 = (f32[2,32768,4]{1,2,0:T(4,128)S(1)}, f32[2,32768,4]{1,2,0:T(4,128)}, u32[]{:S(2)}) copy-start(f32[2,32768,4]{1,2,0:T(4,128)} %param.13) | copy-start | bytes 3145732
  2.3 27.6 %all-to-all-start = ((bf16[64,24,128]{2,1,0:T(8,128)(2,1)}), bf16[64,24,128]{2,1,0:T(8,128)(2,1)S(1)}, u32[]{:S(2)}, u32[]{:S(2)}) async-start(bf16[64,24,128]{2,1,0:T(8,128)(2,1)} %bitcast.38), calls=%async_computation | async-start | bytes 786432 | tf_op jit(solution)/shard_map/all_to_all | solution.py:298
  15.3 0.7 copy-start.4
  16.0 1.1 %copy-start.7 = (bf16[1536,256]{1,0:T(8,128)(2,1)S(1)}, bf16[1536,256]{1,0:T(8,128)(2,1)}, u32[]{:S(2)}) copy-start(bf16[1536,256]{1,0:T(8,128)(2,1)} %constant.21.clone.factor_ref) | copy-start | bytes 2359300
  17.1 0.9 %copy-start.9 = (f32[4,128,128]{2,1,0:T(8,128)S(1)}, f32[4,128,128]{2,1,0:T(8,128)}, u32[]{:S(2)}) copy-start(f32[4,128,128]{2,1,0:T(8,128)} %constant.22.clone.turn_ref) | copy-start | bytes 786436
  18.4 0.7 copy-start.10
  29.9 1.0 %copy-start.11 = (f32[4,128,128]{2,1,0:T(8,128)S(1)}, f32[4,128,128]{2,1,0:T(8,128)}, u32[]{:S(2)}) copy-start(f32[4,128,128]{2,1,0:T(8,128)} %copy-done.10) | copy-start | bytes 786436
  35.4 6.4 %copy-start.2 = (bf16[1,256,256]{2,1,0:T(8,128)(2,1)S(1)}, bf16[1,256,256]{2,1,0:T(8,128)(2,1)}, u32[]{:S(2)}) copy-start(bf16[1,256,256]{2,1,0:T(8,128)(2,1)} %param.15) | copy-start | bytes 393220
  35.4 7.7 %copy-start.3 = (bf16[1,256,256]{2,1,0:T(8,128)(2,1)S(1)}, bf16[1,256,256]{2,1,0:T(8,128)(2,1)}, u32[]{:S(2)}) copy-start(bf16[1,256,256]{2,1,0:T(8,128)(2,1)} %param.16) | copy-start | bytes 393220
  35.4 23.7 %copy-start.8 = (bf16[512,512]{1,0:T(8,128)(2,1)S(1)}, bf16[512,512]{1,0:T(8,128)(2,1)}, u32[]{:S(2)}) copy-start(bf16[512,512]{1,0:T(8,128)(2,1)} %constant.23.clone.lanes_ref) | copy-start | bytes 1572868
  35.4 23.7 %all-to-all-start.1 = ((bf16[64,8,512]{2,1,0:T(8,128)(2,1)}), bf16[64,8,512]{2,1,0:T(8,128)(2,1)S(1)}, u32[]{:S(2)}, u32[]{:S(2)}) async-start(bf16[64,8,512]{2,1,0:T(8,128)(2,1)} %bitcast.7), calls=%async_computation.1 | async-start | bytes 1048576 | tf_op jit(solution)/shard_map/all_to_all | solution.py:298
  41.8 6.0 %collective-permute-start = (bf16[256,256]{1,0:T(8,128)(2,1)S(1)}, bf16[256,256]{1,0:T(8,128)(2,1)S(1)}, u32[]{:S(2)}, u32[]{:S(2)}) collective-permute-start(bf16[256,256]{1,0:T(8,128)(2,1)S(1)} %bitcast.32), channel_id=1, source_target_pairs={{0,1},{1,2},{2,3},{3,0},{4,5},{5,6},{6,7},{7,4},{8,9},{9,10},{10,1... | collective-permute-start | bytes 393224 | tf_op jit(solution)/shard_map/ppermute | solution.py:319
  43.2 4.7 %collective-permute-start.3 = (bf16[256,256]{1,0:T(8,128)(2,1)S(1)}, bf16[256,256]{1,0:T(8,128)(2,1)S(1)}, u32[]{:S(2)}, u32[]{:S(2)}) collective-permute-start(bf16[256,256]{1,0:T(8,128)(2,1)S(1)} %bitcast.35), channel_id=1, source_target_pairs={{0,3},{1,0},{2,1},{3,2},{4,7},{5,4},{6,5},{7,6},{8,11},{9,8},{10,9... | collective-permute-start | bytes 393224 | tf_op jit(solution)/shard_map/ppermute | solution.py:320
  44.7 6.7 %collective-permute-start.1 = (bf16[256,256]{1,0:T(8,128)(2,1)S(1)}, bf16[256,256]{1,0:T(8,128)(2,1)S(1)}, u32[]{:S(2)}, u32[]{:S(2)}) collective-permute-start(bf16[256,256]{1,0:T(8,128)(2,1)S(1)} %bitcast.36), channel_id=1, source_target_pairs={{0,1},{1,2},{2,3},{3,0},{4,5},{5,6},{6,7},{7,4},{8,9},{9,10},{10,1... | collective-permute-start | bytes 393224 | tf_op jit(solution)/shard_map/ppermute | solution.py:323
  44.7 6.7 %collective-permute-start.2 = (bf16[256,256]{1,0:T(8,128)(2,1)S(1)}, bf16[256,256]{1,0:T(8,128)(2,1)S(1)}, u32[]{:S(2)}, u32[]{:S(2)}) collective-permute-start(bf16[256,256]{1,0:T(8,128)(2,1)S(1)} %bitcast.33), channel_id=1, source_target_pairs={{0,3},{1,0},{2,1},{3,2},{4,7},{5,4},{6,5},{7,6},{8,11},{9,8},{10,9... | collective-permute-start | bytes 393224 | tf_op jit(solution)/shard_map/ppermute | solution.py:324
  47.8 5.3 %collective-permute-start.4 = (bf16[256,256]{1,0:T(8,128)(2,1)S(1)}, bf16[256,256]{1,0:T(8,128)(2,1)S(1)}, u32[]{:S(2)}, u32[]{:S(2)}) collective-permute-start(bf16[256,256]{1,0:T(8,128)(2,1)S(1)} %collective-permute-done.refs_2_), channel_id=1, source_target_pairs={{0,1},{1,2},{2,3},{3,0},{4,5},{5,6},{6,7},{7,4},{8,9},{9,10},{10,1... | collective-permute-start | bytes 393224 | tf_op jit(solution)/shard_map/ppermute | solution.py:321
  47.8 5.3 %collective-permute-start.5 = (bf16[256,256]{1,0:T(8,128)(2,1)S(1)}, bf16[256,256]{1,0:T(8,128)(2,1)S(1)}, u32[]{:S(2)}, u32[]{:S(2)}) collective-permute-start(bf16[256,256]{1,0:T(8,128)(2,1)S(1)} %collective-permute-done.3.refs_5_), channel_id=1, source_target_pairs={{0,3},{1,0},{2,1},{3,2},{4,7},{5,4},{6,5},{7,6},{8,11},{9,8},{10,9... | collective-permute-start | bytes 393224 | tf_op jit(solution)/shard_map/ppermute | solution.py:322
  50.5 0.7 copy-start.13
  62.3 6.4 %copy-start.12 = (s32[1,512,1,3]{1,2,3,0:T(1,128)S(1)}, s32[1,512,1,3]{1,2,3,0:T(1,128)}, u32[]{:S(2)}) copy-start(s32[1,512,1,3]{1,2,3,0:T(1,128)} %param.20) | copy-start | bytes 18436
  62.3 6.5 %copy-start.5 = (f32[8,512]{1,0:T(8,128)S(1)}, f32[8,512]{1,0:T(8,128)}, u32[]{:S(2)}) copy-start(f32[8,512]{1,0:T(8,128)} %get-tuple-element.15.after_ref.slot_ref) | copy-start | bytes 49156
  62.3 24.5 %all-to-all-start.2 = ((bf16[64,17,2,128]{3,2,1,0:T(2,128)(2,1)}), bf16[64,17,2,128]{3,2,1,0:T(2,128)(2,1)S(1)}, u32[]{:S(2)}, u32[]{:S(2)}) async-start(bf16[64,17,2,128]{3,2,1,0:T(2,128)(2,1)} %bitcast.12), calls=%async_computation.2 | async-start | bytes 1114112 | tf_op jit(solution)/shard_map/all_to_all | solution.py:349
  68.8 0.7 copy-start.6
